TPU v7x, 32 devices: a whole 2x2x4 slice. The times are simulated.
32 devices in a mesh: grp: 4 (over y, x), tok: 8 (over z, core).
Axes of the slice: x: 2, y: 2, z: 4, core: 2. Of those that a mesh axis runs over, the one named last changes fastest.
Arguments:
- hidden: bfloat16 [64, 64, 1024], P('tok', 'grp'), may hold values from -6 to 6
- draft_qkv: bfloat16 [3, 64, 64, 1024], P(None, 'tok', None, 'grp'), may hold values from -4 to 4
- self_cache: bfloat16 [64, 2, 512, 1024], P('tok', None, None, 'grp'), may hold values from -4 to 4
- cross_cache: bfloat16 [64, 2, 512, 1024], P('tok', None, None, 'grp'), may hold values from -4 to 4
- parents: int32 [64, 64], P('tok'), may hold values from -1 to 62, as said below
- counts: int32 [64], P('tok'), may hold values from 32 to 64, as said below
- self_len: int32 [64], P('tok'), may hold values from 2 to 512, as said below
- enc_len: int32 [64], P('tok'), may hold values from 2 to 512, as said below
- buckets: int32 [64, 64, 64], P('tok'), may hold values from 0 to 31
- bias_table: float32 [32, 16], P(None, 'grp'), may hold values from -4 to 4
- gain_cross: float32 [1024], replicated, may hold values from 0.25 to 1.75
- gain_ffn: float32 [1024], replicated, may hold values from 0.25 to 1.75
- gain_next: float32 [1024], replicated, may hold values from 0.25 to 1.75
- w_out_self: bfloat16 [1024, 1024], P('grp', 'tok'), may hold values from -0.1875 to 0.1875
- w_query_cross: bfloat16 [1024, 1024], P('tok', 'grp'), may hold values from -1 to 1
- w_out_cross: bfloat16 [1024, 1024], P('grp', 'tok'), may hold values from -0.1875 to 0.1875
- w_gate: bfloat16 [1024, 2816], P('tok', 'grp'), may hold values from -0.1875 to 0.1875
- w_up: bfloat16 [1024, 2816], P('tok', 'grp'), may hold values from -0.1875 to 0.1875
- w_down: bfloat16 [2816, 1024], P('grp', 'tok'), may hold values from -0.109375 to 0.109375
- w_qkv: bfloat16 [1024, 3, 1024], P('tok', None, 'grp'), may hold values from -0.1875 to 0.1875
Outputs:
- out_hidden: bfloat16 [64, 64, 1024], P('tok', 'grp')
- next_qkv: bfloat16 [3, 64, 64, 1024], P(None, 'tok', None, 'grp')
Inputs may be any that keep to these rules, and one draw needn't show every extreme that they name: `parents`: slot 0 of every tree has parent -1; every other slot's parent is an earlier slot. `counts`: some request fills all 64 draft slots. `self_len`: some request fills its whole cache. `enc_len`: some request has all 512 encoder positions.
All inputs are finite; a program needn't handle non-finite values.
Results may differ from a plain program's by a relative error of at most 0.025.
Values may be sent and summed in bfloat16 or wider, within the bound.
No kernel may reach another device: no remote copies, remote signals or barrier semaphores. Data moves between devices by JAX's collectives and lax.ppermute only.
A program may use at most 64 MiB of HBM per device.

v0:
```python
import jax
import jax.numpy as jnp
from jax import lax
from jax.sharding import PartitionSpec as P

DH = 64


def ancestor_table(parent_ids):
    count_slots = parent_ids.shape[0]
    slot_ids = jnp.arange(count_slots, dtype=jnp.int32)
    ancestors = jnp.eye(count_slots, dtype=jnp.float32) + (
        parent_ids[:, None] == slot_ids[None, :]
    ).astype(jnp.float32)
    for repeat in range(max(1, count_slots.bit_length())):
        ancestors = jnp.minimum(jnp.dot(ancestors, ancestors, precision=lax.Precision.HIGHEST), 1.0)
    return ancestors


def rms_scale(stream, gain_vec):
    mean_square = jnp.mean(stream * stream, axis=-1, keepdims=True)
    return (stream * lax.rsqrt(mean_square + 1e-06) * gain_vec).astype(jnp.bfloat16)


def draft_attention(projected, cached, parent_ids, draft_count, length, bucket_ids, bias_table):
    requests, draft_slots, head_width = (projected.shape[1], projected.shape[2], projected.shape[3])
    local_heads = bias_table.shape[1]
    head_size = head_width // local_heads
    queries = projected[0].reshape(requests, draft_slots, local_heads, head_size)
    draft_keys = projected[1].reshape(requests, draft_slots, local_heads, head_size)
    draft_values = projected[2].reshape(requests, draft_slots, local_heads, head_size)
    cache_keys = cached[:, 0].reshape(requests, -1, local_heads, head_size)
    cache_values = cached[:, 1].reshape(requests, -1, local_heads, head_size)
    cache_scores = jnp.einsum(
        "rihd,rphd->rhip", queries, cache_keys, preferred_element_type=jnp.float32
    )
    cache_scores = cache_scores + bias_table[-1][None, :, None, None]
    cache_live = jnp.arange(cache_keys.shape[1], dtype=jnp.int32)[None, :] < length[:, None]
    cache_scores = jnp.where(cache_live[:, None, None, :], cache_scores, -1e30)
    onehot = (bucket_ids[..., None] == jnp.arange(bias_table.shape[0], dtype=jnp.int32)).astype(
        jnp.float32
    )
    draft_bias = jnp.einsum("rijb,bh->rhij", onehot, bias_table, precision=lax.Precision.HIGHEST)
    draft_scores = (
        jnp.einsum("rihd,rjhd->rhij", queries, draft_keys, preferred_element_type=jnp.float32)
        + draft_bias
    )
    ancestors = jax.vmap(ancestor_table)(parent_ids)
    draft_live = (ancestors > 0.5) & (
        jnp.arange(draft_slots, dtype=jnp.int32)[None, None, :] < draft_count[:, None, None]
    )
    draft_scores = jnp.where(draft_live[:, None], draft_scores, -1e30)
    highest = jnp.maximum(cache_scores.max(-1, keepdims=True), draft_scores.max(-1, keepdims=True))
    exp_cache = jnp.exp(cache_scores - highest)
    exp_draft = jnp.exp(draft_scores - highest)
    denominator = exp_cache.sum(-1, keepdims=True) + exp_draft.sum(-1, keepdims=True)
    weights_cache = (exp_cache / denominator).astype(jnp.bfloat16)
    weights_draft = (exp_draft / denominator).astype(jnp.bfloat16)
    attended = jnp.einsum(
        "rhip,rphd->rihd", weights_cache, cache_values, preferred_element_type=jnp.float32
    )
    attended = attended + jnp.einsum(
        "rhij,rjhd->rihd", weights_draft, draft_values, preferred_element_type=jnp.float32
    )
    return attended.astype(jnp.bfloat16).reshape(requests * draft_slots, head_width)


def cross_attention(query_rows, cached, length):
    requests, draft_slots, head_width = query_rows.shape
    local_heads = head_width // DH
    queries = query_rows.reshape(requests, draft_slots, local_heads, DH)
    enc_keys = cached[:, 0].reshape(requests, -1, local_heads, DH)
    enc_values = cached[:, 1].reshape(requests, -1, local_heads, DH)
    scores = jnp.einsum("rihd,rphd->rhip", queries, enc_keys, preferred_element_type=jnp.float32)
    live = jnp.arange(enc_keys.shape[1], dtype=jnp.int32)[None, :] < length[:, None]
    scores = jnp.where(live[:, None, None, :], scores, -1e30)
    highest = scores.max(-1, keepdims=True)
    exp_scores = jnp.exp(scores - highest)
    weights = (exp_scores / exp_scores.sum(-1, keepdims=True)).astype(jnp.bfloat16)
    attended = jnp.einsum(
        "rhip,rphd->rihd", weights, enc_values, preferred_element_type=jnp.float32
    )
    return attended.astype(jnp.bfloat16).reshape(requests * draft_slots, head_width)


def layer_sum(summand, base_full):
    return lax.psum(summand.astype(jnp.bfloat16), "grp").astype(jnp.float32) + base_full


def normed_rows(stream, gain_vec):
    scaled = rms_scale(stream, gain_vec)
    return scaled.reshape(-1, scaled.shape[-1])


def shards(
    hidden,
    draft_qkv,
    self_cache,
    cross_cache,
    parents,
    counts,
    self_len,
    enc_len,
    buckets,
    bias_table,
    gain_cross,
    gain_ffn,
    gain_next,
    w_out_self,
    w_query_cross,
    w_out_cross,
    w_gate,
    w_up,
    w_down,
    w_qkv,
):
    requests, share_rows, model_width = hidden.shape
    draft_slots = draft_qkv.shape[2]
    head_width = draft_qkv.shape[3]
    fetched = (
        lax.all_gather(w_out_self, "tok", axis=1, tiled=True),
        lax.all_gather(w_query_cross, "tok", axis=0, tiled=True),
        lax.all_gather(w_out_cross, "tok", axis=1, tiled=True),
        lax.all_gather(w_gate, "tok", axis=0, tiled=True),
        lax.all_gather(w_up, "tok", axis=0, tiled=True),
        lax.all_gather(w_down, "tok", axis=1, tiled=True),
        lax.all_gather(w_qkv, "tok", axis=0, tiled=True),
    )
    self_context = draft_attention(
        draft_qkv, self_cache, parents, counts, self_len, buckets, bias_table
    )
    partial_value = jnp.dot(self_context, fetched[0], preferred_element_type=jnp.float32)
    partial_value = partial_value.reshape(requests, draft_slots, model_width)
    own_rows = hidden.astype(jnp.float32)
    offset = lax.axis_index("grp") * share_rows
    placed = lax.dynamic_update_slice(
        jnp.zeros((requests, draft_slots, model_width), jnp.float32), own_rows, (0, offset, 0)
    )
    stream_one = layer_sum(partial_value + placed, 0.0)
    normed_one = normed_rows(stream_one, gain_cross)
    cross_query = jnp.dot(normed_one, fetched[1], preferred_element_type=jnp.float32)
    cross_query = cross_query.astype(jnp.bfloat16).reshape(requests, draft_slots, head_width)
    cross_context = cross_attention(cross_query, cross_cache, enc_len)
    partial_value = jnp.dot(cross_context, fetched[2], preferred_element_type=jnp.float32)
    stream_two = layer_sum(partial_value.reshape(requests, draft_slots, model_width), stream_one)
    normed_two = normed_rows(stream_two, gain_ffn)
    gate_part = jnp.dot(normed_two, fetched[3], preferred_element_type=jnp.float32)
    up_part = jnp.dot(normed_two, fetched[4], preferred_element_type=jnp.float32)
    gated = (jax.nn.gelu(gate_part, approximate=True) * up_part).astype(jnp.bfloat16)
    partial_value = jnp.dot(gated, fetched[5], preferred_element_type=jnp.float32)
    stream_three = layer_sum(partial_value.reshape(requests, draft_slots, model_width), stream_two)
    normed_three = normed_rows(stream_three, gain_next)
    projected = jnp.dot(
        normed_three,
        fetched[6].reshape(fetched[6].shape[0], -1),
        preferred_element_type=jnp.float32,
    )
    projected = projected.astype(jnp.bfloat16).reshape(requests, draft_slots, 3, head_width)
    next_qkv = jnp.transpose(projected, (2, 0, 1, 3))
    out_hidden = lax.dynamic_slice_in_dim(stream_three, offset, share_rows, 1).astype(jnp.bfloat16)
    return (out_hidden, next_qkv)


def solution(mesh):
    in_specs = (
        P("tok", "grp", None),
        P(None, "tok", None, "grp"),
        P("tok", None, None, "grp"),
        P("tok", None, None, "grp"),
        P("tok", None),
        P("tok"),
        P("tok"),
        P("tok"),
        P("tok", None, None),
        P(None, "grp"),
        P(),
        P(),
        P(),
        P("grp", "tok"),
        P("tok", "grp"),
        P("grp", "tok"),
        P("tok", "grp"),
        P("tok", "grp"),
        P("grp", "tok"),
        P("tok", None, "grp"),
    )
    out_specs = (P("tok", "grp", None), P(None, "tok", None, "grp"))
    return jax.shard_map(shards, mesh=mesh, in_specs=in_specs, out_specs=out_specs, check_vma=False)
```

profile of v0, /device:TPU:0, one launch (start us, length us, event | category | flops | bytes accessed | tf_op | source)
XLA Modules:
  0.0 270.7 jit_solution(9720914103030838507)
XLA Ops:
  8.1 3.9 %fusion.56 = (bf16[8,1,512,256]{3,2,1,0:T(8,128)(2,1)}, bf16[8,1,512,256]{3,2,1,0:T(8,128)(2,1)S(1)}) fusion(bf16[8,2,512,256]{3,2,1,0:T(8,128)(2,1)} %param.22), kind=kLoop, calls=%fused_computation.97 | loop fusion | bytes 8388608 | tf_op jit(solution)/shard_map/slice | solution.py:32
  12.0 2.4 copy.37
  14.6 2.9 %copy.31 = bf16[8,1,512,256]{2,3,0,1:T(8,128)(2,1)S(1)} copy(bf16[8,1,512,256]{3,2,1,0:T(8,128)(2,1)} %get-tuple-element.8) | data formatting | bytes 4194304 | tf_op jit(solution)/shard_map/slice | solution.py:32
  17.5 1.9 fusion.57
  19.7 3.6 %fusion.1 = f32[8,64,64,4]{2,3,1,0:T(4,128)} fusion(s32[8,64,64]{2,1,0:T(8,128)S(1)} %copy-done.19, f32[32,4]{0,1:T(4,128)S(1)} %copy-done.16), kind=kOutput, calls=%fused_computation.2 | convolution fusion | flops 51380224 | bytes 655872 | tf_op jit(solution)/shard_map/rijb,bh->rhij/dot_general | solution.py:43
  23.3 2.6 copy.36
  34.7 3.0 %fusion.14 = f32[8,4,64,64]{3,2,1,0:T(8,128)S(1)} fusion(bf16[8,512,4,64]{1,3,2,0:T(8,128)(2,1)S(1)} %bitcast.63, f32[8,4,64,512]{3,2,1,0:T(8,128)} %copy-done.1, f32[8,4,64]{2,1,0:T(4,128)S(1)} %add.92, f32[8,4,64]{2,1,0:T(4,128)S(1)} %max.8, f32[4]{0:T(128)S(1)} %slice_reduce_fusion, pred[8,512]{1,0:T(8,128)(4,1)S(1)} %iota_compare_fusion.5), kind=kOutput, calls=%fused_computation.28 | convolution fusion | flops 139460608 | bytes 6836240 | tf_op jit(solution)/shard_map/rhip,rphd->rihd/dot_general | solution.py:59
  39.0 15.6 %all_gather.21 = bf16[256,1024]{1,0:T(8,128)(2,1)S(1)} all-gather(bf16[256,128]{1,0:T(8,128)(2,1)S(1)} %copy-done.9), channel_id=1, replica_groups=mesh['grp'=4,'tok'=8] {'tok'}, dimensions={1}, use_global_device_ids=true | all-gather | bytes 589824 | tf_op jit(solution)/shard_map/all_gather | solution.py:121
  56.4 3.9 %fusion.55 = (bf16[8,1,512,256]{3,2,1,0:T(8,128)(2,1)}, bf16[8,1,512,256]{3,2,1,0:T(8,128)(2,1)S(1)}) fusion(bf16[8,2,512,256]{3,2,1,0:T(8,128)(2,1)} %param.23), kind=kLoop, calls=%fused_computation.96 | loop fusion | bytes 8388608 | tf_op jit(solution)/shard_map/slice | solution.py:72
  60.3 2.4 copy.43
  62.7 2.9 %copy.41 = bf16[8,1,512,256]{2,3,0,1:T(8,128)(2,1)S(1)} copy(bf16[8,1,512,256]{3,2,1,0:T(8,128)(2,1)} %get-tuple-element.6) | data formatting | bytes 4194304 | tf_op jit(solution)/shard_map/slice | solution.py:72
  65.7 14.8 %all_gather.22 = bf16[1024,256]{1,0:T(8,128)(2,1)S(1)} all-gather(bf16[128,256]{1,0:T(8,128)(2,1)S(1)} %copy-done.10), channel_id=1, replica_groups=mesh['grp'=4,'tok'=8] {'tok'}, dimensions={0}, use_global_device_ids=true | all-gather | bytes 589824 | tf_op jit(solution)/shard_map/all_gather | solution.py:122
  80.4 13.7 %all_gather.23 = bf16[256,1024]{1,0:T(8,128)(2,1)S(1)} all-gather(bf16[256,128]{1,0:T(8,128)(2,1)S(1)} %copy-done.11), channel_id=1, replica_groups=mesh['grp'=4,'tok'=8] {'tok'}, dimensions={1}, use_global_device_ids=true | all-gather | bytes 589824 | tf_op jit(solution)/shard_map/all_gather | solution.py:123
  94.1 14.9 %all-reduce.4.cloned.1.call-done = bf16[8,64,1024]{2,1,0:T(8,128)(2,1)} async-done(((bf16[8,64,1024]{2,1,0:T(8,128)(2,1)}), bf16[8,64,1024]{2,1,0:T(8,128)(2,1)}) %all-reduce.4.cloned.1.call-update) | async-done | bytes 1048592 | tf_op jit(solution)/shard_map/psum | solution.py:87
  110.5 1.5 fusion.10
  113.5 2.0 fusion.59
  120.2 50.9 %all-reduce.6.cloned.1.call-done = bf16[8,64,1024]{2,1,0:T(8,128)(2,1)} async-done(((bf16[8,64,1024]{2,1,0:T(8,128)(2,1)}), bf16[8,64,1024]{2,1,0:T(8,128)(2,1)}) %all-reduce.6.cloned.1.call-update) | async-done | bytes 1048592 | tf_op jit(solution)/shard_map/psum | solution.py:87
  171.1 1.7 multiply_reduce_fusion.1
  173.3 3.4 %fusion.60 = f32[512,704]{0,1:T(8,128)} fusion(bf16[512,1024]{1,0:T(8,128)(2,1)S(1)} %bitcast.65, bf16[1024,704]{0,1:T(8,128)(2,1)} %all-gather.5.cloned.1.call-done), kind=kOutput, calls=%fused_computation.101 | convolution fusion | flops 738197504 | bytes 3932160 | tf_op jit(solution)/shard_map/dot_general | solution.py:147
  176.8 23.1 %all-gather.7.cloned.1.call-done = bf16[1024,704]{0,1:T(8,128)(2,1)} async-done(((bf16[128,704]{0,1:T(8,128)(2,1)}), bf16[1024,704]{0,1:T(8,128)(2,1)}) %all-gather.7.cloned.1.call-update) | async-done | bytes 1441808 | tf_op jit(solution)/shard_map/all_gather | solution.py:125
  199.8 5.2 %convolution_convert_fusion = bf16[512,1024]{1,0:T(8,128)(2,1)} fusion(bf16[704,1024]{1,0:T(8,128)(2,1)} %all-gather.9.cloned.1.call-done, bf16[512,1024]{1,0:T(8,128)(2,1)S(1)} %bitcast.66, bf16[1024,704]{0,1:T(8,128)(2,1)} %all-gather.7.cloned.1.call-done, f32[512,704]{0,1:T(8,128)} %fusion.60), kind=kOutput, calls=%fused_computation.29 | convolution fusion | flops 1480523776 | bytes 6422528 | tf_op jit(solution)/shard_map/dot_general | solution.py:150
  206.0 50.7 %all-reduce.8.cloned.1.call-done = bf16[8,64,1024]{2,1,0:T(8,128)(2,1)} async-done(((bf16[8,64,1024]{2,1,0:T(8,128)(2,1)}), bf16[8,64,1024]{2,1,0:T(8,128)(2,1)}) %all-reduce.8.cloned.1.call-update) | async-done | bytes 1048592 | tf_op jit(solution)/shard_map/psum | solution.py:87
  256.7 1.8 multiply_reduce_fusion
  259.5 2.4 convolution_convert_fusion.2
  (104 shorter events, 23.7 us)
Async XLA Ops:
  8.0 101.0 %all-reduce.4.cloned.1.call-start = ((), (), s32[]{:S(2)}) async-start(), calls=%async_computation | async-start | bytes 2097152 | tf_op jit(solution)/shard_map/psum | solution.py:87
  12.0 2.4 copy-start.16
  12.0 2.6 copy-start.17
  17.5 2.2 copy-start.19
  19.7 7.4 %copy-start.12 = (s32[8,64]{1,0:T(8,128)S(1)}, s32[8,64]{1,0:T(8,128)}, u32[]{:S(2)}) copy-start(s32[8,64]{1,0:T(8,128)} %param.24) | copy-start | bytes 6148
  27.1 2.5 copy-start.20
  31.9 2.8 %copy-start.4 = (bf16[8,1,512,256]{2,3,0,1:T(8,128)(2,1)S(1)}, bf16[8,1,512,256]{2,3,0,1:T(8,128)(2,1)}, u32[]{:S(2)}) copy-start(bf16[8,1,512,256]{2,3,0,1:T(8,128)(2,1)} %copy.37) | copy-start | bytes 6291460
  34.7 3.0 %copy-start.6 = (bf16[8,64,4,64]{3,2,1,0:T(4,128)(2,1)S(1)}, bf16[8,64,4,64]{3,2,1,0:T(4,128)(2,1)}, u32[]{:S(2)}) copy-start(bf16[8,64,4,64]{3,2,1,0:T(4,128)(2,1)} %reshape_squeeze.25) | copy-start | bytes 786436
  38.6 16.4 %copy-start.7 = (bf16[8,16,1024]{2,1,0:T(8,128)(2,1)S(1)}, bf16[8,16,1024]{2,1,0:T(8,128)(2,1)}, u32[]{:S(2)}) copy-start(bf16[8,16,1024]{2,1,0:T(8,128)(2,1)} %param.20) | copy-start | bytes 786436
  56.3 114.8 %all-reduce.6.cloned.1.call-start = ((), (), s32[]{:S(2)}) async-start(), calls=%async_computation.1 | async-start | bytes 2097152 | tf_op jit(solution)/shard_map/psum | solution.py:87
  62.7 2.9 %copy-start.18 = (s32[8]{0:T(128)S(1)}, s32[8]{0:T(128)}, u32[]{:S(2)}) copy-start(s32[8]{0:T(128)} %param.27) | copy-start | bytes 100
  62.7 3.0 %copy-start.10 = (bf16[128,256]{1,0:T(8,128)(2,1)S(1)}, bf16[128,256]{1,0:T(8,128)(2,1)}, u32[]{:S(2)}) copy-start(bf16[128,256]{1,0:T(8,128)(2,1)} %param.34) | copy-start | bytes 196612
  62.7 17.8 %copy-start.11 = (bf16[256,128]{1,0:T(8,128)(2,1)S(1)}, bf16[256,128]{1,0:T(8,128)(2,1)}, u32[]{:S(2)}) copy-start(bf16[256,128]{1,0:T(8,128)(2,1)} %param.35) | copy-start | bytes 196612
  65.6 45.0 %copy-start.13 = (f32[1024]{0:T(1024)S(1)}, f32[1024]{0:T(1024)}, u32[]{:S(2)}) copy-start(f32[1024]{0:T(1024)} %param.30) | copy-start | bytes 12292
  113.5 2.0 copy-start.5
  116.6 54.5 %copy-start = (bf16[8,64,1024]{2,1,0:T(8,128)(2,1)S(1)}, bf16[8,64,1024]{2,1,0:T(8,128)(2,1)}, u32[]{:S(2)}) copy-start(bf16[8,64,1024]{2,1,0:T(8,128)(2,1)} %all-reduce.4.cloned.1.call-done) | copy-start | bytes 3145732
  118.4 54.5 %copy-start.14 = (f32[1024]{0:T(1024)S(1)}, f32[1024]{0:T(1024)}, u32[]{:S(2)}) copy-start(f32[1024]{0:T(1024)} %param.31) | copy-start | bytes 12292
  118.4 54.9 %all-gather.5.cloned.1.call-start = ((), (), s32[]{:S(2)}) async-start(), calls=%async_computation.2 | async-start | bytes 1622016 | tf_op jit(solution)/shard_map/all_gather | solution.py:124
  119.0 57.8 %all-gather.9.cloned.1.call-start = ((), (), s32[]{:S(2)}) async-start(), calls=%async_computation.4 | async-start | bytes 1622016 | tf_op jit(solution)/shard_map/all_gather | solution.py:126
  119.6 80.2 %all-gather.7.cloned.1.call-start = ((), (), s32[]{:S(2)}) async-start(), calls=%async_computation.3 | async-start | bytes 1622016 | tf_op jit(solution)/shard_map/all_gather | solution.py:125
  120.2 136.5 %all-reduce.8.cloned.1.call-start = ((), (), s32[]{:S(2)}) async-start(), calls=%async_computation.5 | async-start | bytes 2097152 | tf_op jit(solution)/shard_map/psum | solution.py:87
  176.8 28.4 %copy-start.8 = (bf16[128,3,256]{2,0,1:T(8,128)(2,1)S(1)}, bf16[128,3,256]{2,0,1:T(8,128)(2,1)}, u32[]{:S(2)}) copy-start(bf16[128,3,256]{2,0,1:T(8,128)(2,1)} %param.39) | copy-start | bytes 589828
  205.1 54.4 %all-gather.11.cloned.1.call-start = ((), (), s32[]{:S(2)}) async-start(), calls=%async_computation.6 | async-start | bytes 1769472 | tf_op jit(solution)/shard_map/all_gather | solution.py:127
  206.0 53.2 %copy-start.15 = (f32[1024]{0:T(1024)S(1)}, f32[1024]{0:T(1024)}, u32[]{:S(2)}) copy-start(f32[1024]{0:T(1024)} %param.32) | copy-start | bytes 12292
  (4 other events, 6.1 us)
Sparse Core Ops, SparseCore 0:
  56.5 52.5 all-reduce.3
  118.6 52.5 all-reduce.5
  205.2 51.4 all-reduce.7
Sparse Core Ops, SparseCore 1:
  120.5 26.2 all-gather.4
  148.2 25.3 all-gather.8
  175.1 24.7 all-gather.6
  208.0 25.8 all-gather.10
where the time goes:
time: 271 us
  waiting for transfers between devices  141 us (52%)
  blocking collectives  44.1 us (16%)
  local copies, waits for them, and re-layouts  30.9 us (11%)
  matrix products  25.9 us (10%)
  between operations  15.9 us (6%)
  other arithmetic  12.4 us (5%)
    psum x3, waiting for transfers between devices, layer_sum(): lax.psum(summand.astype(jnp.bfloat16), 'grp').astype(jnp.float32)  116 us
    all_gather x1, waiting for transfers between devices, shards(): lax.all_gather(w_up, 'tok', axis=0, tiled=True)  23.1 us
    all_gather x1, blocking collectives, shards(): lax.all_gather(w_out_self, 'tok', axis=1, tiled=True)  15.6 us
    all_gather x1, blocking collectives, shards(): lax.all_gather(w_query_cross, 'tok', axis=0, tiled=True)  14.8 us
    all_gather x1, blocking collectives, shards(): lax.all_gather(w_out_cross, 'tok', axis=1, tiled=True)  13.7 us
    slice x2, local copies, waits for them, and re-layouts, cross_attention(): enc_keys = cached[:, 0].reshape(requests, -1, local_heads, DH)  6.79 us
    slice x2, local copies, waits for them, and re-layouts, draft_attention(): cache_keys = cached[:, 0].reshape(requests, -1, local_heads, head_size)  6.76 us
  transfers between devices with their start and end apart: 7, of which 4 were waited for; matrix products, arithmetic and copies ran while one was open for 7% of the time, Pallas kernels for 0%

commit v1 on v0

v1 whole, which is shorter than its diff:
```python
import functools
import jax
import jax.numpy as jnp
from jax import lax
from jax.experimental import pallas as pl
from jax.experimental.pallas import tpu as pltpu
from jax.sharding import PartitionSpec as P

DH = 64
HALVES = 1
F32 = jnp.float32
BF16 = jnp.bfloat16
NEG = -1e30
VMEM_LIMIT = 48 * 1024 * 1024
ANY = pl.BlockSpec(memory_space=pl.ANY)
SMEM = pl.BlockSpec(memory_space=pltpu.SMEM)
VMEM = pl.BlockSpec(memory_space=pltpu.VMEM)


def params():
    return pltpu.CompilerParams(vmem_limit_bytes=VMEM_LIMIT)


def cost(flops, moved, transcendentals=0):
    return pl.CostEstimate(
        flops=int(flops), bytes_accessed=int(moved), transcendentals=int(transcendentals)
    )


def dot_nt(lhs, rhs):
    return lax.dot_general(lhs, rhs, (((1,), (1,)), ((), ())), preferred_element_type=F32)


def dot(lhs, rhs):
    return jnp.dot(lhs, rhs, preferred_element_type=F32)


def bias_kernel(parents_ref, counts_ref, buckets_ref, table_ref, out_ref):
    requests, slots = parents_ref.shape
    heads = out_ref.shape[1] // slots
    row = lax.broadcasted_iota(jnp.int32, (slots, slots), 0)
    col = lax.broadcasted_iota(jnp.int32, (slots, slots), 1)
    reach = []
    for r in range(requests):
        linked = (row == parents_ref[r : r + 1, :]) | (row == col)
        reach.append(jnp.where(linked, 1.0, 0.0).astype(BF16))
    span = 1
    while span < slots - 1:
        reach = [jnp.minimum(dot(a, a), 1.0).astype(BF16) for a in reach]
        span *= 2
    eye = jnp.where(row == col, 1.0, 0.0).astype(BF16)
    for r in range(requests):
        ancestors = dot_nt(eye, reach[r])
        live = (ancestors > 0.5) & (col < counts_ref[r])
        picked = buckets_ref[r]
        for h in range(heads):
            shift = table_ref[table_ref.shape[0] - 1, h]
            bias = jnp.zeros((slots, slots), F32)
            for b in range(table_ref.shape[0] - 1):
                bias = jnp.where(picked == b, table_ref[b, h] - shift, bias)
            out_ref[r, h * slots : (h + 1) * slots, :] = jnp.where(live, bias, NEG)


def draft_bias(parents, counts, buckets, bias_table):
    requests, slots = parents.shape
    heads = bias_table.shape[1]
    return pl.pallas_call(
        bias_kernel,
        out_shape=jax.ShapeDtypeStruct((requests, heads * slots, slots), F32),
        in_specs=[VMEM, SMEM, VMEM, SMEM],
        out_specs=VMEM,
        compiler_params=params(),
        cost_estimate=cost(6e7, 1.2e6),
        name="draft_bias",
    )(parents, counts, buckets, bias_table)


def spread_heads(queries, heads):
    head_of = lax.broadcasted_iota(jnp.int32, queries.shape, 1) // DH
    return jnp.concatenate(
        [jnp.where(head_of == h, queries, jnp.zeros_like(queries)) for h in range(heads)], axis=0
    )


def gather_heads(attended, heads):
    slots = attended.shape[0] // heads
    head_of = lax.broadcasted_iota(jnp.int32, (slots, attended.shape[1]), 1) // DH
    total = attended[:slots]
    for h in range(1, heads):
        total = jnp.where(head_of == h, attended[h * slots : (h + 1) * slots], total)
    return total.astype(BF16)


def self_kernel(length_ref, qkv_ref, cache_ref, bias_ref, out_ref):
    r = pl.program_id(0)
    width = qkv_ref.shape[-1]
    heads = width // DH
    queries = spread_heads(qkv_ref[0, 0], heads)
    scores = dot_nt(queries, cache_ref[0, 0])
    position = lax.broadcasted_iota(jnp.int32, (1, scores.shape[1]), 1)
    scores = jnp.where(position < length_ref[r], scores, NEG)
    draft = dot_nt(queries, qkv_ref[1, 0]) + bias_ref[0]
    highest = jnp.maximum(scores.max(-1, keepdims=True), draft.max(-1, keepdims=True))
    scores = jnp.exp(scores - highest)
    draft = jnp.exp(draft - highest)
    total = scores.sum(-1, keepdims=True) + draft.sum(-1, keepdims=True)
    attended = dot(scores.astype(BF16), cache_ref[0, 1]) + dot(draft.astype(BF16), qkv_ref[2, 0])
    out_ref[0] = gather_heads(attended / total, heads)


def self_attention(draft_qkv, cache, bias, length):
    _, requests, slots, width = draft_qkv.shape
    depth = cache.shape[2]
    return pl.pallas_call(
        self_kernel,
        grid=(requests,),
        out_shape=jax.ShapeDtypeStruct((requests, slots, width), BF16),
        in_specs=[
            SMEM,
            pl.BlockSpec((3, 1, slots, width), lambda r: (0, r, 0, 0)),
            pl.BlockSpec((1, 2, depth, width), lambda r: (r, 0, 0, 0)),
            pl.BlockSpec((1, bias.shape[1], slots), lambda r: (r, 0, 0)),
        ],
        out_specs=pl.BlockSpec((1, slots, width), lambda r: (r, 0, 0)),
        compiler_params=params(),
        cost_estimate=cost(5e9, 6e6, 1.2e6),
        name="self_attention",
    )(length, draft_qkv, cache, bias)


def self_out_kernel(ways, first, place_ref, ctx_ref, w_ref, hidden_ref, own_ref, *out_refs):
    share = hidden_ref.shape[1]
    count = own_ref.shape[0] // share
    width = ctx_ref.shape[-1]
    for k in list(range(1, ways)) + [0]:
        owner = jnp.bitwise_xor(place_ref[0], k)
        start = pl.multiple_of(owner * share, share)
        rows = ctx_ref[pl.ds(first, count), pl.ds(start, share), :].reshape(count * share, width)
        part = dot(rows, w_ref[...])
        if k == 0:
            base = hidden_ref[pl.ds(first, count)].reshape(count * share, -1)
            own_ref[...] = part + base.astype(F32)
        else:
            out_refs[k - 1][...] = part.astype(BF16)


def self_out(place, ctx, w, hidden, ways, first, count):
    share, model = hidden.shape[1], hidden.shape[2]
    rows = count * share
    return pl.pallas_call(
        functools.partial(self_out_kernel, ways, first),
        out_shape=[jax.ShapeDtypeStruct((rows, model), F32)]
        + [jax.ShapeDtypeStruct((rows, model), BF16)] * (ways - 1),
        in_specs=[SMEM, VMEM, VMEM, VMEM],
        out_specs=[VMEM] * ways,
        compiler_params=params(),
        cost_estimate=cost(2 * rows * ways * ctx.shape[-1] * model, 2e6),
        name="self_out",
    )(place, ctx, w, hidden)


def norm_kernel(own_ref, *refs):
    others = refs[:-3]
    gain_ref, stream_ref, normed_ref = refs[-3:]
    stream = own_ref[...]
    for other in others:
        stream = stream + other[...].astype(F32)
    stream_ref[...] = stream.astype(stream_ref.dtype)
    scale = lax.rsqrt(jnp.mean(stream * stream, axis=-1, keepdims=True) + 1e-06)
    normed_ref[...] = (stream * scale * gain_ref[...]).astype(BF16)


def norm(own, others, gain, kept=F32):
    return pl.pallas_call(
        norm_kernel,
        out_shape=[
            jax.ShapeDtypeStruct(own.shape, kept),
            jax.ShapeDtypeStruct(own.shape, BF16),
        ],
        in_specs=[VMEM] * (len(others) + 2),
        out_specs=[VMEM] * 2,
        compiler_params=params(),
        cost_estimate=cost(1e6, 2e6),
        name="norm",
    )(own, *others, gain.reshape(1, -1))


def cross_kernel(ways, first, length_ref, *refs):
    blocks = refs[:ways]
    wq_ref, cache_ref, wo_ref, stream_ref = refs[ways : ways + 4]
    own_ref = refs[ways + 4]
    out_refs = refs[ways + 5 : 2 * ways + 4]
    query_ref, ctx_ref = refs[-2:]
    r = pl.program_id(0)
    width = wq_ref.shape[1]
    heads = width // DH
    rows = blocks[0].shape[0]
    share = rows // pl.num_programs(0)

    @pl.when(r == 0)
    def _():
        for k in range(ways):
            query_ref[k] = dot(blocks[k][...], wq_ref[...]).astype(BF16)

    start = pl.multiple_of(r * share, share)
    queries = query_ref[:, pl.ds(start, share), :].reshape(ways * share, width)
    scores = dot_nt(spread_heads(queries, heads), cache_ref[0, 0])
    position = lax.broadcasted_iota(jnp.int32, (1, scores.shape[1]), 1)
    scores = jnp.where(position < length_ref[r + first], scores, NEG)
    scores = jnp.exp(scores - scores.max(-1, keepdims=True))
    total = scores.sum(-1, keepdims=True)
    attended = dot(scores.astype(BF16), cache_ref[0, 1])
    ctx = gather_heads(attended / total, heads)
    ctx_ref[:, pl.ds(start, share), :] = ctx.reshape(ways, share, width)

    @pl.when(r == pl.num_programs(0) - 1)
    def _():
        for k in range(ways):
            part = dot(ctx_ref[k], wo_ref[...])
            if k == 0:
                own_ref[...] = part + stream_ref[...]
            else:
                out_refs[k - 1][...] = part.astype(BF16)


def cross_layer(blocks, wq, cache, wo, stream, length, first, count):
    ways = len(blocks)
    rows, model = blocks[0].shape
    depth, width = cache.shape[2], cache.shape[3]
    full = lambda shape: pl.BlockSpec(shape, lambda r: (0,) * len(shape))
    return pl.pallas_call(
        functools.partial(cross_kernel, ways, first),
        grid=(count,),
        out_shape=[jax.ShapeDtypeStruct((rows, model), F32)]
        + [jax.ShapeDtypeStruct((rows, model), BF16)] * (ways - 1),
        in_specs=[SMEM]
        + [full((rows, model))] * ways
        + [
            full(wq.shape),
            pl.BlockSpec((1, 2, depth, width), lambda r: (r + first, 0, 0, 0)),
            full(wo.shape),
            full((rows, model)),
        ],
        out_specs=[full((rows, model))] * ways,
        scratch_shapes=[pltpu.VMEM((ways, rows, width), BF16), pltpu.VMEM((ways, rows, width), BF16)],
        compiler_params=params(),
        cost_estimate=cost(2.5e9 * count / 4, 4e6 * count / 4, 6e5),
        name="cross_layer",
    )(length, *blocks, wq, cache, wo, stream)


def ffn_kernel(ways, *refs):
    blocks = refs[:ways]
    wgu_ref, wd_ref, stream_ref, own_ref = refs[ways : ways + 4]
    out_refs = refs[ways + 4 :]
    hidden = wd_ref.shape[0]
    for k in list(range(1, ways)) + [0]:
        both = dot(blocks[k][...], wgu_ref[...])
        gated = (jax.nn.gelu(both[:, :hidden], approximate=True) * both[:, hidden:]).astype(BF16)
        part = dot(gated, wd_ref[...])
        if k == 0:
            own_ref[...] = part + stream_ref[...]
        else:
            out_refs[k - 1][...] = part.astype(BF16)


def ffn(blocks, wgu, wd, stream):
    ways = len(blocks)
    rows, model = blocks[0].shape
    return pl.pallas_call(
        functools.partial(ffn_kernel, ways),
        out_shape=[jax.ShapeDtypeStruct((rows, model), F32)]
        + [jax.ShapeDtypeStruct((rows, model), BF16)] * (ways - 1),
        in_specs=[VMEM] * (ways + 3),
        out_specs=[VMEM] * ways,
        compiler_params=params(),
        cost_estimate=cost(2 * rows * ways * (wgu.size + wd.size), 6e6, 4e5),
        name="ffn",
    )(*blocks, wgu, wd, stream)


def project_kernel(ways, place_ref, *refs):
    blocks, w_ref, out_ref = refs[:ways], refs[ways], refs[ways + 1]
    _, count, slots, width = out_ref.shape
    share = slots // ways
    for k in range(ways):
        projected = dot(blocks[k][...], w_ref[...]).astype(BF16)
        start = pl.multiple_of(jnp.bitwise_xor(place_ref[0], k) * share, share)
        for c in range(3):
            piece = projected[:, c * width : (c + 1) * width].reshape(count, share, width)
            out_ref[c, :, pl.ds(start, share), :] = piece


def project(place, blocks, w, count, share):
    ways = len(blocks)
    rows = blocks[0].shape[0]
    return pl.pallas_call(
        functools.partial(project_kernel, ways),
        out_shape=jax.ShapeDtypeStruct((3, count, share * ways, w.shape[1] // 3), BF16),
        in_specs=[SMEM] + [VMEM] * (ways + 1),
        out_specs=VMEM,
        compiler_params=params(),
        cost_estimate=cost(2 * rows * ways * w.size, 4e6),
        name="project",
    )(place, *blocks, w)


def place_kernel(plan, shapes, place_ref, *refs):
    pieces = refs[: len(refs) - len(shapes) - 1]
    outs = refs[len(pieces) : -1]
    sem = refs[-1]
    copies = []
    for k, piece in enumerate(pieces):
        source = jnp.bitwise_xor(place_ref[1], k)
        for out, row, rows, by_row, col in plan:
            if by_row:
                target = outs[out].at[pl.ds(pl.multiple_of(source * rows, rows), rows), col]
            else:
                lanes = piece.shape[1]
                target = outs[out].at[:, pl.ds(pl.multiple_of(source * lanes, lanes), lanes)]
            copies.append(
                pltpu.make_async_copy(
                    piece.at[pl.ds(row, rows), :], target, sem.at[len(copies)]
                )
            )
    for copy in copies:
        copy.start()
    for copy in copies:
        copy.wait()


def place_pieces(place, pieces, plan, shapes):
    return pl.pallas_call(
        functools.partial(place_kernel, plan, shapes),
        out_shape=[jax.ShapeDtypeStruct(shape, BF16) for shape in shapes],
        in_specs=[SMEM] + [ANY] * len(pieces),
        out_specs=[ANY] * len(shapes),
        scratch_shapes=[pltpu.SemaphoreType.DMA((len(pieces) * len(plan),))],
        compiler_params=params(),
        cost_estimate=cost(1e3, 2 * len(pieces) * pieces[0].size * 2),
        name="place_pieces",
    )(place, *pieces)


def fetch(shard, total):
    pieces = []
    for k in range(0, total, 2):
        here = shard
        if k:
            here = lax.ppermute(shard, "tok", [(i, i ^ k) for i in range(total)])
        there = lax.ppermute(here, "tok", [(i, i ^ 1) for i in range(total)])
        pieces += [here, there]
    return pieces


def gather_weights(place, total, w_out_self, w_query, w_out_cross, w_gate, w_up, w_down, w_qkv):
    model_slice = w_query.shape[0]
    hidden = w_gate.shape[1]
    w_qkv = w_qkv.reshape(w_qkv.shape[0], -1)
    w_gate_up = jnp.concatenate([w_gate, w_up], axis=1)
    if total != 8 or model_slice != 128 or w_out_self.shape[1] != 128:
        by_row = functools.partial(lax.all_gather, axis_name="tok", axis=0, tiled=True)
        by_col = functools.partial(lax.all_gather, axis_name="tok", axis=1, tiled=True)
        return (
            by_col(w_out_self),
            by_row(w_query),
            by_col(w_out_cross),
            by_row(w_gate_up),
            by_col(w_down),
            by_row(w_qkv),
        )
    model = model_slice * total
    head_width = w_query.shape[1]
    everything = slice(None)
    (out_self,) = place_pieces(
        place, fetch(w_out_self, total), [(0, 0, head_width, False, None)], [(head_width, model)]
    )
    packed = jnp.concatenate([w_query[:, :128], w_query[:, 128:], w_out_cross], axis=0)
    query, out_cross = place_pieces(
        place,
        fetch(packed, total),
        [
            (0, 0, 128, True, pl.ds(0, 128)),
            (0, 128, 128, True, pl.ds(128, 128)),
            (1, 256, head_width, False, None),
        ],
        [(model, head_width), (head_width, model)],
    )
    (gate_up,) = place_pieces(
        place, fetch(w_gate_up, total), [(0, 0, 128, True, everything)], [(model, 2 * hidden)]
    )
    (down,) = place_pieces(
        place, fetch(w_down, total), [(0, 0, hidden, False, None)], [(hidden, model)]
    )
    (qkv,) = place_pieces(
        place, fetch(w_qkv, total), [(0, 0, 128, True, everything)], [(model, w_qkv.shape[1])]
    )
    return out_self, query, out_cross, gate_up, down, qkv


def send_each(parts, ways):
    return [
        lax.ppermute(part, "grp", [(i, i ^ k) for i in range(ways)])
        for k, part in zip(range(1, ways), parts)
    ]


def spread(block, ways):
    return [block] + send_each([block] * (ways - 1), ways)


def shards(
    ways,
    total,
    hidden,
    draft_qkv,
    self_cache,
    cross_cache,
    parents,
    counts,
    self_len,
    enc_len,
    buckets,
    bias_table,
    gain_cross,
    gain_ffn,
    gain_next,
    w_out_self,
    w_query_cross,
    w_out_cross,
    w_gate,
    w_up,
    w_down,
    w_qkv,
):
    requests, share, model = hidden.shape
    count = requests // HALVES
    place = jnp.stack([lax.axis_index("grp"), lax.axis_index("tok")]).astype(jnp.int32)
    out_self, query, out_cross, gate_up, down, qkv = gather_weights(
        place, total, w_out_self, w_query_cross, w_out_cross, w_gate, w_up, w_down, w_qkv
    )
    bias = draft_bias(parents, counts, buckets, bias_table)
    ctx = self_attention(draft_qkv, self_cache, bias, self_len)
    hidden_parts, qkv_parts = [], []
    for part in range(HALVES):
        first = part * count
        own, *parts = self_out(place, ctx, out_self, hidden, ways, first, count)
        stream, normed = norm(own, send_each(parts, ways), gain_cross)
        own, *parts = cross_layer(
            spread(normed, ways), query, cross_cache, out_cross, stream, enc_len, first, count
        )
        stream, normed = norm(own, send_each(parts, ways), gain_ffn)
        own, *parts = ffn(spread(normed, ways), gate_up, down, stream)
        stream, normed = norm(own, send_each(parts, ways), gain_next, BF16)
        hidden_parts.append(stream.reshape(count, share, model))
        qkv_parts.append(project(place, spread(normed, ways), qkv, count, share))
    if HALVES == 1:
        return hidden_parts[0], qkv_parts[0]
    return jnp.concatenate(hidden_parts, axis=0), jnp.concatenate(qkv_parts, axis=1)


def solution(mesh):
    in_specs = (
        P("tok", "grp", None),
        P(None, "tok", None, "grp"),
        P("tok", None, None, "grp"),
        P("tok", None, None, "grp"),
        P("tok", None),
        P("tok"),
        P("tok"),
        P("tok"),
        P("tok", None, None),
        P(None, "grp"),
        P(),
        P(),
        P(),
        P("grp", "tok"),
        P("tok", "grp"),
        P("grp", "tok"),
        P("tok", "grp"),
        P("tok", "grp"),
        P("grp", "tok"),
        P("tok", None, "grp"),
    )
    out_specs = (P("tok", "grp", None), P(None, "tok", None, "grp"))
    body = functools.partial(shards, mesh.shape["grp"], mesh.shape["tok"])
    return jax.shard_map(body, mesh=mesh, in_specs=in_specs, out_specs=out_specs, check_vma=False)
```

time: 271 us -> 167 us (0.62)
  waiting for transfers between devices: 141 us -> 60 us
  starting transfers between devices: 0.29 us -> 57.7 us
  blocking collectives: 44.1 us -> 0 us
  Pallas kernels: 0 us -> 38 us
  matrix products: 25.9 us -> 0 us
  local copies, waits for them, and re-layouts: 30.9 us -> 8.69 us
  between operations: 15.9 us -> 0.93 us
  other arithmetic: 12.4 us -> 1.05 us
    psum x3 -> x0, waiting for transfers between devices: 116 us -> none  [layer_sum(): lax.psum(summand.astype(jnp.bfloat16), 'grp').astype(jnp.float32)]
    ppermute x0 -> x53, waiting for transfers between devices: none -> 60 us  [the longest x15 40.8 us: fetch(): here = lax.ppermute(shard, 'tok', [(i, i ^ k) for i in range(total)])]
    ppermute x0 -> x53, starting transfers between devices: none -> 57.7 us  [the longest x15 29.6 us: fetch(): here = lax.ppermute(shard, 'tok', [(i, i ^ k) for i in range(total)])]
    all_gather x3 -> x0, blocking collectives: 44.1 us -> none  [the longest x1 15.6 us: shards(): lax.all_gather(w_out_self, 'tok', axis=1, tiled=True)]
    pallas_call x0 -> x14, Pallas kernels: none -> 38 us  [the longest x1 8.35 us: self_attention(): pl.pallas_call(self_kernel, grid=(requests,), out_shape=jax.ShapeDtypeStr...]
    dot_general x20 -> x0, matrix products: 25.9 us -> none  [the longest x1 5.23 us: shards(): jnp.dot(gated, fetched[5], preferred_element_type=jnp.float32)]
    all_gather x4 -> x0, waiting for transfers between devices: 23.1 us -> none  [the longest x1 23.1 us: shards(): lax.all_gather(w_up, 'tok', axis=0, tiled=True)]
    slice x8 -> x1, local copies, waits for them, and re-layouts: 20.4 us -> 0.78 us  [gather_weights(): w_query[:, :128]]
  transfers between devices with their start and end apart: 7 -> 53, of which waited for: 4 -> 17; matrix products, arithmetic and copies ran while one was open for 7% -> 2% of each run, Pallas kernels for 0% -> 18%
where the time goes in v1:
time: 167 us; the launch traced here: 166 us
  waiting for transfers between devices  60 us (36%)
  starting transfers between devices  57.7 us (35%)
  Pallas kernels  38 us (23%)
  local copies, waits for them, and re-layouts  8.69 us (5%)
    ppermute x15, waiting for transfers between devices, fetch(): here = lax.ppermute(shard, 'tok', [(i, i ^ k) for i in range(total)])  40.8 us
    ppermute x15, starting transfers between devices, fetch(): here = lax.ppermute(shard, 'tok', [(i, i ^ k) for i in range(total)])  29.6 us
    ppermute x18, starting transfers between devices, send_each(): lax.ppermute(part, 'grp', [(i, i ^ k) for i in range(ways)])  23.6 us
    ppermute x18, waiting for transfers between devices, send_each(): lax.ppermute(part, 'grp', [(i, i ^ k) for i in range(ways)])  16.9 us
    pallas_call x1, Pallas kernels, self_attention(): pl.pallas_call(self_kernel, grid=(requests,), out_shape=jax.ShapeDtypeStr...  8.35 us
    pallas_call x1, Pallas kernels, cross_layer(): pl.pallas_call(functools.partial(cross_kernel, ways, first), grid=(count,...  8.35 us
    unnamed x34, local copies, waits for them, and re-layouts  7.76 us
    pallas_call x5, Pallas kernels, place_pieces(): pl.pallas_call(functools.partial(place_kernel, plan, shapes), out_shape=[...  7.44 us
  transfers between devices with their start and end apart: 53, of which 17 were waited for; matrix products, arithmetic and copies ran while one was open for 2% of the time, Pallas kernels for 18%

profile of v1, /device:TPU:0, one launch (start us, length us, event | category | flops | bytes accessed | tf_op | source)
XLA Modules:
  0.0 166.3 jit_solution(13010585787599734739)
XLA Ops:
  0.6 3.1 %collective-permute-start.1 = (bf16[256,128]{1,0:T(8,128)(2,1)}, bf16[256,128]{1,0:T(8,128)(2,1)S(1)}, u32[]{:S(2)}, u32[]{:S(2)}) collective-permute-start(bf16[256,128]{1,0:T(8,128)(2,1)} %refs_0_.2), channel_id=1, source_target_pairs={{0,2},{1,3},{2,0},{3,1},{4,6},{5,7},{6,4},{7,5},{8,10},{9,11},{10,... | collective-permute-start | bytes 196616 | tf_op jit(solution)/shard_map/ppermute | solution.py:350
  3.7 2.6 %collective-permute-start.3 = (bf16[256,128]{1,0:T(8,128)(2,1)}, bf16[256,128]{1,0:T(8,128)(2,1)S(1)}, u32[]{:S(2)}, u32[]{:S(2)}) collective-permute-start(bf16[256,128]{1,0:T(8,128)(2,1)} %refs_0_.2), channel_id=1, source_target_pairs={{0,4},{1,5},{2,6},{3,7},{4,0},{5,1},{6,2},{7,3},{8,12},{9,13},{10,... | collective-permute-start | bytes 196616 | tf_op jit(solution)/shard_map/ppermute | solution.py:350
  12.0 4.0 %draft_bias.1.bias_ref = f32[8,256,64]{2,1,0:T(8,128)S(1)} custom-call(s32[8,64]{1,0:T(8,128)S(1)} %copy-done.5, s32[8]{0:T(128)S(1)} %copy-done.9, s32[8,64,64]{2,1,0:T(8,128)S(1)} %copy-done.1, f32[32,4]{1,0:T(8,128)S(1)} %copy.26.table_ref), custom_call_target="tpu_custom_call" | custom-call | flops 60000000 | bytes 1200000 | tf_op jit(solution)/shard_map/draft_bias/pallas_call | solution.py:67
  17.7 8.4 %self_attention.1.ctx_ref = bf16[8,64,256]{2,1,0:T(8,128)(2,1)S(1)} custom-call(s32[8]{0:T(128)S(1)} %copy-done.11, bf16[3,8,64,256]{3,2,1,0:T(8,128)(2,1)S(1)} %copy-done.10, bf16[8,2,512,256]{3,2,1,0:T(8,128)(2,1)} %cache_ref.1, f32[8,256,64]{2,1,0:T(8,128)S(1)} %draft_bias.1.bias_ref), custom_call_target="tpu_custom_call" | custom-call | flops 5000000000 | bytes 6000000 | tf_op jit(solution)/shard_map/self_attention/pallas_call | solution.py:114
  33.3 3.5 %collective-permute-start.16 = (bf16[512,128]{1,0:T(8,128)(2,1)S(1)}, bf16[512,128]{1,0:T(8,128)(2,1)S(1)}, u32[]{:S(2)}, u32[]{:S(2)}) collective-permute-start(bf16[512,128]{1,0:T(8,128)(2,1)S(1)} %pad_maximum_fusion.1.refs_0_), channel_id=1, source_target_pairs={{0,4},{1,5},{2,6},{3,7},{4,0},{5,1},{6,2},{7,3},{8,12},{9,13},{10,... | collective-permute-start | bytes 393224 | tf_op jit(solution)/shard_map/ppermute | solution.py:350
  36.8 8.5 %collective-permute-done.16.refs_4_ = bf16[512,128]{1,0:T(8,128)(2,1)S(1)} collective-permute-done((bf16[512,128]{1,0:T(8,128)(2,1)S(1)}, bf16[512,128]{1,0:T(8,128)(2,1)S(1)}, u32[]{:S(2)}, u32[]{:S(2)}) %collective-permute-start.16) | collective-permute-done | bytes 131104 | tf_op jit(solution)/shard_map/ppermute | solution.py:350
  49.2 2.5 %collective-permute-done.34.refs_2_ = bf16[704,128]{1,0:T(8,128)(2,1)S(1)} collective-permute-done((bf16[704,128]{1,0:T(8,128)(2,1)S(1)}, bf16[704,128]{1,0:T(8,128)(2,1)S(1)}, u32[]{:S(2)}, u32[]{:S(2)}) %collective-permute-start.34) | collective-permute-done | bytes 180256 | tf_op jit(solution)/shard_map/ppermute | solution.py:350
  60.2 8.7 %collective-permute-done.36.refs_4_ = bf16[704,128]{1,0:T(8,128)(2,1)S(1)} collective-permute-done((bf16[704,128]{1,0:T(8,128)(2,1)S(1)}, bf16[704,128]{1,0:T(8,128)(2,1)S(1)}, u32[]{:S(2)}, u32[]{:S(2)}) %collective-permute-start.36) | collective-permute-done | bytes 180256 | tf_op jit(solution)/shard_map/ppermute | solution.py:350
  69.0 3.8 %collective-permute-start.29 = (bf16[128,1408]{1,0:T(8,128)(2,1)S(1)}, bf16[128,1408]{1,0:T(8,128)(2,1)S(1)}, u32[]{:S(2)}, u32[]{:S(2)}) collective-permute-start(bf16[128,1408]{1,0:T(8,128)(2,1)S(1)} %pad_maximum_fusion.refs_0_), channel_id=1, source_target_pairs={{0,4},{1,5},{2,6},{3,7},{4,0},{5,1},{6,2},{7,3},{8,12},{9,13},{10,... | collective-permute-start | bytes 1081352 | tf_op jit(solution)/shard_map/ppermute | solution.py:350
  72.8 2.9 %collective-permute-start.31 = (bf16[128,1408]{1,0:T(8,128)(2,1)S(1)}, bf16[128,1408]{1,0:T(8,128)(2,1)S(1)}, u32[]{:S(2)}, u32[]{:S(2)}) collective-permute-start(bf16[128,1408]{1,0:T(8,128)(2,1)S(1)} %pad_maximum_fusion.refs_0_), channel_id=1, source_target_pairs={{0,6},{1,7},{2,4},{3,5},{4,2},{5,3},{6,0},{7,1},{8,14},{9,15},{10,... | collective-permute-start | bytes 1081352 | tf_op jit(solution)/shard_map/ppermute | solution.py:350
  76.1 8.3 %cross_layer.1 = (f32[128,1024]{1,0:T(8,128)S(1)}, bf16[128,1024]{1,0:T(8,128)(2,1)S(1)}, bf16[128,1024]{1,0:T(8,128)(2,1)S(1)}, bf16[128,1024]{1,0:T(8,128)(2,1)S(1)}) custom-call(s32[8]{0:T(128)S(1)} %copy-done.12, bf16[128,1024]{1,0:T(8,128)(2,1)S(1)} %get-tuple-element.26.refs_0_, bf16[128,1024]{1,0:T(8,128)(2,1)S(1)} %collective-permute-done.10.refs_1_, ...), custom_call_target="tpu_custom_call" | custom-call | flops 5000000000 | bytes 8000000 | tf_op jit(solution)/shard_map/cross_layer/pallas_call | solution.py:231
  85.8 11.7 %collective-permute-done.29.refs_4_ = bf16[128,1408]{1,0:T(8,128)(2,1)S(1)} collective-permute-done((bf16[128,1408]{1,0:T(8,128)(2,1)S(1)}, bf16[128,1408]{1,0:T(8,128)(2,1)S(1)}, u32[]{:S(2)}, u32[]{:S(2)}) %collective-permute-start.29) | collective-permute-done | bytes 360480 | tf_op jit(solution)/shard_map/ppermute | solution.py:350
  101.1 7.9 %collective-permute-done.21.refs_1_ = bf16[128,1024]{1,0:T(8,128)(2,1)S(1)} collective-permute-done((bf16[128,1024]{1,0:T(8,128)(2,1)S(1)}, bf16[128,1024]{1,0:T(8,128)(2,1)S(1)}, u32[]{:S(2)}, u32[]{:S(2)}) %collective-permute-start.21) | collective-permute-done | bytes 262176 | tf_op jit(solution)/shard_map/ppermute | solution.py:403
  114.4 1.8 %place_pieces.7.refs_4_ = bf16[1024,1408]{1,0:T(8,128)(2,1)S(1)} custom-call(s32[2]{0:T(128)S(1)} %pad_add_fusion.place_ref, bf16[128,1408]{1,0:T(8,128)(2,1)S(1)} %pad_maximum_fusion.refs_0_, bf16[128,1408]{1,0:T(8,128)(2,1)S(1)} %collective-permute-done.26.refs_1_, bf16[128,1408]{1,0:T(8,128)(2,1)S(1)} %collective-permute-done.27.refs_2_, ...), custom_call_target="tpu_custom_call" | custom-call | flops 1000 | bytes 5767168 | tf_op jit(solution)/shard_map/place_pieces/pallas_call | solution.py:333
  119.0 4.6 %collective-permute-done.24.refs_2_ = bf16[128,1024]{1,0:T(8,128)(2,1)S(1)} collective-permute-done((bf16[128,1024]{1,0:T(8,128)(2,1)S(1)}, bf16[128,1024]{1,0:T(8,128)(2,1)S(1)}, u32[]{:S(2)}, u32[]{:S(2)}) %collective-permute-start.24) | collective-permute-done | bytes 262176 | tf_op jit(solution)/shard_map/ppermute | solution.py:403
  124.6 5.2 %ffn.1 = (f32[128,1024]{1,0:T(8,128)S(1)}, bf16[128,1024]{1,0:T(8,128)(2,1)S(1)}, bf16[128,1024]{1,0:T(8,128)(2,1)S(1)}, bf16[128,1024]{1,0:T(8,128)(2,1)S(1)}) custom-call(bf16[128,1024]{1,0:T(8,128)(2,1)S(1)} %get-tuple-element.34.refs_0_, bf16[128,1024]{1,0:T(8,128)(2,1)S(1)} %collective-permute-done.23.refs_1_, ...), custom_call_target="tpu_custom_call" | custom-call | flops 2214592512 | bytes 6000000 | tf_op jit(solution)/shard_map/ffn/pallas_call | solution.py:270
  132.5 4.2 %collective-permute-start.47 = (bf16[128,768]{1,0:T(8,128)(2,1)S(1)}, bf16[128,768]{1,0:T(8,128)(2,1)S(1)}, u32[]{:S(2)}, u32[]{:S(2)}) collective-permute-start(bf16[128,768]{1,0:T(8,128)(2,1)S(1)} %copy.34.refs_0_), channel_id=1, source_target_pairs={{0,2},{1,3},{2,0},{3,1},{4,6},{5,7},{6,4},{7,5},{8,10},{9,11},{10,... | collective-permute-start | bytes 589832 | tf_op jit(solution)/shard_map/ppermute | solution.py:350
  137.8 2.0 %collective-permute-start.49 = (bf16[128,768]{1,0:T(8,128)(2,1)S(1)}, bf16[128,768]{1,0:T(8,128)(2,1)S(1)}, u32[]{:S(2)}, u32[]{:S(2)}) collective-permute-start(bf16[128,768]{1,0:T(8,128)(2,1)S(1)} %copy.34.refs_0_), channel_id=1, source_target_pairs={{0,4},{1,5},{2,6},{3,7},{4,0},{5,1},{6,2},{7,3},{8,12},{9,13},{10,... | collective-permute-start | bytes 589832 | tf_op jit(solution)/shard_map/ppermute | solution.py:350
  139.8 2.8 %collective-permute-done.47.refs_2_ = bf16[128,768]{1,0:T(8,128)(2,1)S(1)} collective-permute-done((bf16[128,768]{1,0:T(8,128)(2,1)S(1)}, bf16[128,768]{1,0:T(8,128)(2,1)S(1)}, u32[]{:S(2)}, u32[]{:S(2)}) %collective-permute-start.47) | collective-permute-done | bytes 196640 | tf_op jit(solution)/shard_map/ppermute | solution.py:350
  142.6 2.7 %collective-permute-start.51 = (bf16[128,768]{1,0:T(8,128)(2,1)S(1)}, bf16[128,768]{1,0:T(8,128)(2,1)S(1)}, u32[]{:S(2)}, u32[]{:S(2)}) collective-permute-start(bf16[128,768]{1,0:T(8,128)(2,1)S(1)} %copy.34.refs_0_), channel_id=1, source_target_pairs={{0,6},{1,7},{2,4},{3,5},{4,2},{5,3},{6,0},{7,1},{8,14},{9,15},{10,... | collective-permute-start | bytes 589832 | tf_op jit(solution)/shard_map/ppermute | solution.py:350
  148.0 6.5 %collective-permute-done.49.refs_4_ = bf16[128,768]{1,0:T(8,128)(2,1)S(1)} collective-permute-done((bf16[128,768]{1,0:T(8,128)(2,1)S(1)}, bf16[128,768]{1,0:T(8,128)(2,1)S(1)}, u32[]{:S(2)}, u32[]{:S(2)}) %collective-permute-start.49) | collective-permute-done | bytes 196640 | tf_op jit(solution)/shard_map/ppermute | solution.py:350
  159.0 2.7 %place_pieces.9.refs_4_ = bf16[1024,768]{1,0:T(8,128)(2,1)S(1)} custom-call(s32[2]{0:T(128)S(1)} %pad_add_fusion.place_ref, bf16[128,768]{1,0:T(8,128)(2,1)S(1)} %copy.34.refs_0_, bf16[128,768]{1,0:T(8,128)(2,1)S(1)} %collective-permute-done.46.refs_1_, bf16[128,768]{1,0:T(8,128)(2,1)S(1)} %collective-permute-done.47.refs_2_, ...), custom_call_target="tpu_custom_call" | custom-call | flops 1000 | bytes 3145728 | tf_op jit(solution)/shard_map/place_pieces/pallas_call | solution.py:333
  161.7 2.2 %collective-permute-done.44.refs_2_ = bf16[128,1024]{1,0:T(8,128)(2,1)S(1)} collective-permute-done((bf16[128,1024]{1,0:T(8,128)(2,1)S(1)}, bf16[128,1024]{1,0:T(8,128)(2,1)S(1)}, u32[]{:S(2)}, u32[]{:S(2)}) %collective-permute-start.44) | collective-permute-done | bytes 262176 | tf_op jit(solution)/shard_map/ppermute | solution.py:403
  163.9 2.4 %project.1 = bf16[3,8,64,256]{3,2,1,0:T(8,128)(2,1)} custom-call(s32[2]{0:T(128)S(1)} %pad_add_fusion.place_ref, bf16[128,1024]{1,0:T(8,128)(2,1)S(1)} %get-tuple-element.41.refs_0_, bf16[128,1024]{1,0:T(8,128)(2,1)S(1)} %collective-permute-done.43.refs_1_, bf16[128,1024]{1,0:T(8,128)(2,1)S(1)} %collective-permute-done.44.refs_2_, ...), custom_call_target="tpu_custom_call" | custom-call | flops 805306368 | bytes 4000000 | tf_op jit(solution)/shard_map/project/pallas_call | solution.py:297
  (135 shorter events, 52.5 us)
Async XLA Ops:
  0.6 25.5 %collective-permute-start.1 = (bf16[256,128]{1,0:T(8,128)(2,1)}, bf16[256,128]{1,0:T(8,128)(2,1)S(1)}, u32[]{:S(2)}, u32[]{:S(2)}) collective-permute-start(bf16[256,128]{1,0:T(8,128)(2,1)} %refs_0_.2), channel_id=1, source_target_pairs={{0,2},{1,3},{2,0},{3,1},{4,6},{5,7},{6,4},{7,5},{8,10},{9,11},{10,... | collective-permute-start | bytes 196616 | tf_op jit(solution)/shard_map/ppermute | solution.py:350
  3.7 22.7 %collective-permute-start.3 = (bf16[256,128]{1,0:T(8,128)(2,1)}, bf16[256,128]{1,0:T(8,128)(2,1)S(1)}, u32[]{:S(2)}, u32[]{:S(2)}) collective-permute-start(bf16[256,128]{1,0:T(8,128)(2,1)} %refs_0_.2), channel_id=1, source_target_pairs={{0,4},{1,5},{2,6},{3,7},{4,0},{5,1},{6,2},{7,3},{8,12},{9,13},{10,... | collective-permute-start | bytes 196616 | tf_op jit(solution)/shard_map/ppermute | solution.py:350
  6.3 20.4 %collective-permute-start.5 = (bf16[256,128]{1,0:T(8,128)(2,1)}, bf16[256,128]{1,0:T(8,128)(2,1)S(1)}, u32[]{:S(2)}, u32[]{:S(2)}) collective-permute-start(bf16[256,128]{1,0:T(8,128)(2,1)} %refs_0_.2), channel_id=1, source_target_pairs={{0,6},{1,7},{2,4},{3,5},{4,2},{5,3},{6,0},{7,1},{8,14},{9,15},{10,... | collective-permute-start | bytes 196616 | tf_op jit(solution)/shard_map/ppermute | solution.py:350
  6.3 20.7 %collective-permute-start = (bf16[256,128]{1,0:T(8,128)(2,1)}, bf16[256,128]{1,0:T(8,128)(2,1)S(1)}, u32[]{:S(2)}, u32[]{:S(2)}) collective-permute-start(bf16[256,128]{1,0:T(8,128)(2,1)} %refs_0_.2), channel_id=1, source_target_pairs={{0,1},{1,0},{2,3},{3,2},{4,5},{5,4},{6,7},{7,6},{8,9},{9,8},{10,11... | collective-permute-start | bytes 196616 | tf_op jit(solution)/shard_map/ppermute | solution.py:351
  7.9 28.9 %collective-permute-start.14 = (bf16[512,128]{1,0:T(8,128)(2,1)S(1)}, bf16[512,128]{1,0:T(8,128)(2,1)S(1)}, u32[]{:S(2)}, u32[]{:S(2)}) collective-permute-start(bf16[512,128]{1,0:T(8,128)(2,1)S(1)} %pad_maximum_fusion.1.refs_0_), channel_id=1, source_target_pairs={{0,2},{1,3},{2,0},{3,1},{4,6},{5,7},{6,4},{7,5},{8,10},{9,11},{10,... | collective-permute-start | bytes 393224 | tf_op jit(solution)/shard_map/ppermute | solution.py:350
  29.8 16.6 %collective-permute-start.7 = (bf16[128,1024]{1,0:T(8,128)(2,1)S(1)}, bf16[128,1024]{1,0:T(8,128)(2,1)S(1)}, u32[]{:S(2)}, u32[]{:S(2)}) collective-permute-start(bf16[128,1024]{1,0:T(8,128)(2,1)S(1)} %get-tuple-element.23), channel_id=1, source_target_pairs={{0,8},{8,0},{16,24},{24,16},{1,9},{9,1},{17,25},{25,17},{2,10},{10... | collective-permute-start | bytes 786440 | tf_op jit(solution)/shard_map/ppermute | solution.py:403
  31.4 15.6 %collective-permute-start.8 = (bf16[128,1024]{1,0:T(8,128)(2,1)S(1)}, bf16[128,1024]{1,0:T(8,128)(2,1)S(1)}, u32[]{:S(2)}, u32[]{:S(2)}) collective-permute-start(bf16[128,1024]{1,0:T(8,128)(2,1)S(1)} %get-tuple-element.24), channel_id=1, source_target_pairs={{0,16},{8,24},{16,0},{24,8},{1,17},{9,25},{17,1},{25,9},{2,18},{10... | collective-permute-start | bytes 786440 | tf_op jit(solution)/shard_map/ppermute | solution.py:403
  32.9 14.1 %collective-permute-start.9 = (bf16[128,1024]{1,0:T(8,128)(2,1)S(1)}, bf16[128,1024]{1,0:T(8,128)(2,1)S(1)}, u32[]{:S(2)}, u32[]{:S(2)}) collective-permute-start(bf16[128,1024]{1,0:T(8,128)(2,1)S(1)} %get-tuple-element.25), channel_id=1, source_target_pairs={{0,24},{8,16},{16,8},{24,0},{1,25},{9,17},{17,9},{25,1},{2,26},{10... | collective-permute-start | bytes 786440 | tf_op jit(solution)/shard_map/ppermute | solution.py:403
  47.7 25.0 %collective-permute-start.10 = (bf16[128,1024]{1,0:T(8,128)(2,1)S(1)}, bf16[128,1024]{1,0:T(8,128)(2,1)S(1)}, u32[]{:S(2)}, u32[]{:S(2)}) collective-permute-start(bf16[128,1024]{1,0:T(8,128)(2,1)S(1)} %get-tuple-element.26.refs_0_), channel_id=1, source_target_pairs={{0,8},{8,0},{16,24},{24,16},{1,9},{9,1},{17,25},{25,17},{2,10},{10... | collective-permute-start | bytes 786440 | tf_op jit(solution)/shard_map/ppermute | solution.py:403
  51.7 23.9 %collective-permute-start.11 = (bf16[128,1024]{1,0:T(8,128)(2,1)S(1)}, bf16[128,1024]{1,0:T(8,128)(2,1)S(1)}, u32[]{:S(2)}, u32[]{:S(2)}) collective-permute-start(bf16[128,1024]{1,0:T(8,128)(2,1)S(1)} %get-tuple-element.26.refs_0_), channel_id=1, source_target_pairs={{0,16},{8,24},{16,0},{24,8},{1,17},{9,25},{17,1},{25,9},{2,18},{10... | collective-permute-start | bytes 786440 | tf_op jit(solution)/shard_map/ppermute | solution.py:403
  53.4 22.2 %collective-permute-start.12 = (bf16[128,1024]{1,0:T(8,128)(2,1)S(1)}, bf16[128,1024]{1,0:T(8,128)(2,1)S(1)}, u32[]{:S(2)}, u32[]{:S(2)}) collective-permute-start(bf16[128,1024]{1,0:T(8,128)(2,1)S(1)} %get-tuple-element.26.refs_0_), channel_id=1, source_target_pairs={{0,24},{8,16},{16,8},{24,0},{1,25},{9,17},{17,9},{25,1},{2,26},{10... | collective-permute-start | bytes 786440 | tf_op jit(solution)/shard_map/ppermute | solution.py:403
  56.1 12.9 %collective-permute-start.36 = (bf16[704,128]{1,0:T(8,128)(2,1)S(1)}, bf16[704,128]{1,0:T(8,128)(2,1)S(1)}, u32[]{:S(2)}, u32[]{:S(2)}) collective-permute-start(bf16[704,128]{1,0:T(8,128)(2,1)S(1)} %copy-done.3), channel_id=1, source_target_pairs={{0,4},{1,5},{2,6},{3,7},{4,0},{5,1},{6,2},{7,3},{8,12},{9,13},{10,... | collective-permute-start | bytes 540680 | tf_op jit(solution)/shard_map/ppermute | solution.py:350
  69.0 16.8 %collective-permute-start.27 = (bf16[128,1408]{1,0:T(8,128)(2,1)S(1)}, bf16[128,1408]{1,0:T(8,128)(2,1)S(1)}, u32[]{:S(2)}, u32[]{:S(2)}) collective-permute-start(bf16[128,1408]{1,0:T(8,128)(2,1)S(1)} %pad_maximum_fusion.refs_0_), channel_id=1, source_target_pairs={{0,2},{1,3},{2,0},{3,1},{4,6},{5,7},{6,4},{7,5},{8,10},{9,11},{10,... | collective-permute-start | bytes 1081352 | tf_op jit(solution)/shard_map/ppermute | solution.py:350
  69.0 28.5 %collective-permute-start.29 = (bf16[128,1408]{1,0:T(8,128)(2,1)S(1)}, bf16[128,1408]{1,0:T(8,128)(2,1)S(1)}, u32[]{:S(2)}, u32[]{:S(2)}) collective-permute-start(bf16[128,1408]{1,0:T(8,128)(2,1)S(1)} %pad_maximum_fusion.refs_0_), channel_id=1, source_target_pairs={{0,4},{1,5},{2,6},{3,7},{4,0},{5,1},{6,2},{7,3},{8,12},{9,13},{10,... | collective-permute-start | bytes 1081352 | tf_op jit(solution)/shard_map/ppermute | solution.py:350
  72.8 26.3 %collective-permute-start.31 = (bf16[128,1408]{1,0:T(8,128)(2,1)S(1)}, bf16[128,1408]{1,0:T(8,128)(2,1)S(1)}, u32[]{:S(2)}, u32[]{:S(2)}) collective-permute-start(bf16[128,1408]{1,0:T(8,128)(2,1)S(1)} %pad_maximum_fusion.refs_0_), channel_id=1, source_target_pairs={{0,6},{1,7},{2,4},{3,5},{4,2},{5,3},{6,0},{7,1},{8,14},{9,15},{10,... | collective-permute-start | bytes 1081352 | tf_op jit(solution)/shard_map/ppermute | solution.py:350
  75.6 24.9 %collective-permute-start.26 = (bf16[128,1408]{1,0:T(8,128)(2,1)S(1)}, bf16[128,1408]{1,0:T(8,128)(2,1)S(1)}, u32[]{:S(2)}, u32[]{:S(2)}) collective-permute-start(bf16[128,1408]{1,0:T(8,128)(2,1)S(1)} %pad_maximum_fusion.refs_0_), channel_id=1, source_target_pairs={{0,1},{1,0},{2,3},{3,2},{4,5},{5,4},{6,7},{7,6},{8,9},{9,8},{10,11... | collective-permute-start | bytes 1081352 | tf_op jit(solution)/shard_map/ppermute | solution.py:351
  84.5 16.5 %collective-permute-start.20 = (bf16[128,1024]{1,0:T(8,128)(2,1)S(1)}, bf16[128,1024]{1,0:T(8,128)(2,1)S(1)}, u32[]{:S(2)}, u32[]{:S(2)}) collective-permute-start(bf16[128,1024]{1,0:T(8,128)(2,1)S(1)} %get-tuple-element.31), channel_id=1, source_target_pairs={{0,8},{8,0},{16,24},{24,16},{1,9},{9,1},{17,25},{25,17},{2,10},{10... | collective-permute-start | bytes 786440 | tf_op jit(solution)/shard_map/ppermute | solution.py:403
  85.8 14.7 %collective-permute-start.35 = (bf16[704,128]{1,0:T(8,128)(2,1)S(1)}, bf16[704,128]{1,0:T(8,128)(2,1)S(1)}, u32[]{:S(2)}, u32[]{:S(2)}) collective-permute-start(bf16[704,128]{1,0:T(8,128)(2,1)S(1)} %collective-permute-done.34.refs_2_), channel_id=1, source_target_pairs={{0,1},{1,0},{2,3},{3,2},{4,5},{5,4},{6,7},{7,6},{8,9},{9,8},{10,11... | collective-permute-start | bytes 540680 | tf_op jit(solution)/shard_map/ppermute | solution.py:351
  110.8 12.8 %collective-permute-start.24 = (bf16[128,1024]{1,0:T(8,128)(2,1)S(1)}, bf16[128,1024]{1,0:T(8,128)(2,1)S(1)}, u32[]{:S(2)}, u32[]{:S(2)}) collective-permute-start(bf16[128,1024]{1,0:T(8,128)(2,1)S(1)} %get-tuple-element.34.refs_0_), channel_id=1, source_target_pairs={{0,16},{8,24},{16,0},{24,8},{1,17},{9,25},{17,1},{25,9},{2,18},{10... | collective-permute-start | bytes 786440 | tf_op jit(solution)/shard_map/ppermute | solution.py:403
  129.8 15.6 %collective-permute-start.40 = (bf16[128,1024]{1,0:T(8,128)(2,1)S(1)}, bf16[128,1024]{1,0:T(8,128)(2,1)S(1)}, u32[]{:S(2)}, u32[]{:S(2)}) collective-permute-start(bf16[128,1024]{1,0:T(8,128)(2,1)S(1)} %get-tuple-element.37), channel_id=1, source_target_pairs={{0,8},{8,0},{16,24},{24,16},{1,9},{9,1},{17,25},{25,17},{2,10},{10... | collective-permute-start | bytes 786440 | tf_op jit(solution)/shard_map/ppermute | solution.py:403
  131.0 14.4 %collective-permute-start.41 = (bf16[128,1024]{1,0:T(8,128)(2,1)S(1)}, bf16[128,1024]{1,0:T(8,128)(2,1)S(1)}, u32[]{:S(2)}, u32[]{:S(2)}) collective-permute-start(bf16[128,1024]{1,0:T(8,128)(2,1)S(1)} %get-tuple-element.38), channel_id=1, source_target_pairs={{0,16},{8,24},{16,0},{24,8},{1,17},{9,25},{17,1},{25,9},{2,18},{10... | collective-permute-start | bytes 786440 | tf_op jit(solution)/shard_map/ppermute | solution.py:403
  137.8 16.7 %collective-permute-start.49 = (bf16[128,768]{1,0:T(8,128)(2,1)S(1)}, bf16[128,768]{1,0:T(8,128)(2,1)S(1)}, u32[]{:S(2)}, u32[]{:S(2)}) collective-permute-start(bf16[128,768]{1,0:T(8,128)(2,1)S(1)} %copy.34.refs_0_), channel_id=1, source_target_pairs={{0,4},{1,5},{2,6},{3,7},{4,0},{5,1},{6,2},{7,3},{8,12},{9,13},{10,... | collective-permute-start | bytes 589832 | tf_op jit(solution)/shard_map/ppermute | solution.py:350
  142.6 13.1 %collective-permute-start.51 = (bf16[128,768]{1,0:T(8,128)(2,1)S(1)}, bf16[128,768]{1,0:T(8,128)(2,1)S(1)}, u32[]{:S(2)}, u32[]{:S(2)}) collective-permute-start(bf16[128,768]{1,0:T(8,128)(2,1)S(1)} %copy.34.refs_0_), channel_id=1, source_target_pairs={{0,6},{1,7},{2,4},{3,5},{4,2},{5,3},{6,0},{7,1},{8,14},{9,15},{10,... | collective-permute-start | bytes 589832 | tf_op jit(solution)/shard_map/ppermute | solution.py:350
  146.8 14.9 %collective-permute-start.43 = (bf16[128,1024]{1,0:T(8,128)(2,1)S(1)}, bf16[128,1024]{1,0:T(8,128)(2,1)S(1)}, u32[]{:S(2)}, u32[]{:S(2)}) collective-permute-start(bf16[128,1024]{1,0:T(8,128)(2,1)S(1)} %get-tuple-element.41.refs_0_), channel_id=1, source_target_pairs={{0,8},{8,0},{16,24},{24,16},{1,9},{9,1},{17,25},{25,17},{2,10},{10... | collective-permute-start | bytes 786440 | tf_op jit(solution)/shard_map/ppermute | solution.py:403
  (44 other events, 452.8 us)

commit v2 on v0

v2 whole, which is shorter than its diff:
```python
import functools
import jax
import jax.numpy as jnp
from jax import lax
from jax.experimental import pallas as pl
from jax.experimental.pallas import tpu as pltpu
from jax.sharding import PartitionSpec as P

DH = 64
F32 = jnp.float32
BF16 = jnp.bfloat16
NEG = -1e30
MIB = 1024 * 1024
HBM = pl.BlockSpec(memory_space=pl.ANY)
SMEM = pl.BlockSpec(memory_space=pltpu.SMEM)
VMEM = pl.BlockSpec(memory_space=pltpu.VMEM)


def params(limit=28):
    return pltpu.CompilerParams(vmem_limit_bytes=limit * MIB)


def cost(flops, moved, transcendentals=0):
    return pl.CostEstimate(
        flops=int(flops), bytes_accessed=int(moved), transcendentals=int(transcendentals)
    )


def dot_nt(lhs, rhs):
    return lax.dot_general(lhs, rhs, (((1,), (1,)), ((), ())), preferred_element_type=F32)


def dot(lhs, rhs):
    return jnp.dot(lhs, rhs, preferred_element_type=F32)


def ancestor_masks(parents_ref, counts_ref):
    requests, slots = parents_ref.shape
    row = lax.broadcasted_iota(jnp.int32, (slots, slots), 0)
    col = lax.broadcasted_iota(jnp.int32, (slots, slots), 1)
    reach = []
    for r in range(requests):
        linked = (row == parents_ref[r : r + 1, :]) | (row == col)
        reach.append(jnp.where(linked, 1.0, 0.0).astype(BF16))
    span = 1
    while span < slots - 1:
        reach = [jnp.minimum(dot(a, a), 1.0).astype(BF16) for a in reach]
        span *= 2
    eye = jnp.where(row == col, 1.0, 0.0).astype(BF16)
    return [
        (dot_nt(eye, reach[r]) > 0.5) & (col < counts_ref[r]) for r in range(requests)
    ]


def bias_rows(table_ref):
    heads, kinds = table_ref.shape
    shifted = table_ref[...] - table_ref[:, kinds - 1 :]
    return jnp.concatenate([shifted, jnp.zeros((heads, 128 - kinds), F32)], axis=1)


def draft_bias(live, picked, table):
    slots, lanes = live.shape[0], table.shape[1]
    picked = jnp.concatenate([picked, jnp.zeros((slots, lanes - slots), jnp.int32)], axis=1)
    parts = []
    for h in range(table.shape[0]):
        row_of = jnp.broadcast_to(table[h : h + 1, :], (slots, lanes))
        bias = jnp.take_along_axis(row_of, picked, axis=1)[:, :slots]
        parts.append(jnp.where(live, bias, NEG))
    return jnp.concatenate(parts, axis=0)


def spread_heads(queries, heads):
    head_of = lax.broadcasted_iota(jnp.int32, queries.shape, 1) // DH
    return jnp.concatenate(
        [jnp.where(head_of == h, queries, jnp.zeros_like(queries)) for h in range(heads)], axis=0
    )


def gather_heads(attended, heads):
    slots = attended.shape[0] // heads
    head_of = lax.broadcasted_iota(jnp.int32, (slots, attended.shape[1]), 1) // DH
    total = attended[:slots]
    for h in range(1, heads):
        total = jnp.where(head_of == h, attended[h * slots : (h + 1) * slots], total)
    return total.astype(BF16)


def fetch_requests(pairs, sems):
    copies = []
    for r in range(pairs[0][1].shape[0]):
        copies.append([])
        for at, (source, target) in enumerate(pairs):
            copy = pltpu.make_async_copy(source(r), target.at[r], sems.at[r, at])
            copy.start()
            copies[r].append(copy)
    return copies


def self_kernel(
    counts_ref, length_ref, parents_ref, buckets_ref, table_ref, qkv_hbm, cache_hbm, out_ref,
    qkv_ref, cache_ref, sems,
):
    requests, slots, width = out_ref.shape
    heads = width // DH
    copies = fetch_requests(
        [(lambda r: cache_hbm.at[r], cache_ref), (lambda r: qkv_hbm.at[:, r], qkv_ref)], sems
    )
    live = ancestor_masks(parents_ref, counts_ref)
    table = bias_rows(table_ref)
    position = lax.broadcasted_iota(jnp.int32, (1, cache_ref.shape[2]), 1)
    for r in range(requests):
        for copy in copies[r]:
            copy.wait()
        queries = spread_heads(qkv_ref[r, 0], heads)
        scores = dot_nt(queries, cache_ref[r, 0])
        scores = jnp.where(position < length_ref[r], scores, NEG)
        draft = dot_nt(queries, qkv_ref[r, 1]) + draft_bias(live[r], buckets_ref[r], table)
        highest = jnp.maximum(scores.max(-1, keepdims=True), draft.max(-1, keepdims=True))
        scores = jnp.exp(scores - highest)
        draft = jnp.exp(draft - highest)
        total = scores.sum(-1, keepdims=True) + draft.sum(-1, keepdims=True)
        attended = dot(scores.astype(BF16), cache_ref[r, 1])
        attended = attended + dot(draft.astype(BF16), qkv_ref[r, 2])
        out_ref[r] = gather_heads(attended / total, heads)


def self_attention(draft_qkv, cache, parents, counts, buckets, bias_table, length):
    _, requests, slots, width = draft_qkv.shape
    return pl.pallas_call(
        self_kernel,
        out_shape=jax.ShapeDtypeStruct((requests, slots, width), BF16),
        in_specs=[SMEM, SMEM, VMEM, VMEM, VMEM, HBM, HBM],
        out_specs=VMEM,
        scratch_shapes=[
            pltpu.VMEM((requests, 3, slots, width), BF16),
            pltpu.VMEM(cache.shape, BF16),
            pltpu.SemaphoreType.DMA((requests, 2)),
        ],
        compiler_params=params(60),
        cost_estimate=cost(5e9, 6e6, 1.2e6),
        name="self_attention",
    )(counts, length, parents, buckets, bias_table.T, draft_qkv, cache)


def columns(ref, place_ref, pieces, j):
    lanes = ref.shape[-1] // pieces
    return pl.ds(pl.multiple_of(jnp.bitwise_xor(place_ref[1], j) * lanes, lanes), lanes)


def each_slice(stacks, orders):
    for stack, order in zip(stacks, orders):
        for at, k in enumerate(order):
            yield k, stack.at[at]


def join_columns(out_ref, slices, first, rows):
    for k, piece in slices:
        lanes = piece.shape[1]
        out_ref[:, k * lanes : (k + 1) * lanes] = piece[first : first + rows, :]


def self_out_kernel(ways, orders, place_ref, *refs):
    stacks = refs[: len(orders)]
    ctx_ref, hidden_ref, own_ref = refs[len(orders) : len(orders) + 3]
    out_refs = refs[-ways:-1]
    w_ref = refs[-1]
    pieces = sum(len(order) for order in orders)
    requests, share, model = hidden_ref.shape
    width = w_ref.shape[0]
    join_columns(w_ref, each_slice(stacks, orders), 0, width)
    for k in list(range(ways - 1, 0, -1)) + [0]:
        owner = jnp.bitwise_xor(place_ref[0], k)
        start = pl.multiple_of(owner * share, share)
        rows = ctx_ref[:, pl.ds(start, share), :]
        part = dot(rows.reshape(requests * share, width), w_ref[...])
        if k == 0:
            lanes = model // pieces
            for j in range(pieces):
                base = hidden_ref[:, :, columns(hidden_ref, place_ref, pieces, j)]
                base = base.astype(F32).reshape(requests * share, lanes)
                here = slice(j * lanes, (j + 1) * lanes)
                own_ref[:, here] = part[:, here] + base
        else:
            out_refs[k - 1][...] = part.astype(BF16)


def self_out(place, ctx, stacks, orders, hidden, ways):
    requests, share, model = hidden.shape
    rows = requests * share
    width = ctx.shape[2]
    return pl.pallas_call(
        functools.partial(self_out_kernel, ways, orders),
        out_shape=[jax.ShapeDtypeStruct((rows, model), F32)]
        + [jax.ShapeDtypeStruct((rows, model), BF16)] * (ways - 1),
        in_specs=[SMEM] + [VMEM] * (len(stacks) + 2),
        out_specs=[VMEM] * ways,
        scratch_shapes=[pltpu.VMEM((width, model), BF16)],
        compiler_params=params(),
        cost_estimate=cost(2 * rows * ways * width * model, 2e6),
        name="self_out",
    )(place, *stacks, ctx, hidden)


def norm_kernel(pieces, last, place_ref, own_ref, *refs):
    others = refs[:-3]
    gain_ref, stream_ref, normed_ref = refs[-3:]
    stream = own_ref[...]
    for other in others:
        stream = stream + other[...].astype(F32)
    lanes = stream.shape[1] // pieces
    scale = lax.rsqrt(jnp.mean(stream * stream, axis=-1, keepdims=True) + 1e-06)
    for j in range(pieces):
        here = slice(j * lanes, (j + 1) * lanes)
        there = columns(gain_ref, place_ref, pieces, j)
        stream_ref[:, there if last else here] = stream[:, here].astype(stream_ref.dtype)
        normed_ref[:, here] = (stream[:, here] * scale * gain_ref[:, there]).astype(BF16)


def norm(place, own, others, gain, pieces, last=False):
    return pl.pallas_call(
        functools.partial(norm_kernel, pieces, last),
        out_shape=[
            jax.ShapeDtypeStruct(own.shape, BF16 if last else F32),
            jax.ShapeDtypeStruct(own.shape, BF16),
        ],
        in_specs=[SMEM] + [VMEM] * (len(others) + 2),
        out_specs=[VMEM] * 2,
        compiler_params=params(),
        cost_estimate=cost(1e6, 2e6),
        name="norm",
    )(place, own, *others, gain.reshape(1, -1))


def cross_kernel(ways, orders, length_ref, cache_hbm, stream_ref, *refs):
    blocks = refs[:ways]
    stacks = refs[ways : -(ways + 5)]
    own_ref = refs[-(ways + 5)]
    out_refs = refs[-(ways + 4) : -5]
    wq_ref, wo_ref, ctx_ref, cache_ref, sems = refs[-5:]
    requests = cache_ref.shape[0]
    width = wq_ref.shape[1]
    heads = width // DH
    rows = blocks[0].shape[0]
    share = rows // requests
    copies = fetch_requests([(lambda r: cache_hbm.at[r], cache_ref)], sems)
    if orders:
        lanes = stacks[0].shape[2]
        parts = width // lanes
        for k, piece in each_slice(stacks, orders):
            for c in range(parts):
                here = slice(c * lanes, (c + 1) * lanes)
                at = width + c * lanes
                wq_ref[k * lanes : (k + 1) * lanes, here] = piece[at : at + lanes, :]
        join_columns(wo_ref, each_slice(stacks, orders), width + parts * lanes, width)
    else:
        wq_ref[...] = stacks[0][...]
        wo_ref[...] = stacks[1][...]
    query = [dot(block[...], wq_ref[...]).astype(BF16) for block in blocks]
    position = lax.broadcasted_iota(jnp.int32, (1, cache_ref.shape[2]), 1)
    for r in range(requests):
        for copy in copies[r]:
            copy.wait()
        here = slice(r * share, (r + 1) * share)
        queries = spread_heads(jnp.concatenate([q[here] for q in query], axis=0), heads)
        scores = dot_nt(queries, cache_ref[r, 0])
        scores = jnp.where(position < length_ref[r], scores, NEG)
        scores = jnp.exp(scores - scores.max(-1, keepdims=True))
        total = scores.sum(-1, keepdims=True)
        attended = dot(scores.astype(BF16), cache_ref[r, 1])
        ctx = gather_heads(attended / total, heads)
        ctx_ref[:, here, :] = ctx.reshape(ways, share, width)
    for k in list(range(ways - 1, 0, -1)) + [0]:
        part = dot(ctx_ref[k], wo_ref[...])
        if k == 0:
            own_ref[...] = part + stream_ref[...]
        else:
            out_refs[k - 1][...] = part.astype(BF16)


def cross_layer(blocks, stacks, orders, cache, stream, length):
    ways = len(blocks)
    rows, model = blocks[0].shape
    width = cache.shape[3]
    return pl.pallas_call(
        functools.partial(cross_kernel, ways, orders),
        out_shape=[jax.ShapeDtypeStruct((rows, model), F32)]
        + [jax.ShapeDtypeStruct((rows, model), BF16)] * (ways - 1),
        in_specs=[SMEM, HBM] + [VMEM] * (1 + ways + len(stacks)),
        out_specs=[VMEM] * ways,
        scratch_shapes=[
            pltpu.VMEM((model, width), BF16),
            pltpu.VMEM((width, model), BF16),
            pltpu.VMEM((ways, rows, width), BF16),
            pltpu.VMEM(cache.shape, BF16),
            pltpu.SemaphoreType.DMA((cache.shape[0], 1)),
        ],
        compiler_params=params(54),
        cost_estimate=cost(5e9, 8e6, 1.2e6),
        name="cross_layer",
    )(length, cache, stream, *blocks, *stacks)


def join_kernel(place_ref, slices_ref, out_ref):
    pieces, _, lanes = slices_ref.shape
    for k in range(pieces):
        source = jnp.bitwise_xor(place_ref[1], k)
        out_ref[:, k * lanes : (k + 1) * lanes] = slices_ref[source]


def join(place, slices):
    pieces, rows, lanes = slices.shape
    return pl.pallas_call(
        join_kernel,
        out_shape=jax.ShapeDtypeStruct((rows, lanes * pieces), BF16),
        in_specs=[SMEM, VMEM],
        out_specs=VMEM,
        compiler_params=params(),
        cost_estimate=cost(1e3, 4 * rows * lanes * pieces),
        name="join",
    )(place, slices)


def ffn_kernel(block_ref, w_ref, *refs):
    hidden = w_ref.shape[0] // 3
    gate = dot_nt(block_ref[...], w_ref[:hidden, :])
    up = dot_nt(block_ref[...], w_ref[hidden : 2 * hidden, :])
    gated = (jax.nn.gelu(gate, approximate=True) * up).astype(BF16)
    part = dot(gated, w_ref[2 * hidden :, :])
    if len(refs) == 2:
        part = part + refs[0][...]
    refs[-1][...] = part.astype(refs[-1].dtype)


def ffn(block, w, stream=None):
    rows, model = block.shape
    given = [] if stream is None else [stream]
    return pl.pallas_call(
        ffn_kernel,
        out_shape=jax.ShapeDtypeStruct((rows, model), F32 if given else BF16),
        in_specs=[VMEM] * (2 + len(given)),
        out_specs=VMEM,
        compiler_params=params(),
        cost_estimate=cost(2 * rows * w.size, 6e6, 1e5),
        name="ffn",
    )(block, w, *given)


def project_kernel(ways, place_ref, *refs):
    blocks, slices_ref, out_ref, w_ref = refs[:ways], *refs[ways:]
    _, count, slots, width = out_ref.shape
    share = slots // ways
    pieces, _, depth, _ = slices_ref.shape
    for k in range(pieces):
        source = jnp.bitwise_xor(place_ref[1], k) if pieces > 1 else 0
        w_ref[:, k * depth : (k + 1) * depth, :] = slices_ref[source]
    for k in range(ways):
        start = pl.multiple_of(jnp.bitwise_xor(place_ref[0], k) * share, share)
        for c in range(3):
            projected = dot(blocks[k][...], w_ref[c]).astype(BF16)
            out_ref[c, :, pl.ds(start, share), :] = projected.reshape(count, share, width)


def project(place, blocks, slices, count, share):
    ways = len(blocks)
    rows, model = blocks[0].shape
    width = slices.shape[3]
    return pl.pallas_call(
        functools.partial(project_kernel, ways),
        out_shape=jax.ShapeDtypeStruct((3, count, share * ways, width), BF16),
        in_specs=[SMEM] + [VMEM] * (ways + 1),
        out_specs=VMEM,
        scratch_shapes=[pltpu.VMEM((3, model, width), BF16)],
        compiler_params=params(),
        cost_estimate=cost(6 * rows * ways * model * width, 4e6),
        name="project",
    )(place, *blocks, slices)


ATTN_ORDERS = ((0, 4, 6, 2), (1, 5, 7, 3))


def gate(*values):
    return lax.optimization_barrier(values)


def partner(value, axis, size, k):
    return lax.ppermute(value, axis, [(i, i ^ k) for i in range(size)])


def all_slices(shard):
    return lax.all_gather(shard, "tok", axis=0, tiled=False)


def along(value, k):
    return partner(value, "tok", 8, k)


def send_each(parts, ways):
    return [partner(part, "grp", ways, k) for k, part in zip(range(1, ways), parts)]


def spread(block, ways):
    return [block] + send_each([block] * (ways - 1), ways)


def shards(
    ways,
    total,
    hidden,
    draft_qkv,
    self_cache,
    cross_cache,
    parents,
    counts,
    self_len,
    enc_len,
    buckets,
    bias_table,
    gain_cross,
    gain_ffn,
    gain_next,
    w_out_self,
    w_query_cross,
    w_out_cross,
    w_gate,
    w_up,
    w_down,
    w_qkv,
):
    requests, share, model = hidden.shape
    slice_lanes = model // total
    head_width = w_query_cross.shape[1]
    place = jnp.stack([lax.axis_index("grp"), lax.axis_index("tok")]).astype(jnp.int32)
    paired = total == 8 and slice_lanes == 128 and head_width % slice_lanes == 0
    qkv_shard = jnp.transpose(w_qkv, (1, 0, 2))
    if not paired:
        by_row = functools.partial(lax.all_gather, axis_name="tok", axis=0, tiled=True)
        by_col = functools.partial(lax.all_gather, axis_name="tok", axis=1, tiled=True)
        whole = ((0,),)
        ctx = self_attention(draft_qkv, self_cache, parents, counts, buckets, bias_table, self_len)
        own, *parts = self_out(place, ctx, [by_col(w_out_self)[None]], whole, hidden, ways)
        stream, normed = norm(place, own, send_each(parts, ways), gain_cross, 1)
        attn_w = [by_row(w_query_cross), by_col(w_out_cross)]
        own, *parts = cross_layer(spread(normed, ways), attn_w, (), cross_cache, stream, enc_len)
        stream, normed = norm(place, own, send_each(parts, ways), gain_ffn, 1)
        ffn_w = jnp.concatenate([by_row(w_gate).T, by_row(w_up).T, by_col(w_down)], axis=0)
        others = spread(normed, ways)[1:]
        own = ffn(normed, ffn_w, stream)
        parts = [ffn(block, ffn_w) for block in others]
        stream, normed = norm(place, own, send_each(parts, ways), gain_next, 1, True)
        qkv_w = by_col(qkv_shard)[None]
        next_qkv = project(place, spread(normed, ways), qkv_w, requests, share)
        return stream.reshape(requests, share, model), next_qkv

    pieces = total
    query_slices = jnp.split(w_query_cross, head_width // slice_lanes, axis=1)
    attn_shard = jnp.concatenate([w_out_self] + query_slices + [w_out_cross], axis=0)
    ffn_shard = jnp.concatenate([w_gate.T, w_up.T, w_down], axis=0)
    attn_here = [attn_shard] + [along(attn_shard, k) for k in (4, 6, 2)]
    ctx = self_attention(draft_qkv, self_cache, parents, counts, buckets, bias_table, self_len)
    ctx, ffn_shard, qkv_shard, *attn_here = gate(ctx, ffn_shard, qkv_shard, *attn_here)
    ffn_w = all_slices(ffn_shard)
    attn_here = jnp.stack(attn_here)
    attn_w = [attn_here, along(attn_here, 1)]
    own, *parts = self_out(place, ctx, attn_w, ATTN_ORDERS, hidden, ways)
    own, qkv_shard, *parts = gate(own, qkv_shard, *parts)
    qkv_w = all_slices(qkv_shard)
    stream, normed = norm(place, own, send_each(parts, ways), gain_cross, pieces)
    blocks = spread(normed, ways)
    own, *parts = cross_layer(blocks, attn_w, ATTN_ORDERS, cross_cache, stream, enc_len)
    stream, normed = norm(place, own, send_each(parts, ways), gain_ffn, pieces)
    blocks = spread(normed, ways)
    ffn_w = join(place, ffn_w)
    own = ffn(normed, ffn_w, stream)
    parts = [ffn(block, ffn_w) for block in blocks[1:]]
    stream, normed = norm(place, own, send_each(parts, ways), gain_next, pieces, True)
    blocks = spread(normed, ways)
    next_qkv = project(place, blocks, qkv_w, requests, share)
    return stream.reshape(requests, share, model), next_qkv


def solution(mesh):
    in_specs = (
        P("tok", "grp", None),
        P(None, "tok", None, "grp"),
        P("tok", None, None, "grp"),
        P("tok", None, None, "grp"),
        P("tok", None),
        P("tok"),
        P("tok"),
        P("tok"),
        P("tok", None, None),
        P(None, "grp"),
        P(),
        P(),
        P(),
        P("grp", "tok"),
        P("tok", "grp"),
        P("grp", "tok"),
        P("tok", "grp"),
        P("tok", "grp"),
        P("grp", "tok"),
        P("tok", None, "grp"),
    )
    out_specs = (P("tok", "grp", None), P(None, "tok", None, "grp"))
    body = functools.partial(shards, mesh.shape["grp"], mesh.shape["tok"])
    return jax.shard_map(body, mesh=mesh, in_specs=in_specs, out_specs=out_specs, check_vma=False)
```

time: 271 us -> 135 us (0.50)
  waiting for transfers between devices: 141 us -> 49.6 us
  blocking collectives: 44.1 us -> 0 us
  Pallas kernels: 0 us -> 32.3 us
  starting transfers between devices: 0.29 us -> 28.2 us
  matrix products: 25.9 us -> 0 us
  local copies, waits for them, and re-layouts: 30.9 us -> 7.15 us
  other arithmetic: 12.4 us -> 1.9 us
    psum x3 -> x0, waiting for transfers between devices: 116 us -> none  [layer_sum(): lax.psum(summand.astype(jnp.bfloat16), 'grp').astype(jnp.float32)]
    ppermute x0 -> x22, waiting for transfers between devices: none -> 49.6 us  [partner(): return lax.ppermute(value, axis, [(i, i ^ k) for i in range(size)])]
    all_gather x3 -> x0, blocking collectives: 44.1 us -> none  [the longest x1 15.6 us: shards(): lax.all_gather(w_out_self, 'tok', axis=1, tiled=True)]
    pallas_call x0 -> x12, Pallas kernels: none -> 32.3 us  [the longest x1 9.43 us: cross_layer(): pl.pallas_call(functools.partial(cross_kernel, ways, orders), out_shape=[...]
    ppermute x0 -> x22, starting transfers between devices: none -> 27.9 us  [partner(): return lax.ppermute(value, axis, [(i, i ^ k) for i in range(size)])]
    dot_general x20 -> x0, matrix products: 25.9 us -> none  [the longest x1 5.23 us: shards(): jnp.dot(gated, fetched[5], preferred_element_type=jnp.float32)]
    all_gather x4 -> x2, waiting for transfers between devices: 23.1 us -> 0.01 us  [all_slices(): return lax.all_gather(shard, 'tok', axis=0, tiled=False)]
    slice x8 -> x0, local copies, waits for them, and re-layouts: 20.4 us -> none  [the longest x2 6.79 us: cross_attention(): enc_keys = cached[:, 0].reshape(requests, -1, local_heads, DH)]
  transfers between devices with their start and end apart: 7 -> 24, of which waited for: 4 -> 15; matrix products, arithmetic and copies ran while one was open for 7% -> 1% of each run, Pallas kernels for 0% -> 22%
where the time goes in v2:
time: 135 us; the launch traced here: 133 us
  waiting for transfers between devices  49.6 us (37%)
  Pallas kernels  32.3 us (24%)
  starting transfers between devices  28.2 us (21%)
  between operations  14.3 us (11%)
  local copies, waits for them, and re-layouts  7.15 us (5%)
  other arithmetic  1.9 us (1%)
    ppermute x22, waiting for transfers between devices, partner(): return lax.ppermute(value, axis, [(i, i ^ k) for i in range(size)])  49.6 us
    ppermute x22, starting transfers between devices, partner(): return lax.ppermute(value, axis, [(i, i ^ k) for i in range(size)])  27.9 us
    pallas_call x1, Pallas kernels, cross_layer(): pl.pallas_call(functools.partial(cross_kernel, ways, orders), out_shape=[...  9.43 us
    pallas_call x1, Pallas kernels, self_attention(): pl.pallas_call(self_kernel, out_shape=jax.ShapeDtypeStruct((requests, slo...  9.29 us
    unnamed x36, local copies, waits for them, and re-layouts  6.37 us
    pallas_call x4, Pallas kernels, ffn(): pl.pallas_call(ffn_kernel, out_shape=jax.ShapeDtypeStruct((rows, model),...  5.2 us
    pallas_call x3, Pallas kernels, norm(): pl.pallas_call(functools.partial(norm_kernel, pieces, last), out_shape=[j...  3.02 us
  transfers between devices with their start and end apart: 24, of which 15 were waited for; matrix products, arithmetic and copies ran while one was open for 1% of the time, Pallas kernels for 22%

profile of v2, /device:TPU:0, one launch (start us, length us, event | category | flops | bytes accessed | tf_op | source)
XLA Modules:
  0.0 133.4 jit_solution(2366806884657451811)
XLA Ops:
  8.9 4.1 %collective-permute-start = (bf16[768,128]{1,0:T(8,128)(2,1)S(1)}, bf16[768,128]{1,0:T(8,128)(2,1)S(1)}, u32[]{:S(2)}, u32[]{:S(2)}) collective-permute-start(bf16[768,128]{1,0:T(8,128)(2,1)S(1)} %pad_maximum_fusion.2), channel_id=1, source_target_pairs={{0,4},{1,5},{2,6},{3,7},{4,0},{5,1},{6,2},{7,3},{8,12},{9,13},{10,... | collective-permute-start | bytes 589832 | tf_op jit(solution)/shard_map/ppermute | solution.py:387
  14.6 9.3 %self_attention.1.refs_2_ = bf16[8,64,256]{2,1,0:T(8,128)(2,1)} custom-call(s32[8]{0:T(128)} %counts_ref.1, s32[8]{0:T(128)} %length_ref.2, s32[8,64]{1,0:T(8,128)} %parents_ref.1, s32[8,64,64]{2,1,0:T(8,128)} %buckets_ref.1, f32[4,32]{1,0:T(4,128)} %bitcast.29, bf16[3,8,64,256]{3,2,1,0:T(8,128)(2,1)} %qkv_hbm.1, bf16[8,2,512,256]{3,2,1,0:T(8,128)(2,1)} %cache_hbm.2), custom_call_target="tpu_custom_call" | custom-call | flops 5000000000 | bytes 6000000 | tf_op jit(solution)/shard_map/self_attention/pallas_call | solution.py:129
  24.8 2.4 %collective-permute-done = bf16[768,128]{1,0:T(8,128)(2,1)S(1)} collective-permute-done((bf16[768,128]{1,0:T(8,128)(2,1)S(1)}, bf16[768,128]{1,0:T(8,128)(2,1)S(1)}, u32[]{:S(2)}, u32[]{:S(2)}) %collective-permute-start) | collective-permute-done | bytes 196640 | tf_op jit(solution)/shard_map/ppermute | solution.py:387
  28.2 2.2 %collective-permute-done.3.refs_1_.refs_5_ = bf16[4,768,128]{2,1,0:T(8,128)(2,1)S(1)} collective-permute-done((bf16[4,768,128]{2,1,0:T(8,128)(2,1)S(1)}, bf16[4,768,128]{2,1,0:T(8,128)(2,1)S(1)}, u32[]{:S(2)}, u32[]{:S(2)}) %collective-permute-start.3) | collective-permute-done | bytes 786464 | tf_op jit(solution)/shard_map/ppermute | solution.py:387
  31.5 1.6 %collective-permute-start.4 = (bf16[128,1024]{1,0:T(8,128)(2,1)S(1)}, bf16[128,1024]{1,0:T(8,128)(2,1)S(1)}, u32[]{:S(2)}, u32[]{:S(2)}) collective-permute-start(bf16[128,1024]{1,0:T(8,128)(2,1)S(1)} %get-tuple-element.39), channel_id=1, source_target_pairs={{0,8},{8,0},{16,24},{24,16},{1,9},{9,1},{17,25},{25,17},{2,10},{10... | collective-permute-start | bytes 786440 | tf_op jit(solution)/shard_map/ppermute | solution.py:387
  33.1 1.5 %collective-permute-start.5 = (bf16[128,1024]{1,0:T(8,128)(2,1)S(1)}, bf16[128,1024]{1,0:T(8,128)(2,1)S(1)}, u32[]{:S(2)}, u32[]{:S(2)}) collective-permute-start(bf16[128,1024]{1,0:T(8,128)(2,1)S(1)} %get-tuple-element.40), channel_id=1, source_target_pairs={{0,16},{8,24},{16,0},{24,8},{1,17},{9,25},{17,1},{25,9},{2,18},{10... | collective-permute-start | bytes 786440 | tf_op jit(solution)/shard_map/ppermute | solution.py:387
  35.1 5.7 %collective-permute-done.4.refs_0_ = bf16[128,1024]{1,0:T(8,128)(2,1)S(1)} collective-permute-done((bf16[128,1024]{1,0:T(8,128)(2,1)S(1)}, bf16[128,1024]{1,0:T(8,128)(2,1)S(1)}, u32[]{:S(2)}, u32[]{:S(2)}) %collective-permute-start.4) | collective-permute-done | bytes 262176 | tf_op jit(solution)/shard_map/ppermute | solution.py:387
  40.8 6.1 %collective-permute-done.5.refs_1_ = bf16[128,1024]{1,0:T(8,128)(2,1)S(1)} collective-permute-done((bf16[128,1024]{1,0:T(8,128)(2,1)S(1)}, bf16[128,1024]{1,0:T(8,128)(2,1)S(1)}, u32[]{:S(2)}, u32[]{:S(2)}) %collective-permute-start.5) | collective-permute-done | bytes 262176 | tf_op jit(solution)/shard_map/ppermute | solution.py:387
  52.0 5.8 %collective-permute-done.7.refs_1_ = bf16[128,1024]{1,0:T(8,128)(2,1)S(1)} collective-permute-done((bf16[128,1024]{1,0:T(8,128)(2,1)S(1)}, bf16[128,1024]{1,0:T(8,128)(2,1)S(1)}, u32[]{:S(2)}, u32[]{:S(2)}) %collective-permute-start.7) | collective-permute-done | bytes 262176 | tf_op jit(solution)/shard_map/ppermute | solution.py:387
  57.7 4.9 %collective-permute-done.8.refs_2_ = bf16[128,1024]{1,0:T(8,128)(2,1)S(1)} collective-permute-done((bf16[128,1024]{1,0:T(8,128)(2,1)S(1)}, bf16[128,1024]{1,0:T(8,128)(2,1)S(1)}, u32[]{:S(2)}, u32[]{:S(2)}) %collective-permute-start.8) | collective-permute-done | bytes 262176 | tf_op jit(solution)/shard_map/ppermute | solution.py:387
  63.5 9.4 %cross_layer.1 = (f32[128,1024]{1,0:T(8,128)}, bf16[128,1024]{1,0:T(8,128)(2,1)}, bf16[128,1024]{1,0:T(8,128)(2,1)}, bf16[128,1024]{1,0:T(8,128)(2,1)}) custom-call(s32[8]{0:T(128)} %length_ref.3, bf16[8,2,512,256]{3,2,1,0:T(8,128)(2,1)} %cache_hbm.3, f32[128,1024]{1,0:T(8,128)} %copy-done.10, bf16[128,1024]{1,0:T(8,128)(2,1)} %copy-done.11, ...), custom_call_target="tpu_custom_call" | custom-call | flops 5000000000 | bytes 8000000 | tf_op jit(solution)/shard_map/cross_layer/pallas_call | solution.py:284
  74.9 1.6 %collective-permute-start.12 = (bf16[128,1024]{1,0:T(8,128)(2,1)}, bf16[128,1024]{1,0:T(8,128)(2,1)S(1)}, u32[]{:S(2)}, u32[]{:S(2)}) collective-permute-start(bf16[128,1024]{1,0:T(8,128)(2,1)} %get-tuple-element.47), channel_id=1, source_target_pairs={{0,24},{8,16},{16,8},{24,0},{1,25},{9,17},{17,9},{25,1},{2,26},{10... | collective-permute-start | bytes 786440 | tf_op jit(solution)/shard_map/ppermute | solution.py:387
  76.5 5.6 %collective-permute-done.10.refs_0_ = bf16[128,1024]{1,0:T(8,128)(2,1)S(1)} collective-permute-done((bf16[128,1024]{1,0:T(8,128)(2,1)}, bf16[128,1024]{1,0:T(8,128)(2,1)S(1)}, u32[]{:S(2)}, u32[]{:S(2)}) %collective-permute-start.10) | collective-permute-done | bytes 262176 | tf_op jit(solution)/shard_map/ppermute | solution.py:387
  82.1 3.2 %collective-permute-done.11.refs_1_ = bf16[128,1024]{1,0:T(8,128)(2,1)S(1)} collective-permute-done((bf16[128,1024]{1,0:T(8,128)(2,1)}, bf16[128,1024]{1,0:T(8,128)(2,1)S(1)}, u32[]{:S(2)}, u32[]{:S(2)}) %collective-permute-start.11) | collective-permute-done | bytes 262176 | tf_op jit(solution)/shard_map/ppermute | solution.py:387
  87.2 1.7 %collective-permute-start.13 = (bf16[128,1024]{1,0:T(8,128)(2,1)S(1)}, bf16[128,1024]{1,0:T(8,128)(2,1)S(1)}, u32[]{:S(2)}, u32[]{:S(2)}) collective-permute-start(bf16[128,1024]{1,0:T(8,128)(2,1)S(1)} %get-tuple-element.48.block_ref), channel_id=1, source_target_pairs={{0,8},{8,0},{16,24},{24,16},{1,9},{9,1},{17,25},{25,17},{2,10},{10... | collective-permute-start | bytes 786440 | tf_op jit(solution)/shard_map/ppermute | solution.py:387
  90.7 2.2 %copy-done = bf16[16896,128]{1,0:T(8,128)(2,1)S(1)} copy-done((bf16[16896,128]{1,0:T(8,128)(2,1)S(1)}, bf16[16896,128]{1,0:T(8,128)(2,1)}, u32[]{:S(2)}) %copy-start) | copy-done | bytes 4325400
  93.0 1.8 %join.1.w_ref = bf16[2112,1024]{1,0:T(8,128)(2,1)S(1)} custom-call(s32[2]{0:T(128)S(1)} %pad_add_fusion.place_ref, bf16[8,2112,128]{2,1,0:T(8,128)(2,1)S(1)} %bitcast.16), custom_call_target="tpu_custom_call" | custom-call | flops 1000 | bytes 8650752 | tf_op jit(solution)/shard_map/join/pallas_call | solution.py:312
  96.8 1.8 %collective-permute-start.14 = (bf16[128,1024]{1,0:T(8,128)(2,1)S(1)}, bf16[128,1024]{1,0:T(8,128)(2,1)S(1)}, u32[]{:S(2)}, u32[]{:S(2)}) collective-permute-start(bf16[128,1024]{1,0:T(8,128)(2,1)S(1)} %ffn.5), channel_id=1, source_target_pairs={{0,8},{8,0},{16,24},{24,16},{1,9},{9,1},{17,25},{25,17},{2,10},{10... | collective-permute-start | bytes 786440 | tf_op jit(solution)/shard_map/ppermute | solution.py:387
  102.5 2.7 %collective-permute-start.18 = (bf16[128,1024]{1,0:T(8,128)(2,1)S(1)}, bf16[128,1024]{1,0:T(8,128)(2,1)S(1)}, u32[]{:S(2)}, u32[]{:S(2)}) collective-permute-start(bf16[128,1024]{1,0:T(8,128)(2,1)S(1)} %ffn.7), channel_id=1, source_target_pairs={{0,24},{8,16},{16,8},{24,0},{1,25},{9,17},{17,9},{25,1},{2,26},{10... | collective-permute-start | bytes 786440 | tf_op jit(solution)/shard_map/ppermute | solution.py:387
  106.5 4.9 %collective-permute-done.16.refs_1_ = bf16[128,1024]{1,0:T(8,128)(2,1)S(1)} collective-permute-done((bf16[128,1024]{1,0:T(8,128)(2,1)S(1)}, bf16[128,1024]{1,0:T(8,128)(2,1)S(1)}, u32[]{:S(2)}, u32[]{:S(2)}) %collective-permute-start.16) | collective-permute-done | bytes 262176 | tf_op jit(solution)/shard_map/ppermute | solution.py:387
  114.5 1.9 %collective-permute-start.21 = (bf16[128,1024]{1,0:T(8,128)(2,1)S(1)}, bf16[128,1024]{1,0:T(8,128)(2,1)S(1)}, u32[]{:S(2)}, u32[]{:S(2)}) collective-permute-start(bf16[128,1024]{1,0:T(8,128)(2,1)S(1)} %get-tuple-element.52.refs_0_), channel_id=1, source_target_pairs={{0,24},{8,16},{16,8},{24,0},{1,25},{9,17},{17,9},{25,1},{2,26},{10... | collective-permute-start | bytes 786440 | tf_op jit(solution)/shard_map/ppermute | solution.py:387
  116.4 2.9 %collective-permute-done.19.refs_1_ = bf16[128,1024]{1,0:T(8,128)(2,1)S(1)} collective-permute-done((bf16[128,1024]{1,0:T(8,128)(2,1)S(1)}, bf16[128,1024]{1,0:T(8,128)(2,1)S(1)}, u32[]{:S(2)}, u32[]{:S(2)}) %collective-permute-start.19) | collective-permute-done | bytes 262176 | tf_op jit(solution)/shard_map/ppermute | solution.py:387
  119.3 2.7 %collective-permute-done.20.refs_2_ = bf16[128,1024]{1,0:T(8,128)(2,1)S(1)} collective-permute-done((bf16[128,1024]{1,0:T(8,128)(2,1)S(1)}, bf16[128,1024]{1,0:T(8,128)(2,1)S(1)}, u32[]{:S(2)}, u32[]{:S(2)}) %collective-permute-start.20) | collective-permute-done | bytes 262176 | tf_op jit(solution)/shard_map/ppermute | solution.py:387
  124.1 2.5 %project.1 = bf16[3,8,64,256]{3,2,1,0:T(8,128)(2,1)} custom-call(s32[2]{0:T(128)S(1)} %pad_add_fusion.place_ref, bf16[128,1024]{1,0:T(8,128)(2,1)S(1)} %get-tuple-element.52.refs_0_, bf16[128,1024]{1,0:T(8,128)(2,1)S(1)} %collective-permute-done.19.refs_1_, bf16[128,1024]{1,0:T(8,128)(2,1)S(1)} %collective-permute-done.20.refs_2_, ...), custom_call_target="tpu_custom_call" | custom-call | flops 805306368 | bytes 4000000 | tf_op jit(solution)/shard_map/project/pallas_call | solution.py:367
  (79 shorter events, 30.6 us)
Async XLA Ops:
  7.2 83.6 %all-gather.5.cloned.1.call-start = ((), (), s32[]{:S(2)}) async-start(), calls=%async_computation | async-start | bytes 4866048 | tf_op jit(solution)/shard_map/all_gather | solution.py:391
  8.9 18.3 %collective-permute-start = (bf16[768,128]{1,0:T(8,128)(2,1)S(1)}, bf16[768,128]{1,0:T(8,128)(2,1)S(1)}, u32[]{:S(2)}, u32[]{:S(2)}) collective-permute-start(bf16[768,128]{1,0:T(8,128)(2,1)S(1)} %pad_maximum_fusion.2), channel_id=1, source_target_pairs={{0,4},{1,5},{2,6},{3,7},{4,0},{5,1},{6,2},{7,3},{8,12},{9,13},{10,... | collective-permute-start | bytes 589832 | tf_op jit(solution)/shard_map/ppermute | solution.py:387
  13.0 14.2 %collective-permute-start.1 = (bf16[768,128]{1,0:T(8,128)(2,1)S(1)}, bf16[768,128]{1,0:T(8,128)(2,1)S(1)}, u32[]{:S(2)}, u32[]{:S(2)}) collective-permute-start(bf16[768,128]{1,0:T(8,128)(2,1)S(1)} %pad_maximum_fusion.2), channel_id=1, source_target_pairs={{0,6},{1,7},{2,4},{3,5},{4,2},{5,3},{6,0},{7,1},{8,14},{9,15},{10,... | collective-permute-start | bytes 589832 | tf_op jit(solution)/shard_map/ppermute | solution.py:387
  14.3 13.4 %collective-permute-start.2 = (bf16[768,128]{1,0:T(8,128)(2,1)S(1)}, bf16[768,128]{1,0:T(8,128)(2,1)S(1)}, u32[]{:S(2)}, u32[]{:S(2)}) collective-permute-start(bf16[768,128]{1,0:T(8,128)(2,1)S(1)} %pad_maximum_fusion.2), channel_id=1, source_target_pairs={{0,2},{1,3},{2,0},{3,1},{4,6},{5,7},{6,4},{7,5},{8,10},{9,11},{10,... | collective-permute-start | bytes 589832 | tf_op jit(solution)/shard_map/ppermute | solution.py:387
  27.7 88.7 %all-gather.7.cloned.1.call-start = ((), (), s32[]{:S(2)}) async-start(), calls=%async_computation.1 | async-start | bytes 1769472 | tf_op jit(solution)/shard_map/all_gather | solution.py:391
  28.1 2.4 %collective-permute-start.3 = (bf16[4,768,128]{2,1,0:T(8,128)(2,1)S(1)}, bf16[4,768,128]{2,1,0:T(8,128)(2,1)S(1)}, u32[]{:S(2)}, u32[]{:S(2)}) collective-permute-start(bf16[4,768,128]{2,1,0:T(8,128)(2,1)S(1)} %pad_maximum_fusion.refs_0_.refs_4_), channel_id=1, source_target_pairs={{0,1},{1,0},{2,3},{3,2},{4,5},{5,4},{6,7},{7,6},{8,9},{9,8},{10,11... | collective-permute-start | bytes 2359304 | tf_op jit(solution)/shard_map/ppermute | solution.py:387
  31.5 9.2 %collective-permute-start.4 = (bf16[128,1024]{1,0:T(8,128)(2,1)S(1)}, bf16[128,1024]{1,0:T(8,128)(2,1)S(1)}, u32[]{:S(2)}, u32[]{:S(2)}) collective-permute-start(bf16[128,1024]{1,0:T(8,128)(2,1)S(1)} %get-tuple-element.39), channel_id=1, source_target_pairs={{0,8},{8,0},{16,24},{24,16},{1,9},{9,1},{17,25},{25,17},{2,10},{10... | collective-permute-start | bytes 786440 | tf_op jit(solution)/shard_map/ppermute | solution.py:387
  33.1 13.7 %collective-permute-start.5 = (bf16[128,1024]{1,0:T(8,128)(2,1)S(1)}, bf16[128,1024]{1,0:T(8,128)(2,1)S(1)}, u32[]{:S(2)}, u32[]{:S(2)}) collective-permute-start(bf16[128,1024]{1,0:T(8,128)(2,1)S(1)} %get-tuple-element.40), channel_id=1, source_target_pairs={{0,16},{8,24},{16,0},{24,8},{1,17},{9,25},{17,1},{25,9},{2,18},{10... | collective-permute-start | bytes 786440 | tf_op jit(solution)/shard_map/ppermute | solution.py:387
  34.7 12.2 %collective-permute-start.6 = (bf16[128,1024]{1,0:T(8,128)(2,1)S(1)}, bf16[128,1024]{1,0:T(8,128)(2,1)S(1)}, u32[]{:S(2)}, u32[]{:S(2)}) collective-permute-start(bf16[128,1024]{1,0:T(8,128)(2,1)S(1)} %get-tuple-element.41), channel_id=1, source_target_pairs={{0,24},{8,16},{16,8},{24,0},{1,25},{9,17},{17,9},{25,1},{2,26},{10... | collective-permute-start | bytes 786440 | tf_op jit(solution)/shard_map/ppermute | solution.py:387
  48.5 9.2 %collective-permute-start.7 = (bf16[128,1024]{1,0:T(8,128)(2,1)S(1)}, bf16[128,1024]{1,0:T(8,128)(2,1)S(1)}, u32[]{:S(2)}, u32[]{:S(2)}) collective-permute-start(bf16[128,1024]{1,0:T(8,128)(2,1)S(1)} %get-tuple-element.43.refs_0_), channel_id=1, source_target_pairs={{0,8},{8,0},{16,24},{24,16},{1,9},{9,1},{17,25},{25,17},{2,10},{10... | collective-permute-start | bytes 786440 | tf_op jit(solution)/shard_map/ppermute | solution.py:387
  49.7 13.0 %collective-permute-start.8 = (bf16[128,1024]{1,0:T(8,128)(2,1)S(1)}, bf16[128,1024]{1,0:T(8,128)(2,1)S(1)}, u32[]{:S(2)}, u32[]{:S(2)}) collective-permute-start(bf16[128,1024]{1,0:T(8,128)(2,1)S(1)} %get-tuple-element.43.refs_0_), channel_id=1, source_target_pairs={{0,16},{8,24},{16,0},{24,8},{1,17},{9,25},{17,1},{25,9},{2,18},{10... | collective-permute-start | bytes 786440 | tf_op jit(solution)/shard_map/ppermute | solution.py:387
  50.5 12.1 %collective-permute-start.9 = (bf16[128,1024]{1,0:T(8,128)(2,1)S(1)}, bf16[128,1024]{1,0:T(8,128)(2,1)S(1)}, u32[]{:S(2)}, u32[]{:S(2)}) collective-permute-start(bf16[128,1024]{1,0:T(8,128)(2,1)S(1)} %get-tuple-element.43.refs_0_), channel_id=1, source_target_pairs={{0,24},{8,16},{16,8},{24,0},{1,25},{9,17},{17,9},{25,1},{2,26},{10... | collective-permute-start | bytes 786440 | tf_op jit(solution)/shard_map/ppermute | solution.py:387
  72.9 9.2 %collective-permute-start.10 = (bf16[128,1024]{1,0:T(8,128)(2,1)}, bf16[128,1024]{1,0:T(8,128)(2,1)S(1)}, u32[]{:S(2)}, u32[]{:S(2)}) collective-permute-start(bf16[128,1024]{1,0:T(8,128)(2,1)} %get-tuple-element.45), channel_id=1, source_target_pairs={{0,8},{8,0},{16,24},{24,16},{1,9},{9,1},{17,25},{25,17},{2,10},{10... | collective-permute-start | bytes 786440 | tf_op jit(solution)/shard_map/ppermute | solution.py:387
  73.5 11.8 %collective-permute-start.11 = (bf16[128,1024]{1,0:T(8,128)(2,1)}, bf16[128,1024]{1,0:T(8,128)(2,1)S(1)}, u32[]{:S(2)}, u32[]{:S(2)}) collective-permute-start(bf16[128,1024]{1,0:T(8,128)(2,1)} %get-tuple-element.46), channel_id=1, source_target_pairs={{0,16},{8,24},{16,0},{24,8},{1,17},{9,25},{17,1},{25,9},{2,18},{10... | collective-permute-start | bytes 786440 | tf_op jit(solution)/shard_map/ppermute | solution.py:387
  74.9 10.4 %collective-permute-start.12 = (bf16[128,1024]{1,0:T(8,128)(2,1)}, bf16[128,1024]{1,0:T(8,128)(2,1)S(1)}, u32[]{:S(2)}, u32[]{:S(2)}) collective-permute-start(bf16[128,1024]{1,0:T(8,128)(2,1)} %get-tuple-element.47), channel_id=1, source_target_pairs={{0,24},{8,16},{16,8},{24,0},{1,25},{9,17},{17,9},{25,1},{2,26},{10... | collective-permute-start | bytes 786440 | tf_op jit(solution)/shard_map/ppermute | solution.py:387
  87.2 8.3 %collective-permute-start.13 = (bf16[128,1024]{1,0:T(8,128)(2,1)S(1)}, bf16[128,1024]{1,0:T(8,128)(2,1)S(1)}, u32[]{:S(2)}, u32[]{:S(2)}) collective-permute-start(bf16[128,1024]{1,0:T(8,128)(2,1)S(1)} %get-tuple-element.48.block_ref), channel_id=1, source_target_pairs={{0,8},{8,0},{16,24},{24,16},{1,9},{9,1},{17,25},{25,17},{2,10},{10... | collective-permute-start | bytes 786440 | tf_op jit(solution)/shard_map/ppermute | solution.py:387
  88.9 9.6 %collective-permute-start.15 = (bf16[128,1024]{1,0:T(8,128)(2,1)S(1)}, bf16[128,1024]{1,0:T(8,128)(2,1)S(1)}, u32[]{:S(2)}, u32[]{:S(2)}) collective-permute-start(bf16[128,1024]{1,0:T(8,128)(2,1)S(1)} %get-tuple-element.48.block_ref), channel_id=1, source_target_pairs={{0,16},{8,24},{16,0},{24,8},{1,17},{9,25},{17,1},{25,9},{2,18},{10... | collective-permute-start | bytes 786440 | tf_op jit(solution)/shard_map/ppermute | solution.py:387
  89.3 11.9 %collective-permute-start.17 = (bf16[128,1024]{1,0:T(8,128)(2,1)S(1)}, bf16[128,1024]{1,0:T(8,128)(2,1)S(1)}, u32[]{:S(2)}, u32[]{:S(2)}) collective-permute-start(bf16[128,1024]{1,0:T(8,128)(2,1)S(1)} %get-tuple-element.48.block_ref), channel_id=1, source_target_pairs={{0,24},{8,16},{16,8},{24,0},{1,25},{9,17},{17,9},{25,1},{2,26},{10... | collective-permute-start | bytes 786440 | tf_op jit(solution)/shard_map/ppermute | solution.py:387
  96.8 9.7 %collective-permute-start.14 = (bf16[128,1024]{1,0:T(8,128)(2,1)S(1)}, bf16[128,1024]{1,0:T(8,128)(2,1)S(1)}, u32[]{:S(2)}, u32[]{:S(2)}) collective-permute-start(bf16[128,1024]{1,0:T(8,128)(2,1)S(1)} %ffn.5), channel_id=1, source_target_pairs={{0,8},{8,0},{16,24},{24,16},{1,9},{9,1},{17,25},{25,17},{2,10},{10... | collective-permute-start | bytes 786440 | tf_op jit(solution)/shard_map/ppermute | solution.py:387
  99.9 11.6 %collective-permute-start.16 = (bf16[128,1024]{1,0:T(8,128)(2,1)S(1)}, bf16[128,1024]{1,0:T(8,128)(2,1)S(1)}, u32[]{:S(2)}, u32[]{:S(2)}) collective-permute-start(bf16[128,1024]{1,0:T(8,128)(2,1)S(1)} %ffn.6), channel_id=1, source_target_pairs={{0,16},{8,24},{16,0},{24,8},{1,17},{9,25},{17,1},{25,9},{2,18},{10... | collective-permute-start | bytes 786440 | tf_op jit(solution)/shard_map/ppermute | solution.py:387
  102.5 9.0 %collective-permute-start.18 = (bf16[128,1024]{1,0:T(8,128)(2,1)S(1)}, bf16[128,1024]{1,0:T(8,128)(2,1)S(1)}, u32[]{:S(2)}, u32[]{:S(2)}) collective-permute-start(bf16[128,1024]{1,0:T(8,128)(2,1)S(1)} %ffn.7), channel_id=1, source_target_pairs={{0,24},{8,16},{16,8},{24,0},{1,25},{9,17},{17,9},{25,1},{2,26},{10... | collective-permute-start | bytes 786440 | tf_op jit(solution)/shard_map/ppermute | solution.py:387
  112.9 6.4 %collective-permute-start.19 = (bf16[128,1024]{1,0:T(8,128)(2,1)S(1)}, bf16[128,1024]{1,0:T(8,128)(2,1)S(1)}, u32[]{:S(2)}, u32[]{:S(2)}) collective-permute-start(bf16[128,1024]{1,0:T(8,128)(2,1)S(1)} %get-tuple-element.52.refs_0_), channel_id=1, source_target_pairs={{0,8},{8,0},{16,24},{24,16},{1,9},{9,1},{17,25},{25,17},{2,10},{10... | collective-permute-start | bytes 786440 | tf_op jit(solution)/shard_map/ppermute | solution.py:387
  113.0 8.9 %collective-permute-start.20 = (bf16[128,1024]{1,0:T(8,128)(2,1)S(1)}, bf16[128,1024]{1,0:T(8,128)(2,1)S(1)}, u32[]{:S(2)}, u32[]{:S(2)}) collective-permute-start(bf16[128,1024]{1,0:T(8,128)(2,1)S(1)} %get-tuple-element.52.refs_0_), channel_id=1, source_target_pairs={{0,16},{8,24},{16,0},{24,8},{1,17},{9,25},{17,1},{25,9},{2,18},{10... | collective-permute-start | bytes 786440 | tf_op jit(solution)/shard_map/ppermute | solution.py:387
  114.5 8.2 %collective-permute-start.21 = (bf16[128,1024]{1,0:T(8,128)(2,1)S(1)}, bf16[128,1024]{1,0:T(8,128)(2,1)S(1)}, u32[]{:S(2)}, u32[]{:S(2)}) collective-permute-start(bf16[128,1024]{1,0:T(8,128)(2,1)S(1)} %get-tuple-element.52.refs_0_), channel_id=1, source_target_pairs={{0,24},{8,16},{16,8},{24,0},{1,25},{9,17},{17,9},{25,1},{2,26},{10... | collective-permute-start | bytes 786440 | tf_op jit(solution)/shard_map/ppermute | solution.py:387
  (18 other events, 151.0 us)
Sparse Core Ops, SparseCore 0:
  27.8 51.6 all-gather.4
  81.1 23.7 all-gather.6

commit v3 on v2

v3 whole, which is shorter than its diff:
```python
import functools
import jax
import jax.numpy as jnp
from jax import lax
from jax.experimental import pallas as pl
from jax.experimental.pallas import tpu as pltpu
from jax.sharding import PartitionSpec as P

DH = 64
HALVES = 2
F32 = jnp.float32
BF16 = jnp.bfloat16
NEG = -1e30
MIB = 1024 * 1024
CROSS_LIMIT = 28
HBM = pl.BlockSpec(memory_space=pl.ANY)
SMEM = pl.BlockSpec(memory_space=pltpu.SMEM)
VMEM = pl.BlockSpec(memory_space=pltpu.VMEM)


def params(limit=28):
    return pltpu.CompilerParams(vmem_limit_bytes=limit * MIB)


def cost(flops, moved, transcendentals=0):
    return pl.CostEstimate(
        flops=int(flops), bytes_accessed=int(moved), transcendentals=int(transcendentals)
    )


def dot_nt(lhs, rhs):
    return lax.dot_general(lhs, rhs, (((1,), (1,)), ((), ())), preferred_element_type=F32)


def dot(lhs, rhs):
    return jnp.dot(lhs, rhs, preferred_element_type=F32)


def ancestor_masks(parents_ref, counts_ref):
    requests, slots = parents_ref.shape
    row = lax.broadcasted_iota(jnp.int32, (slots, slots), 0)
    col = lax.broadcasted_iota(jnp.int32, (slots, slots), 1)
    reach = []
    for r in range(requests):
        linked = (row == parents_ref[r : r + 1, :]) | (row == col)
        reach.append(jnp.where(linked, 1.0, 0.0).astype(BF16))
    span = 1
    while span < slots - 1:
        reach = [jnp.minimum(dot(a, a), 1.0).astype(BF16) for a in reach]
        span *= 2
    eye = jnp.where(row == col, 1.0, 0.0).astype(BF16)
    return [(dot_nt(eye, reach[r]) > 0.5) & (col < counts_ref[r]) for r in range(requests)]


def draft_biases(parents_ref, counts_ref, buckets_ref, table_ref):
    requests, slots = parents_ref.shape
    heads, kinds = table_ref.shape
    lanes = 2 * slots
    live = ancestor_masks(parents_ref, counts_ref)
    shifted = table_ref[...] - table_ref[:, kinds - 1 :]
    table = jnp.concatenate([shifted, jnp.zeros((heads, lanes - kinds), F32)], axis=1)
    biases = [[] for _ in range(requests)]
    for r in range(0, requests, 2):
        picked = jnp.concatenate([buckets_ref[r], buckets_ref[r + 1]], axis=1)
        for h in range(heads):
            row_of = jnp.broadcast_to(table[h : h + 1, :], (slots, lanes))
            both = jnp.take_along_axis(row_of, picked, axis=1)
            biases[r].append(jnp.where(live[r], both[:, :slots], NEG))
            biases[r + 1].append(jnp.where(live[r + 1], both[:, slots:], NEG))
    return [jnp.concatenate(parts, axis=0) for parts in biases]


def spread_heads(queries, heads):
    head_of = lax.broadcasted_iota(jnp.int32, queries.shape, 1) // DH
    return jnp.concatenate(
        [jnp.where(head_of == h, queries, jnp.zeros_like(queries)) for h in range(heads)], axis=0
    )


def gather_heads(attended, heads):
    slots = attended.shape[0] // heads
    head_of = lax.broadcasted_iota(jnp.int32, (slots, attended.shape[1]), 1) // DH
    total = attended[:slots]
    for h in range(1, heads):
        total = jnp.where(head_of == h, attended[h * slots : (h + 1) * slots], total)
    return total.astype(BF16)


def bias_kernel(parents_ref, counts_ref, buckets_ref, table_ref, out_ref):
    for r, bias in enumerate(draft_biases(parents_ref, counts_ref, buckets_ref, table_ref)):
        out_ref[r] = bias


def bias_and_mask(parents, counts, buckets, bias_table):
    requests, slots = parents.shape
    heads = bias_table.shape[1]
    return pl.pallas_call(
        bias_kernel,
        out_shape=jax.ShapeDtypeStruct((requests, heads * slots, slots), F32),
        in_specs=[VMEM, SMEM, VMEM, VMEM],
        out_specs=VMEM,
        compiler_params=params(60),
        cost_estimate=cost(6e7, 1.2e6),
        name="bias_and_mask",
    )(parents, counts, buckets, bias_table.T)


def self_kernel(length_ref, qkv_ref, cache_ref, bias_ref, out_ref):
    step, width = out_ref.shape[0], out_ref.shape[2]
    heads = width // DH
    position = lax.broadcasted_iota(jnp.int32, (1, cache_ref.shape[2]), 1)
    for s in range(step):
        length = length_ref[pl.program_id(0) * step + s]
        queries = spread_heads(qkv_ref[0, s], heads)
        scores = dot_nt(queries, cache_ref[s, 0])
        scores = jnp.where(position < length, scores, NEG)
        draft = dot_nt(queries, qkv_ref[1, s]) + bias_ref[s]
        highest = jnp.maximum(scores.max(-1, keepdims=True), draft.max(-1, keepdims=True))
        scores = jnp.exp(scores - highest)
        draft = jnp.exp(draft - highest)
        total = scores.sum(-1, keepdims=True) + draft.sum(-1, keepdims=True)
        attended = dot(scores.astype(BF16), cache_ref[s, 1])
        attended = attended + dot(draft.astype(BF16), qkv_ref[2, s])
        out_ref[s] = gather_heads(attended / total, heads)


def self_attention(draft_qkv, cache, length, bias):
    _, requests, slots, width = draft_qkv.shape
    step = requests // HALVES
    depth = cache.shape[2]
    return pl.pallas_call(
        self_kernel,
        grid=(HALVES,),
        out_shape=jax.ShapeDtypeStruct((requests, slots, width), BF16),
        in_specs=[
            SMEM,
            pl.BlockSpec((3, step, slots, width), lambda h: (0, h, 0, 0)),
            pl.BlockSpec((step, 2, depth, width), lambda h: (h, 0, 0, 0)),
            pl.BlockSpec((step, bias.shape[1], slots), lambda h: (h, 0, 0)),
        ],
        out_specs=pl.BlockSpec((step, slots, width), lambda h: (h, 0, 0)),
        compiler_params=params(60),
        cost_estimate=cost(5e9, 6e6, 1.2e6),
        name="self_attention",
    )(length, draft_qkv, cache, bias)


def columns(ref, pieces, j):
    lanes = ref.shape[-1] // pieces
    return pl.ds(pl.multiple_of(jnp.bitwise_xor(lax.axis_index("tok"), j) * lanes, lanes), lanes)


def each_slice(stacks, orders):
    for stack, order in zip(stacks, orders):
        for at, k in enumerate(order):
            yield k, stack.at[at]


def join_columns(out_ref, slices, first, rows):
    for k, piece in slices:
        lanes = piece.shape[1]
        out_ref[:, k * lanes : (k + 1) * lanes] = piece[first : first + rows, :]


def self_out_kernel(ways, orders, first, *refs):
    stacks = refs[: len(orders)]
    ctx_ref, hidden_ref, own_ref = refs[len(orders) : len(orders) + 3]
    out_refs = refs[-ways:-1]
    w_ref = refs[-1]
    pieces = sum(len(order) for order in orders)
    width = ctx_ref.shape[2]
    share, model = hidden_ref.shape[1:]
    rows = own_ref.shape[0]
    requests = rows // share
    join_columns(w_ref, each_slice(stacks, orders), 0, width)
    taken = []
    for k in range(ways):
        owner = jnp.bitwise_xor(lax.axis_index("grp"), k)
        start = pl.multiple_of(owner * share, share)
        taken.append(
            ctx_ref[first : first + requests, pl.ds(start, share), :].reshape(rows, width)
        )
    part = dot(jnp.concatenate(taken, axis=0), w_ref[...])
    for k in range(1, ways):
        out_refs[k - 1][...] = part[k * rows : (k + 1) * rows].astype(BF16)
    lanes = model // pieces
    for j in range(pieces):
        base = hidden_ref[first : first + requests, :, columns(hidden_ref, pieces, j)]
        here = slice(j * lanes, (j + 1) * lanes)
        own_ref[:, here] = part[:rows, here] + base.astype(F32).reshape(rows, lanes)


def self_out(ctx, stacks, orders, hidden, ways, first, count):
    width = ctx.shape[2]
    share, model = hidden.shape[1:]
    rows = count * share
    return pl.pallas_call(
        functools.partial(self_out_kernel, ways, orders, first),
        out_shape=[jax.ShapeDtypeStruct((rows, model), F32)]
        + [jax.ShapeDtypeStruct((rows, model), BF16)] * (ways - 1),
        in_specs=[VMEM] * (len(stacks) + 2),
        out_specs=[VMEM] * ways,
        scratch_shapes=[pltpu.VMEM((width, model), BF16)],
        compiler_params=params(),
        cost_estimate=cost(2 * rows * ways * width * model, 2e6),
        name="self_out",
    )(*stacks, ctx, hidden)


def norm_kernel(pieces, last, own_ref, *refs):
    others = refs[:-3]
    gain_ref, stream_ref, normed_ref = refs[-3:]
    stream = own_ref[...]
    for other in others:
        stream = stream + other[...].astype(F32)
    lanes = stream.shape[1] // pieces
    scale = lax.rsqrt(jnp.mean(stream * stream, axis=-1, keepdims=True) + 1e-06)
    for j in range(pieces):
        here = slice(j * lanes, (j + 1) * lanes)
        there = columns(gain_ref, pieces, j)
        stream_ref[:, there if last else here] = stream[:, here].astype(stream_ref.dtype)
        normed_ref[:, here] = (stream[:, here] * scale * gain_ref[:, there]).astype(BF16)


def norm(own, others, gain, pieces, last=False):
    return pl.pallas_call(
        functools.partial(norm_kernel, pieces, last),
        out_shape=[
            jax.ShapeDtypeStruct(own.shape, BF16 if last else F32),
            jax.ShapeDtypeStruct(own.shape, BF16),
        ],
        in_specs=[VMEM] * (len(others) + 2),
        out_specs=[VMEM] * 2,
        compiler_params=params(),
        cost_estimate=cost(1e6, 2e6),
        name="norm",
    )(own, *others, gain.reshape(1, -1))


def cross_kernel(ways, first, length_ref, cache_ref, stream_ref, *refs):
    blocks = refs[:ways]
    given = refs[ways : -(ways + 3)]
    own_ref = refs[-(ways + 3)]
    out_refs = refs[-(ways + 2) : -3]
    wq_ref, wo_ref, ctx_ref = refs[-3:]
    requests = cache_ref.shape[0]
    width = wq_ref.shape[1]
    heads = width // DH
    rows = blocks[0].shape[0]
    share = rows // requests
    if len(given) == 1:
        (slices_ref,) = given
        pieces, _, lanes = slices_ref.shape
        parts = width // lanes
        for k in range(pieces):
            piece = slices_ref.at[jnp.bitwise_xor(lax.axis_index("tok"), k)]
            for c in range(parts):
                here = slice(c * lanes, (c + 1) * lanes)
                block = piece[c * lanes : (c + 1) * lanes, :]
                wq_ref[k * lanes : (k + 1) * lanes, here] = block
            wo_ref[:, k * lanes : (k + 1) * lanes] = piece[parts * lanes :, :]
    else:
        wq_ref[...] = given[0][...]
        wo_ref[...] = given[1][...]
    normed = jnp.concatenate([block[...] for block in blocks], axis=0)
    query = dot(normed, wq_ref[...]).astype(BF16).reshape(ways, rows, width)
    position = lax.broadcasted_iota(jnp.int32, (1, cache_ref.shape[2]), 1)
    for r in range(requests):
        here = slice(r * share, (r + 1) * share)
        queries = spread_heads(query[:, here].reshape(ways * share, width), heads)
        scores = dot_nt(queries, cache_ref[r, 0])
        scores = jnp.where(position < length_ref[first + r], scores, NEG)
        scores = jnp.exp(scores - scores.max(-1, keepdims=True))
        total = scores.sum(-1, keepdims=True)
        attended = dot(scores.astype(BF16), cache_ref[r, 1])
        ctx = gather_heads(attended / total, heads)
        ctx_ref[:, here, :] = ctx.reshape(ways, share, width)
    part = dot(ctx_ref[...].reshape(ways * rows, width), wo_ref[...])
    own_ref[...] = part[:rows] + stream_ref[...]
    for k in range(1, ways):
        out_refs[k - 1][...] = part[k * rows : (k + 1) * rows].astype(BF16)


def cross_layer(blocks, weights, cache, stream, length, first, count):
    ways = len(blocks)
    rows, model = blocks[0].shape
    depth, width = cache.shape[2:]
    full = lambda shape: pl.BlockSpec(shape, lambda i: (0,) * len(shape))
    return pl.pallas_call(
        functools.partial(cross_kernel, ways, first),
        grid=(1,),
        out_shape=[jax.ShapeDtypeStruct((rows, model), F32)]
        + [jax.ShapeDtypeStruct((rows, model), BF16)] * (ways - 1),
        in_specs=[
            SMEM,
            pl.BlockSpec((count, 2, depth, width), lambda i: (first // count, 0, 0, 0)),
            full((rows, model)),
        ]
        + [full((rows, model))] * ways
        + [full(weight.shape) for weight in weights],
        out_specs=[full((rows, model))] * ways,
        scratch_shapes=[
            pltpu.VMEM((model, width), BF16),
            pltpu.VMEM((width, model), BF16),
            pltpu.VMEM((ways, rows, width), BF16),
        ],
        compiler_params=params(CROSS_LIMIT),
        cost_estimate=cost(5e9 * count / 8, 8e6 * count / 8, 1.2e6 * count / 8),
        name="cross_layer",
    )(length, cache, stream, *blocks, *weights)


def join_kernel(slices_ref, out_ref):
    pieces, _, lanes = slices_ref.shape
    for k in range(pieces):
        source = jnp.bitwise_xor(lax.axis_index("tok"), k)
        out_ref[:, k * lanes : (k + 1) * lanes] = slices_ref[source]


def join(slices):
    pieces, rows, lanes = slices.shape
    return pl.pallas_call(
        join_kernel,
        out_shape=jax.ShapeDtypeStruct((rows, lanes * pieces), BF16),
        in_specs=[VMEM],
        out_specs=VMEM,
        compiler_params=params(),
        cost_estimate=cost(1e3, 4 * rows * lanes * pieces),
        name="join",
    )(slices)


def ffn_kernel(ways, w_ref, stream_ref, *refs):
    blocks, own_ref, out_refs = refs[:ways], refs[ways], refs[ways + 1 :]
    hidden = w_ref.shape[0] // 3
    rows = stream_ref.shape[0]
    normed = jnp.concatenate([block[...] for block in blocks], axis=0)
    gate = dot_nt(normed, w_ref[:hidden, :])
    up = dot_nt(normed, w_ref[hidden : 2 * hidden, :])
    gated = (jax.nn.gelu(gate, approximate=True) * up).astype(BF16)
    part = dot(gated, w_ref[2 * hidden :, :])
    own_ref[...] = part[:rows] + stream_ref[...]
    for k in range(1, ways):
        out_refs[k - 1][...] = part[k * rows : (k + 1) * rows].astype(BF16)


def ffn(blocks, w, stream):
    ways = len(blocks)
    rows, model = stream.shape
    return pl.pallas_call(
        functools.partial(ffn_kernel, ways),
        out_shape=[jax.ShapeDtypeStruct((rows, model), F32)]
        + [jax.ShapeDtypeStruct((rows, model), BF16)] * (ways - 1),
        in_specs=[VMEM] * (2 + ways),
        out_specs=[VMEM] * ways,
        compiler_params=params(),
        cost_estimate=cost(2 * rows * ways * w.size, 6e6, 4e5),
        name="ffn",
    )(w, stream, *blocks)


def project_kernel(ways, first, slices_ref, *refs):
    blocks, out_hbm, w_ref, made_ref, sem = refs[:ways], *refs[-4:]
    _, count, slots, width = made_ref.shape
    share = slots // ways
    pieces, _, depth, _ = slices_ref.shape
    for k in range(pieces):
        source = jnp.bitwise_xor(lax.axis_index("tok"), k) if pieces > 1 else 0
        w_ref[:, k * depth : (k + 1) * depth, :] = slices_ref[source]
    normed = jnp.concatenate([block[...] for block in blocks], axis=0)
    for c in range(3):
        projected = dot(normed, w_ref[c]).astype(BF16).reshape(ways, count, share, width)
        for k in range(ways):
            start = pl.multiple_of(jnp.bitwise_xor(lax.axis_index("grp"), k) * share, share)
            made_ref[c, :, pl.ds(start, share), :] = projected[k]
    copy = pltpu.make_async_copy(made_ref, out_hbm.at[:, first : first + count], sem)
    copy.start()
    copy.wait()


def project(blocks, slices, requests, share, first, count, base):
    ways = len(blocks)
    model = blocks[0].shape[1]
    width = slices.shape[3]
    given = [] if base is None else [base]
    return pl.pallas_call(
        functools.partial(project_kernel, ways, first),
        out_shape=jax.ShapeDtypeStruct((3, requests, share * ways, width), BF16),
        in_specs=[VMEM] * (ways + 1) + [HBM] * len(given),
        out_specs=HBM,
        scratch_shapes=[
            pltpu.VMEM((3, model, width), BF16),
            pltpu.VMEM((3, count, share * ways, width), BF16),
            pltpu.SemaphoreType.DMA,
        ],
        input_output_aliases={ways + 1: 0} if given else {},
        compiler_params=params(),
        cost_estimate=cost(6 * count * share * ways * model * width, 4e6),
        name="project",
    )(slices, *blocks, *given)


ATTN_ORDERS = ((0, 4, 6, 2), (1, 5, 7, 3))


def gate(*values):
    return lax.optimization_barrier(values)


def partner(value, axis, size, k):
    return lax.ppermute(value, axis, [(i, i ^ k) for i in range(size)])


def all_slices(shard):
    return lax.all_gather(shard, "tok", axis=0, tiled=False)


def along(value, k):
    return partner(value, "tok", 8, k)


def send_each(parts, ways):
    return [partner(part, "grp", ways, k) for k, part in zip(range(1, ways), parts)]


def spread(block, ways):
    return [block] + send_each([block] * (ways - 1), ways)


def shards(
    ways,
    total,
    hidden,
    draft_qkv,
    self_cache,
    cross_cache,
    parents,
    counts,
    self_len,
    enc_len,
    buckets,
    bias_table,
    gain_cross,
    gain_ffn,
    gain_next,
    w_out_self,
    w_query_cross,
    w_out_cross,
    w_gate,
    w_up,
    w_down,
    w_qkv,
):
    requests, share, model = hidden.shape
    slice_lanes = model // total
    head_width = w_query_cross.shape[1]
    paired = total == 8 and slice_lanes == 128 and head_width % slice_lanes == 0
    qkv_shard = jnp.transpose(w_qkv, (1, 0, 2))
    halves = range(HALVES)
    count = requests // HALVES
    starts = [h * count for h in halves]
    bias = bias_and_mask(parents, counts, buckets, bias_table)
    ctx = self_attention(draft_qkv, self_cache, self_len, bias)
    if paired:
        pieces, orders = total, ATTN_ORDERS
        query_slices = jnp.split(w_query_cross, head_width // slice_lanes, axis=1)
        attn_w = [all_slices(jnp.concatenate(query_slices + [w_out_cross], axis=0))]
        out_here = [w_out_self] + [along(w_out_self, k) for k in (4, 6, 2)]
        ctx, out_here = gate(ctx, out_here)
        out_here = jnp.stack(out_here)
        out_w = [out_here, along(out_here, 1)]
        out_here, w_gate, w_up, w_down, qkv_shard = gate(
            out_here, w_gate, w_up, w_down, qkv_shard
        )
        ffn_w = all_slices(jnp.concatenate([w_gate.T, w_up.T, w_down], axis=0))
    else:
        pieces = 1
        by_row = functools.partial(lax.all_gather, axis_name="tok", axis=0, tiled=True)
        by_col = functools.partial(lax.all_gather, axis_name="tok", axis=1, tiled=True)
        out_w, orders = [by_col(w_out_self)[None]], ((0,),)
        attn_w = [by_row(w_query_cross), by_col(w_out_cross)]
        ffn_w = jnp.concatenate([by_row(w_gate).T, by_row(w_up).T, by_col(w_down)], axis=0)
        qkv_w = by_col(qkv_shard)[None]
    made = [self_out(ctx, out_w, orders, hidden, ways, start, count) for start in starts]
    if paired:
        *made[-1], qkv_shard = gate(*made[-1], qkv_shard)
        qkv_w = all_slices(qkv_shard)
    sent = [send_each(made[h][1:], ways) for h in halves]
    kept = [norm(made[h][0], sent[h], gain_cross, pieces) for h in halves]
    blocks = [spread(kept[h][1], ways) for h in halves]
    made = [
        cross_layer(blocks[h], attn_w, cross_cache, kept[h][0], enc_len, starts[h], count)
        for h in halves
    ]
    sent = [send_each(made[h][1:], ways) for h in halves]
    kept = [norm(made[h][0], sent[h], gain_ffn, pieces) for h in halves]
    blocks = [spread(kept[h][1], ways) for h in halves]
    if paired:
        ffn_w = join(ffn_w)
    made = [ffn(blocks[h], ffn_w, kept[h][0]) for h in halves]
    sent = [send_each(made[h][1:], ways) for h in halves]
    kept = [norm(made[h][0], sent[h], gain_next, pieces, True) for h in halves]
    blocks = [spread(kept[h][1], ways) for h in halves]
    next_qkv = None
    for h in halves:
        next_qkv = project(blocks[h], qkv_w, requests, share, starts[h], count, next_qkv)
    out_hidden = jnp.concatenate([kept[h][0] for h in halves], axis=0)
    return out_hidden.reshape(requests, share, model), next_qkv


def solution(mesh):
    in_specs = (
        P("tok", "grp", None),
        P(None, "tok", None, "grp"),
        P("tok", None, None, "grp"),
        P("tok", None, None, "grp"),
        P("tok", None),
        P("tok"),
        P("tok"),
        P("tok"),
        P("tok", None, None),
        P(None, "grp"),
        P(),
        P(),
        P(),
        P("grp", "tok"),
        P("tok", "grp"),
        P("grp", "tok"),
        P("tok", "grp"),
        P("tok", "grp"),
        P("grp", "tok"),
        P("tok", None, "grp"),
    )
    out_specs = (P("tok", "grp", None), P(None, "tok", None, "grp"))
    body = functools.partial(shards, mesh.shape["grp"], mesh.shape["tok"])
    return jax.shard_map(body, mesh=mesh, in_specs=in_specs, out_specs=out_specs, check_vma=False)
```

time: 135 us -> 125 us (0.926)
  waiting for transfers between devices: 49.6 us -> 23.7 us
  starting transfers between devices: 28.2 us -> 52.7 us
  Pallas kernels: 32.3 us -> 22.7 us
    ppermute x22 -> x40, waiting for transfers between devices: 49.6 us -> 15.7 us  [partner(): return lax.ppermute(value, axis, [(i, i ^ k) for i in range(size)])]
    ppermute x22 -> x40, starting transfers between devices: 27.9 us -> 52.4 us  [partner(): return lax.ppermute(value, axis, [(i, i ^ k) for i in range(size)])]
    all_gather x2 -> x3, waiting for transfers between devices: 0.01 us -> 7.99 us  [all_slices(): return lax.all_gather(shard, 'tok', axis=0, tiled=False)]
    pallas_call x8 -> x10, Pallas kernels: 27.5 us -> 20.5 us  [the longest x1 5.92 us: self_attention(): pl.pallas_call(self_kernel, grid=(HALVES,), out_shape=jax.ShapeDtypeStruc...]
    pallas_call x3 -> x6, Pallas kernels: 3.02 us -> 0.97 us  [norm(): pl.pallas_call(functools.partial(norm_kernel, pieces, last), out_shape=[j...]
    concatenate x2 -> x3, other arithmetic: 1.72 us -> 3.07 us  [the longest x1 1.51 us: shards(): attn_w = [all_slices(jnp.concatenate(query_slices + [w_out_cross], axis=0))]]
    unnamed x36 -> x32, local copies, waits for them, and re-layouts: 6.37 us -> 7.13 us
  transfers between devices with their start and end apart: 24 -> 43, of which waited for: 15 -> 17; matrix products, arithmetic and copies ran while one was open for 1% -> 1% of each run, Pallas kernels for 22% -> 17%
where the time goes in v3:
time: 125 us; the launch traced here: 124 us
  starting transfers between devices  52.7 us (42%)
  waiting for transfers between devices  23.7 us (19%)
  Pallas kernels  22.7 us (18%)
  between operations  14 us (11%)
  local copies, waits for them, and re-layouts  7.91 us (6%)
  other arithmetic  3.1 us (2%)
    ppermute x40, starting transfers between devices, partner(): return lax.ppermute(value, axis, [(i, i ^ k) for i in range(size)])  52.4 us
    ppermute x40, waiting for transfers between devices, partner(): return lax.ppermute(value, axis, [(i, i ^ k) for i in range(size)])  15.7 us
    all_gather x3, waiting for transfers between devices, all_slices(): return lax.all_gather(shard, 'tok', axis=0, tiled=False)  7.99 us
    unnamed x32, local copies, waits for them, and re-layouts  7.13 us
    pallas_call x1, Pallas kernels, self_attention(): pl.pallas_call(self_kernel, grid=(HALVES,), out_shape=jax.ShapeDtypeStruc...  5.92 us
    pallas_call x2, Pallas kernels, cross_layer(): pl.pallas_call(functools.partial(cross_kernel, ways, first), grid=(1,), o...  5.07 us
    pallas_call x1, Pallas kernels, bias_and_mask(): pl.pallas_call(bias_kernel, out_shape=jax.ShapeDtypeStruct((requests, hea...  3.28 us
    pallas_call x2, Pallas kernels, ffn(): pl.pallas_call(functools.partial(ffn_kernel, ways), out_shape=[jax.ShapeD...  2.85 us
  transfers between devices with their start and end apart: 43, of which 17 were waited for; matrix products, arithmetic and copies ran while one was open for 1% of the time, Pallas kernels for 17%

profile of v3, /device:TPU:0, one launch (start us, length us, event | category | flops | bytes accessed | tf_op | source)
XLA Modules:
  0.0 124.2 jit_solution(10674809591589084943)
XLA Ops:
  8.0 1.5 %pad_maximum_fusion.3 = bf16[512,128]{1,0:T(8,128)(2,1)} fusion(bf16[256,128]{1,0:T(8,128)(2,1)} %param.35, bf16[128,128]{1,0:T(8,128)(2,1)S(1)} %get-tuple-element.103, bf16[128,128]{1,0:T(8,128)(2,1)S(1)} %get-tuple-element.102), kind=kLoop, calls=%fused_computation.3 | loop fusion | flops 393216 | bytes 262144 | tf_op jit(solution)/shard_map/concatenate | solution.py:467
  9.6 4.1 %collective-permute-start = (bf16[256,128]{1,0:T(8,128)(2,1)}, bf16[256,128]{1,0:T(8,128)(2,1)S(1)}, u32[]{:S(2)}, u32[]{:S(2)}) collective-permute-start(bf16[256,128]{1,0:T(8,128)(2,1)} %param.33), channel_id=1, source_target_pairs={{0,4},{1,5},{2,6},{3,7},{4,0},{5,1},{6,2},{7,3},{8,12},{9,13},{10,... | collective-permute-start | bytes 196616 | tf_op jit(solution)/shard_map/ppermute | solution.py:411
  15.3 3.3 %bias_and_mask.1.bias_ref = f32[8,256,64]{2,1,0:T(8,128)} custom-call(s32[8,64]{1,0:T(8,128)} %parents_ref.1, s32[8]{0:T(128)} %counts_ref.1, s32[8,64,64]{2,1,0:T(8,128)} %buckets_ref.1, f32[4,32]{1,0:T(4,128)} %bitcast.34), custom_call_target="tpu_custom_call" | custom-call | flops 60000000 | bytes 1200000 | tf_op jit(solution)/shard_map/bias_and_mask/pallas_call | solution.py:97
  18.6 5.9 %self_attention.1.refs_2_ = bf16[8,64,256]{2,1,0:T(8,128)(2,1)} custom-call(s32[8]{0:T(128)} %length_ref.3, bf16[3,8,64,256]{3,2,1,0:T(8,128)(2,1)} %qkv_ref.1, bf16[8,2,512,256]{3,2,1,0:T(8,128)(2,1)} %cache_ref.3, f32[8,256,64]{2,1,0:T(8,128)} %bias_and_mask.1.bias_ref), custom_call_target="tpu_custom_call" | custom-call | flops 5000000000 | bytes 6000000 | tf_op jit(solution)/shard_map/self_attention/pallas_call | solution.py:131
  25.8 1.5 %collective-permute-done.3.refs_1_ = bf16[4,256,128]{2,1,0:T(8,128)(2,1)S(1)} collective-permute-done((bf16[4,256,128]{2,1,0:T(8,128)(2,1)S(1)}, bf16[4,256,128]{2,1,0:T(8,128)(2,1)S(1)}, u32[]{:S(2)}, u32[]{:S(2)}) %collective-permute-start.3) | collective-permute-done | bytes 262176 | tf_op jit(solution)/shard_map/ppermute | solution.py:411
  28.1 1.6 %collective-permute-start.4 = (bf16[64,1024]{1,0:T(8,128)(2,1)S(1)}, bf16[64,1024]{1,0:T(8,128)(2,1)S(1)}, u32[]{:S(2)}, u32[]{:S(2)}) collective-permute-start(bf16[64,1024]{1,0:T(8,128)(2,1)S(1)} %get-tuple-element.61), channel_id=1, source_target_pairs={{0,8},{8,0},{16,24},{24,16},{1,9},{9,1},{17,25},{25,17},{2,10},{10... | collective-permute-start | bytes 393224 | tf_op jit(solution)/shard_map/ppermute | solution.py:411
  29.6 1.5 %collective-permute-start.5 = (bf16[64,1024]{1,0:T(8,128)(2,1)S(1)}, bf16[64,1024]{1,0:T(8,128)(2,1)S(1)}, u32[]{:S(2)}, u32[]{:S(2)}) collective-permute-start(bf16[64,1024]{1,0:T(8,128)(2,1)S(1)} %get-tuple-element.62), channel_id=1, source_target_pairs={{0,16},{8,24},{16,0},{24,8},{1,17},{9,25},{17,1},{25,9},{2,18},{10... | collective-permute-start | bytes 393224 | tf_op jit(solution)/shard_map/ppermute | solution.py:411
  31.6 1.5 %collective-permute-start.19 = (bf16[64,1024]{1,0:T(8,128)(2,1)S(1)}, bf16[64,1024]{1,0:T(8,128)(2,1)S(1)}, u32[]{:S(2)}, u32[]{:S(2)}) collective-permute-start(bf16[64,1024]{1,0:T(8,128)(2,1)S(1)} %get-tuple-element.83), channel_id=1, source_target_pairs={{0,8},{8,0},{16,24},{24,16},{1,9},{9,1},{17,25},{25,17},{2,10},{10... | collective-permute-start | bytes 393224 | tf_op jit(solution)/shard_map/ppermute | solution.py:411
  33.1 1.5 %collective-permute-start.20 = (bf16[64,1024]{1,0:T(8,128)(2,1)S(1)}, bf16[64,1024]{1,0:T(8,128)(2,1)S(1)}, u32[]{:S(2)}, u32[]{:S(2)}) collective-permute-start(bf16[64,1024]{1,0:T(8,128)(2,1)S(1)} %get-tuple-element.84), channel_id=1, source_target_pairs={{0,16},{8,24},{16,0},{24,8},{1,17},{9,25},{17,1},{25,9},{2,18},{10... | collective-permute-start | bytes 393224 | tf_op jit(solution)/shard_map/ppermute | solution.py:411
  34.6 2.3 %collective-permute-start.21 = (bf16[64,1024]{1,0:T(8,128)(2,1)S(1)}, bf16[64,1024]{1,0:T(8,128)(2,1)S(1)}, u32[]{:S(2)}, u32[]{:S(2)}) collective-permute-start(bf16[64,1024]{1,0:T(8,128)(2,1)S(1)} %get-tuple-element.85), channel_id=1, source_target_pairs={{0,24},{8,16},{16,8},{24,0},{1,25},{9,17},{17,9},{25,1},{2,26},{10... | collective-permute-start | bytes 393224 | tf_op jit(solution)/shard_map/ppermute | solution.py:411
  49.9 2.2 %copy-done.7 = bf16[8,2,512,256]{3,2,1,0:T(8,128)(2,1)S(1)} copy-done((bf16[8,2,512,256]{3,2,1,0:T(8,128)(2,1)S(1)}, bf16[8,2,512,256]{3,2,1,0:T(8,128)(2,1)}, u32[]{:S(2)}) %copy-start.7) | copy-done | bytes 4194328
  53.3 2.5 %cross_layer.2 = (f32[64,1024]{1,0:T(8,128)S(1)}, bf16[64,1024]{1,0:T(8,128)(2,1)S(1)}, bf16[64,1024]{1,0:T(8,128)(2,1)S(1)}, bf16[64,1024]{1,0:T(8,128)(2,1)S(1)}) custom-call(s32[8]{0:T(128)S(1)} %copy-done.11, bf16[8,2,512,256]{3,2,1,0:T(8,128)(2,1)S(1)} %copy-done.7, f32[64,1024]{1,0:T(8,128)S(1)} %get-tuple-element.64.stream_ref, ...), custom_call_target="tpu_custom_call" | custom-call | flops 2500000000 | bytes 4000000 | tf_op jit(solution)/shard_map/cross_layer/pallas_call | solution.py:289
  59.7 2.5 %cross_layer.3 = (f32[64,1024]{1,0:T(8,128)S(1)}, bf16[64,1024]{1,0:T(8,128)(2,1)S(1)}, bf16[64,1024]{1,0:T(8,128)(2,1)S(1)}, bf16[64,1024]{1,0:T(8,128)(2,1)S(1)}) custom-call(s32[8]{0:T(128)S(1)} %copy-done.11, bf16[8,2,512,256]{3,2,1,0:T(8,128)(2,1)S(1)} %copy-done.8, f32[64,1024]{1,0:T(8,128)S(1)} %get-tuple-element.86.stream_ref, ...), custom_call_target="tpu_custom_call" | custom-call | flops 2500000000 | bytes 4000000 | tf_op jit(solution)/shard_map/cross_layer/pallas_call | solution.py:289
  69.0 1.5 %collective-permute-start.15 = (bf16[64,1024]{1,0:T(8,128)(2,1)S(1)}, bf16[64,1024]{1,0:T(8,128)(2,1)S(1)}, u32[]{:S(2)}, u32[]{:S(2)}) collective-permute-start(bf16[64,1024]{1,0:T(8,128)(2,1)S(1)} %get-tuple-element.71.refs_0_), channel_id=1, source_target_pairs={{0,24},{8,16},{16,8},{24,0},{1,25},{9,17},{17,9},{25,1},{2,26},{10... | collective-permute-start | bytes 393224 | tf_op jit(solution)/shard_map/ppermute | solution.py:411
  70.4 1.7 %collective-permute-done.26.refs_1_ = bf16[64,1024]{1,0:T(8,128)(2,1)S(1)} collective-permute-done((bf16[64,1024]{1,0:T(8,128)(2,1)S(1)}, bf16[64,1024]{1,0:T(8,128)(2,1)S(1)}, u32[]{:S(2)}, u32[]{:S(2)}) %collective-permute-start.26) | collective-permute-done | bytes 131104 | tf_op jit(solution)/shard_map/ppermute | solution.py:411
  74.0 1.6 %collective-permute-start.29 = (bf16[64,1024]{1,0:T(8,128)(2,1)S(1)}, bf16[64,1024]{1,0:T(8,128)(2,1)S(1)}, u32[]{:S(2)}, u32[]{:S(2)}) collective-permute-start(bf16[64,1024]{1,0:T(8,128)(2,1)S(1)} %get-tuple-element.93.refs_0_), channel_id=1, source_target_pairs={{0,16},{8,24},{16,0},{24,8},{1,17},{9,25},{17,1},{25,9},{2,18},{10... | collective-permute-start | bytes 393224 | tf_op jit(solution)/shard_map/ppermute | solution.py:411
  76.8 8.0 %all-gather.7.cloned.1.call-done = bf16[16896,128]{1,0:T(8,128)(2,1)} async-done(((bf16[2112,128]{1,0:T(8,128)(2,1)}), bf16[16896,128]{1,0:T(8,128)(2,1)}) %all-gather.7.cloned.1.call-update) | async-done | bytes 4325392 | tf_op jit(solution)/shard_map/all_gather | solution.py:415
  84.8 2.2 %copy-done.1 = bf16[16896,128]{1,0:T(8,128)(2,1)S(1)} copy-done((bf16[16896,128]{1,0:T(8,128)(2,1)S(1)}, bf16[16896,128]{1,0:T(8,128)(2,1)}, u32[]{:S(2)}) %copy-start.1) | copy-done | bytes 4325400
  89.7 1.5 %collective-permute-start.16 = (bf16[64,1024]{1,0:T(8,128)(2,1)S(1)}, bf16[64,1024]{1,0:T(8,128)(2,1)S(1)}, u32[]{:S(2)}, u32[]{:S(2)}) collective-permute-start(bf16[64,1024]{1,0:T(8,128)(2,1)S(1)} %get-tuple-element.73), channel_id=1, source_target_pairs={{0,8},{8,0},{16,24},{24,16},{1,9},{9,1},{17,25},{25,17},{2,10},{10... | collective-permute-start | bytes 393224 | tf_op jit(solution)/shard_map/ppermute | solution.py:411
  91.3 1.5 %collective-permute-start.17 = (bf16[64,1024]{1,0:T(8,128)(2,1)S(1)}, bf16[64,1024]{1,0:T(8,128)(2,1)S(1)}, u32[]{:S(2)}, u32[]{:S(2)}) collective-permute-start(bf16[64,1024]{1,0:T(8,128)(2,1)S(1)} %get-tuple-element.74), channel_id=1, source_target_pairs={{0,16},{8,24},{16,0},{24,8},{1,17},{9,25},{17,1},{25,9},{2,18},{10... | collective-permute-start | bytes 393224 | tf_op jit(solution)/shard_map/ppermute | solution.py:411
  94.7 1.5 %collective-permute-start.31 = (bf16[64,1024]{1,0:T(8,128)(2,1)S(1)}, bf16[64,1024]{1,0:T(8,128)(2,1)S(1)}, u32[]{:S(2)}, u32[]{:S(2)}) collective-permute-start(bf16[64,1024]{1,0:T(8,128)(2,1)S(1)} %get-tuple-element.95), channel_id=1, source_target_pairs={{0,8},{8,0},{16,24},{24,16},{1,9},{9,1},{17,25},{25,17},{2,10},{10... | collective-permute-start | bytes 393224 | tf_op jit(solution)/shard_map/ppermute | solution.py:411
  102.2 2.0 %collective-permute-start.39 = (bf16[64,1024]{1,0:T(8,128)(2,1)S(1)}, bf16[64,1024]{1,0:T(8,128)(2,1)S(1)}, u32[]{:S(2)}, u32[]{:S(2)}) collective-permute-start(bf16[64,1024]{1,0:T(8,128)(2,1)S(1)} %get-tuple-element.101.refs_0_), channel_id=1, source_target_pairs={{0,24},{8,16},{16,8},{24,0},{1,25},{9,17},{17,9},{25,1},{2,26},{10... | collective-permute-start | bytes 393224 | tf_op jit(solution)/shard_map/ppermute | solution.py:411
  107.8 2.0 %collective-permute-start.36 = (bf16[64,1024]{1,0:T(8,128)(2,1)S(1)}, bf16[64,1024]{1,0:T(8,128)(2,1)S(1)}, u32[]{:S(2)}, u32[]{:S(2)}) collective-permute-start(bf16[64,1024]{1,0:T(8,128)(2,1)S(1)} %get-tuple-element.100.refs_0_), channel_id=1, source_target_pairs={{0,24},{8,16},{16,8},{24,0},{1,25},{9,17},{17,9},{25,1},{2,26},{10... | collective-permute-start | bytes 393224 | tf_op jit(solution)/shard_map/ppermute | solution.py:411
  114.2 2.1 %collective-permute-done.35.refs_2_ = bf16[64,1024]{1,0:T(8,128)(2,1)S(1)} collective-permute-done((bf16[64,1024]{1,0:T(8,128)(2,1)S(1)}, bf16[64,1024]{1,0:T(8,128)(2,1)S(1)}, u32[]{:S(2)}, u32[]{:S(2)}) %collective-permute-start.35) | collective-permute-done | bytes 131104 | tf_op jit(solution)/shard_map/ppermute | solution.py:411
  (119 shorter events, 52.5 us)
Async XLA Ops:
  7.2 42.7 %all-gather.9.cloned.1.call-start = ((), (), s32[]{:S(2)}) async-start(), calls=%async_computation.1 | async-start | bytes 1179648 | tf_op jit(solution)/shard_map/all_gather | solution.py:415
  9.5 75.3 %all-gather.7.cloned.1.call-start = ((), (), s32[]{:S(2)}) async-start(), calls=%async_computation | async-start | bytes 4866048 | tf_op jit(solution)/shard_map/all_gather | solution.py:415
  9.6 14.9 %collective-permute-start = (bf16[256,128]{1,0:T(8,128)(2,1)}, bf16[256,128]{1,0:T(8,128)(2,1)S(1)}, u32[]{:S(2)}, u32[]{:S(2)}) collective-permute-start(bf16[256,128]{1,0:T(8,128)(2,1)} %param.33), channel_id=1, source_target_pairs={{0,4},{1,5},{2,6},{3,7},{4,0},{5,1},{6,2},{7,3},{8,12},{9,13},{10,... | collective-permute-start | bytes 196616 | tf_op jit(solution)/shard_map/ppermute | solution.py:411
  13.7 10.8 %collective-permute-start.1 = (bf16[256,128]{1,0:T(8,128)(2,1)}, bf16[256,128]{1,0:T(8,128)(2,1)S(1)}, u32[]{:S(2)}, u32[]{:S(2)}) collective-permute-start(bf16[256,128]{1,0:T(8,128)(2,1)} %param.33), channel_id=1, source_target_pairs={{0,6},{1,7},{2,4},{3,5},{4,2},{5,3},{6,0},{7,1},{8,14},{9,15},{10,... | collective-permute-start | bytes 196616 | tf_op jit(solution)/shard_map/ppermute | solution.py:411
  15.0 9.5 %collective-permute-start.2 = (bf16[256,128]{1,0:T(8,128)(2,1)}, bf16[256,128]{1,0:T(8,128)(2,1)S(1)}, u32[]{:S(2)}, u32[]{:S(2)}) collective-permute-start(bf16[256,128]{1,0:T(8,128)(2,1)} %param.33), channel_id=1, source_target_pairs={{0,2},{1,3},{2,0},{3,1},{4,6},{5,7},{6,4},{7,5},{8,10},{9,11},{10,... | collective-permute-start | bytes 196616 | tf_op jit(solution)/shard_map/ppermute | solution.py:411
  25.5 85.0 %all-gather.11.cloned.1.call-start = ((), (), s32[]{:S(2)}) async-start(), calls=%async_computation.2 | async-start | bytes 1769472 | tf_op jit(solution)/shard_map/all_gather | solution.py:415
  31.6 9.6 %collective-permute-start.19 = (bf16[64,1024]{1,0:T(8,128)(2,1)S(1)}, bf16[64,1024]{1,0:T(8,128)(2,1)S(1)}, u32[]{:S(2)}, u32[]{:S(2)}) collective-permute-start(bf16[64,1024]{1,0:T(8,128)(2,1)S(1)} %get-tuple-element.83), channel_id=1, source_target_pairs={{0,8},{8,0},{16,24},{24,16},{1,9},{9,1},{17,25},{25,17},{2,10},{10... | collective-permute-start | bytes 393224 | tf_op jit(solution)/shard_map/ppermute | solution.py:411
  33.1 10.5 %collective-permute-start.20 = (bf16[64,1024]{1,0:T(8,128)(2,1)S(1)}, bf16[64,1024]{1,0:T(8,128)(2,1)S(1)}, u32[]{:S(2)}, u32[]{:S(2)}) collective-permute-start(bf16[64,1024]{1,0:T(8,128)(2,1)S(1)} %get-tuple-element.84), channel_id=1, source_target_pairs={{0,16},{8,24},{16,0},{24,8},{1,17},{9,25},{17,1},{25,9},{2,18},{10... | collective-permute-start | bytes 393224 | tf_op jit(solution)/shard_map/ppermute | solution.py:411
  34.6 9.5 %collective-permute-start.21 = (bf16[64,1024]{1,0:T(8,128)(2,1)S(1)}, bf16[64,1024]{1,0:T(8,128)(2,1)S(1)}, u32[]{:S(2)}, u32[]{:S(2)}) collective-permute-start(bf16[64,1024]{1,0:T(8,128)(2,1)S(1)} %get-tuple-element.85), channel_id=1, source_target_pairs={{0,24},{8,16},{16,8},{24,0},{1,25},{9,17},{17,9},{25,1},{2,26},{10... | collective-permute-start | bytes 393224 | tf_op jit(solution)/shard_map/ppermute | solution.py:411
  40.0 9.2 %collective-permute-start.8 = (bf16[64,1024]{1,0:T(8,128)(2,1)S(1)}, bf16[64,1024]{1,0:T(8,128)(2,1)S(1)}, u32[]{:S(2)}, u32[]{:S(2)}) collective-permute-start(bf16[64,1024]{1,0:T(8,128)(2,1)S(1)} %get-tuple-element.65.refs_0_), channel_id=1, source_target_pairs={{0,16},{8,24},{16,0},{24,8},{1,17},{9,25},{17,1},{25,9},{2,18},{10... | collective-permute-start | bytes 393224 | tf_op jit(solution)/shard_map/ppermute | solution.py:411
  44.3 14.0 %collective-permute-start.22 = (bf16[64,1024]{1,0:T(8,128)(2,1)S(1)}, bf16[64,1024]{1,0:T(8,128)(2,1)S(1)}, u32[]{:S(2)}, u32[]{:S(2)}) collective-permute-start(bf16[64,1024]{1,0:T(8,128)(2,1)S(1)} %get-tuple-element.87.refs_0_), channel_id=1, source_target_pairs={{0,8},{8,0},{16,24},{24,16},{1,9},{9,1},{17,25},{25,17},{2,10},{10... | collective-permute-start | bytes 393224 | tf_op jit(solution)/shard_map/ppermute | solution.py:411
  45.7 14.0 %collective-permute-start.23 = (bf16[64,1024]{1,0:T(8,128)(2,1)S(1)}, bf16[64,1024]{1,0:T(8,128)(2,1)S(1)}, u32[]{:S(2)}, u32[]{:S(2)}) collective-permute-start(bf16[64,1024]{1,0:T(8,128)(2,1)S(1)} %get-tuple-element.87.refs_0_), channel_id=1, source_target_pairs={{0,16},{8,24},{16,0},{24,8},{1,17},{9,25},{17,1},{25,9},{2,18},{10... | collective-permute-start | bytes 393224 | tf_op jit(solution)/shard_map/ppermute | solution.py:411
  46.9 12.8 %collective-permute-start.24 = (bf16[64,1024]{1,0:T(8,128)(2,1)S(1)}, bf16[64,1024]{1,0:T(8,128)(2,1)S(1)}, u32[]{:S(2)}, u32[]{:S(2)}) collective-permute-start(bf16[64,1024]{1,0:T(8,128)(2,1)S(1)} %get-tuple-element.87.refs_0_), channel_id=1, source_target_pairs={{0,24},{8,16},{16,8},{24,0},{1,25},{9,17},{17,9},{25,1},{2,26},{10... | collective-permute-start | bytes 393224 | tf_op jit(solution)/shard_map/ppermute | solution.py:411
  57.2 8.7 %collective-permute-start.11 = (bf16[64,1024]{1,0:T(8,128)(2,1)S(1)}, bf16[64,1024]{1,0:T(8,128)(2,1)S(1)}, u32[]{:S(2)}, u32[]{:S(2)}) collective-permute-start(bf16[64,1024]{1,0:T(8,128)(2,1)S(1)} %get-tuple-element.68), channel_id=1, source_target_pairs={{0,16},{8,24},{16,0},{24,8},{1,17},{9,25},{17,1},{25,9},{2,18},{10... | collective-permute-start | bytes 393224 | tf_op jit(solution)/shard_map/ppermute | solution.py:411
  63.3 8.9 %collective-permute-start.26 = (bf16[64,1024]{1,0:T(8,128)(2,1)S(1)}, bf16[64,1024]{1,0:T(8,128)(2,1)S(1)}, u32[]{:S(2)}, u32[]{:S(2)}) collective-permute-start(bf16[64,1024]{1,0:T(8,128)(2,1)S(1)} %get-tuple-element.90), channel_id=1, source_target_pairs={{0,16},{8,24},{16,0},{24,8},{1,17},{9,25},{17,1},{25,9},{2,18},{10... | collective-permute-start | bytes 393224 | tf_op jit(solution)/shard_map/ppermute | solution.py:411
  66.6 9.1 %collective-permute-start.13 = (bf16[64,1024]{1,0:T(8,128)(2,1)S(1)}, bf16[64,1024]{1,0:T(8,128)(2,1)S(1)}, u32[]{:S(2)}, u32[]{:S(2)}) collective-permute-start(bf16[64,1024]{1,0:T(8,128)(2,1)S(1)} %get-tuple-element.71.refs_0_), channel_id=1, source_target_pairs={{0,8},{8,0},{16,24},{24,16},{1,9},{9,1},{17,25},{25,17},{2,10},{10... | collective-permute-start | bytes 393224 | tf_op jit(solution)/shard_map/ppermute | solution.py:411
  67.9 20.4 %collective-permute-start.14 = (bf16[64,1024]{1,0:T(8,128)(2,1)S(1)}, bf16[64,1024]{1,0:T(8,128)(2,1)S(1)}, u32[]{:S(2)}, u32[]{:S(2)}) collective-permute-start(bf16[64,1024]{1,0:T(8,128)(2,1)S(1)} %get-tuple-element.71.refs_0_), channel_id=1, source_target_pairs={{0,16},{8,24},{16,0},{24,8},{1,17},{9,25},{17,1},{25,9},{2,18},{10... | collective-permute-start | bytes 393224 | tf_op jit(solution)/shard_map/ppermute | solution.py:411
  69.0 19.3 %collective-permute-start.15 = (bf16[64,1024]{1,0:T(8,128)(2,1)S(1)}, bf16[64,1024]{1,0:T(8,128)(2,1)S(1)}, u32[]{:S(2)}, u32[]{:S(2)}) collective-permute-start(bf16[64,1024]{1,0:T(8,128)(2,1)S(1)} %get-tuple-element.71.refs_0_), channel_id=1, source_target_pairs={{0,24},{8,16},{16,8},{24,0},{1,25},{9,17},{17,9},{25,1},{2,26},{10... | collective-permute-start | bytes 393224 | tf_op jit(solution)/shard_map/ppermute | solution.py:411
  73.3 19.5 %collective-permute-start.28 = (bf16[64,1024]{1,0:T(8,128)(2,1)S(1)}, bf16[64,1024]{1,0:T(8,128)(2,1)S(1)}, u32[]{:S(2)}, u32[]{:S(2)}) collective-permute-start(bf16[64,1024]{1,0:T(8,128)(2,1)S(1)} %get-tuple-element.93.refs_0_), channel_id=1, source_target_pairs={{0,8},{8,0},{16,24},{24,16},{1,9},{9,1},{17,25},{25,17},{2,10},{10... | collective-permute-start | bytes 393224 | tf_op jit(solution)/shard_map/ppermute | solution.py:411
  74.0 19.3 %collective-permute-start.29 = (bf16[64,1024]{1,0:T(8,128)(2,1)S(1)}, bf16[64,1024]{1,0:T(8,128)(2,1)S(1)}, u32[]{:S(2)}, u32[]{:S(2)}) collective-permute-start(bf16[64,1024]{1,0:T(8,128)(2,1)S(1)} %get-tuple-element.93.refs_0_), channel_id=1, source_target_pairs={{0,16},{8,24},{16,0},{24,8},{1,17},{9,25},{17,1},{25,9},{2,18},{10... | collective-permute-start | bytes 393224 | tf_op jit(solution)/shard_map/ppermute | solution.py:411
  75.6 17.6 %collective-permute-start.30 = (bf16[64,1024]{1,0:T(8,128)(2,1)S(1)}, bf16[64,1024]{1,0:T(8,128)(2,1)S(1)}, u32[]{:S(2)}, u32[]{:S(2)}) collective-permute-start(bf16[64,1024]{1,0:T(8,128)(2,1)S(1)} %get-tuple-element.93.refs_0_), channel_id=1, source_target_pairs={{0,24},{8,16},{16,8},{24,0},{1,25},{9,17},{17,9},{25,1},{2,26},{10... | collective-permute-start | bytes 393224 | tf_op jit(solution)/shard_map/ppermute | solution.py:411
  101.5 9.0 %collective-permute-start.38 = (bf16[64,1024]{1,0:T(8,128)(2,1)S(1)}, bf16[64,1024]{1,0:T(8,128)(2,1)S(1)}, u32[]{:S(2)}, u32[]{:S(2)}) collective-permute-start(bf16[64,1024]{1,0:T(8,128)(2,1)S(1)} %get-tuple-element.101.refs_0_), channel_id=1, source_target_pairs={{0,16},{8,24},{16,0},{24,8},{1,17},{9,25},{17,1},{25,9},{2,18},{10... | collective-permute-start | bytes 393224 | tf_op jit(solution)/shard_map/ppermute | solution.py:411
  102.2 9.3 %collective-permute-start.39 = (bf16[64,1024]{1,0:T(8,128)(2,1)S(1)}, bf16[64,1024]{1,0:T(8,128)(2,1)S(1)}, u32[]{:S(2)}, u32[]{:S(2)}) collective-permute-start(bf16[64,1024]{1,0:T(8,128)(2,1)S(1)} %get-tuple-element.101.refs_0_), channel_id=1, source_target_pairs={{0,24},{8,16},{16,8},{24,0},{1,25},{9,17},{17,9},{25,1},{2,26},{10... | collective-permute-start | bytes 393224 | tf_op jit(solution)/shard_map/ppermute | solution.py:411
  107.2 9.1 %collective-permute-start.35 = (bf16[64,1024]{1,0:T(8,128)(2,1)S(1)}, bf16[64,1024]{1,0:T(8,128)(2,1)S(1)}, u32[]{:S(2)}, u32[]{:S(2)}) collective-permute-start(bf16[64,1024]{1,0:T(8,128)(2,1)S(1)} %get-tuple-element.100.refs_0_), channel_id=1, source_target_pairs={{0,16},{8,24},{16,0},{24,8},{1,17},{9,25},{17,1},{25,9},{2,18},{10... | collective-permute-start | bytes 393224 | tf_op jit(solution)/shard_map/ppermute | solution.py:411
  (35 other events, 244.9 us)
Sparse Core Ops, SparseCore 0:
  9.6 24.8 all-gather.8
  36.8 47.9 all-gather.6
  86.5 23.7 all-gather.10

commit v4 on v3

--- a/solution.py
+++ b/solution.py
@@ -237,31 +237,28 @@
     )(own, *others, gain.reshape(1, -1))
 
 
-def cross_kernel(ways, first, length_ref, cache_ref, stream_ref, *refs):
+def cross_kernel(ways, orders, first, length_ref, cache_ref, stream_ref, *refs):
     blocks = refs[:ways]
-    given = refs[ways : -(ways + 3)]
-    own_ref = refs[-(ways + 3)]
-    out_refs = refs[-(ways + 2) : -3]
-    wq_ref, wo_ref, ctx_ref = refs[-3:]
+    given = refs[ways : -(ways + 2)]
+    own_ref = refs[-(ways + 2)]
+    out_refs = refs[-(ways + 1) : -2]
+    wq_ref, ctx_ref = refs[-2:]
     requests = cache_ref.shape[0]
     width = wq_ref.shape[1]
     heads = width // DH
     rows = blocks[0].shape[0]
     share = rows // requests
-    if len(given) == 1:
-        (slices_ref,) = given
-        pieces, _, lanes = slices_ref.shape
-        parts = width // lanes
+    wo_ref = given[-1]
+    if orders:
+        pieces, _, lanes = given[0].shape
         for k in range(pieces):
-            piece = slices_ref.at[jnp.bitwise_xor(lax.axis_index("tok"), k)]
-            for c in range(parts):
+            piece = given[0].at[jnp.bitwise_xor(lax.axis_index("tok"), k)]
+            for c in range(width // lanes):
                 here = slice(c * lanes, (c + 1) * lanes)
                 block = piece[c * lanes : (c + 1) * lanes, :]
                 wq_ref[k * lanes : (k + 1) * lanes, here] = block
-            wo_ref[:, k * lanes : (k + 1) * lanes] = piece[parts * lanes :, :]
     else:
         wq_ref[...] = given[0][...]
-        wo_ref[...] = given[1][...]
     normed = jnp.concatenate([block[...] for block in blocks], axis=0)
     query = dot(normed, wq_ref[...]).astype(BF16).reshape(ways, rows, width)
     position = lax.broadcasted_iota(jnp.int32, (1, cache_ref.shape[2]), 1)
@@ -281,13 +278,13 @@
         out_refs[k - 1][...] = part[k * rows : (k + 1) * rows].astype(BF16)
 
 
-def cross_layer(blocks, weights, cache, stream, length, first, count):
+def cross_layer(blocks, weights, orders, cache, stream, length, first, count):
     ways = len(blocks)
     rows, model = blocks[0].shape
     depth, width = cache.shape[2:]
     full = lambda shape: pl.BlockSpec(shape, lambda i: (0,) * len(shape))
     return pl.pallas_call(
-        functools.partial(cross_kernel, ways, first),
+        functools.partial(cross_kernel, ways, orders, first),
         grid=(1,),
         out_shape=[jax.ShapeDtypeStruct((rows, model), F32)]
         + [jax.ShapeDtypeStruct((rows, model), BF16)] * (ways - 1),
@@ -301,7 +298,6 @@
         out_specs=[full((rows, model))] * ways,
         scratch_shapes=[
             pltpu.VMEM((model, width), BF16),
-            pltpu.VMEM((width, model), BF16),
             pltpu.VMEM((ways, rows, width), BF16),
         ],
         compiler_params=params(CROSS_LIMIT),
@@ -310,53 +306,57 @@
     )(length, cache, stream, *blocks, *weights)
 
 
-def join_kernel(slices_ref, out_ref):
+def join_kernel(slices_ref, *out_refs):
     pieces, _, lanes = slices_ref.shape
     for k in range(pieces):
         source = jnp.bitwise_xor(lax.axis_index("tok"), k)
-        out_ref[:, k * lanes : (k + 1) * lanes] = slices_ref[source]
-
-
-def join(slices):
+        at = slices_ref.shape[1] - sum(ref.shape[0] for ref in out_refs)
+        for out_ref in out_refs:
+            rows = out_ref.shape[0]
+            out_ref[:, k * lanes : (k + 1) * lanes] = slices_ref[source, at : at + rows, :]
+            at += rows
+
+
+def join(slices, *depths):
     pieces, rows, lanes = slices.shape
     return pl.pallas_call(
         join_kernel,
-        out_shape=jax.ShapeDtypeStruct((rows, lanes * pieces), BF16),
+        out_shape=[jax.ShapeDtypeStruct((depth, lanes * pieces), BF16) for depth in depths],
         in_specs=[VMEM],
-        out_specs=VMEM,
+        out_specs=[VMEM] * len(depths),
         compiler_params=params(),
         cost_estimate=cost(1e3, 4 * rows * lanes * pieces),
         name="join",
     )(slices)
 
 
-def ffn_kernel(ways, w_ref, stream_ref, *refs):
+def ffn_kernel(ways, gate_ref, late_ref, stream_ref, *refs):
     blocks, own_ref, out_refs = refs[:ways], refs[ways], refs[ways + 1 :]
-    hidden = w_ref.shape[0] // 3
+    hidden = gate_ref.shape[0]
     rows = stream_ref.shape[0]
     normed = jnp.concatenate([block[...] for block in blocks], axis=0)
-    gate = dot_nt(normed, w_ref[:hidden, :])
-    up = dot_nt(normed, w_ref[hidden : 2 * hidden, :])
+    gate = dot_nt(normed, gate_ref[...])
+    up = dot_nt(normed, late_ref[:hidden, :])
     gated = (jax.nn.gelu(gate, approximate=True) * up).astype(BF16)
-    part = dot(gated, w_ref[2 * hidden :, :])
+    part = dot(gated, late_ref[hidden:, :])
     own_ref[...] = part[:rows] + stream_ref[...]
     for k in range(1, ways):
         out_refs[k - 1][...] = part[k * rows : (k + 1) * rows].astype(BF16)
 
 
-def ffn(blocks, w, stream):
+def ffn(blocks, w_gate, w_late, stream):
     ways = len(blocks)
     rows, model = stream.shape
     return pl.pallas_call(
         functools.partial(ffn_kernel, ways),
         out_shape=[jax.ShapeDtypeStruct((rows, model), F32)]
         + [jax.ShapeDtypeStruct((rows, model), BF16)] * (ways - 1),
-        in_specs=[VMEM] * (2 + ways),
+        in_specs=[VMEM] * (3 + ways),
         out_specs=[VMEM] * ways,
         compiler_params=params(),
-        cost_estimate=cost(2 * rows * ways * w.size, 6e6, 4e5),
+        cost_estimate=cost(2 * rows * ways * (w_gate.size + w_late.size), 6e6, 4e5),
         name="ffn",
-    )(w, stream, *blocks)
+    )(w_gate, w_late, stream, *blocks)
 
 
 def project_kernel(ways, first, slices_ref, *refs):
@@ -462,24 +462,24 @@
     bias = bias_and_mask(parents, counts, buckets, bias_table)
     ctx = self_attention(draft_qkv, self_cache, self_len, bias)
     if paired:
-        pieces, orders = total, ATTN_ORDERS
+        pieces, orders, cross_orders = total, ATTN_ORDERS, ATTN_ORDERS
         query_slices = jnp.split(w_query_cross, head_width // slice_lanes, axis=1)
-        attn_w = [all_slices(jnp.concatenate(query_slices + [w_out_cross], axis=0))]
-        out_here = [w_out_self] + [along(w_out_self, k) for k in (4, 6, 2)]
+        early = all_slices(jnp.concatenate(query_slices + [w_out_cross, w_gate.T], axis=0))
+        out_shard = w_out_self
+        out_here = [out_shard] + [along(out_shard, k) for k in (4, 6, 2)]
         ctx, out_here = gate(ctx, out_here)
         out_here = jnp.stack(out_here)
         out_w = [out_here, along(out_here, 1)]
-        out_here, w_gate, w_up, w_down, qkv_shard = gate(
-            out_here, w_gate, w_up, w_down, qkv_shard
-        )
-        ffn_w = all_slices(jnp.concatenate([w_gate.T, w_up.T, w_down], axis=0))
+        out_here, w_up, w_down, qkv_shard = gate(out_here, w_up, w_down, qkv_shard)
+        late = all_slices(jnp.concatenate([w_up.T, w_down], axis=0))
     else:
         pieces = 1
         by_row = functools.partial(lax.all_gather, axis_name="tok", axis=0, tiled=True)
         by_col = functools.partial(lax.all_gather, axis_name="tok", axis=1, tiled=True)
-        out_w, orders = [by_col(w_out_self)[None]], ((0,),)
+        out_w, orders, cross_orders = [by_col(w_out_self)[None]], ((0,),), ()
         attn_w = [by_row(w_query_cross), by_col(w_out_cross)]
-        ffn_w = jnp.concatenate([by_row(w_gate).T, by_row(w_up).T, by_col(w_down)], axis=0)
+        ffn_gate = by_row(w_gate).T
+        ffn_late = jnp.concatenate([by_row(w_up).T, by_col(w_down)], axis=0)
         qkv_w = by_col(qkv_shard)[None]
     made = [self_out(ctx, out_w, orders, hidden, ways, start, count) for start in starts]
     if paired:
@@ -488,16 +488,21 @@
     sent = [send_each(made[h][1:], ways) for h in halves]
     kept = [norm(made[h][0], sent[h], gain_cross, pieces) for h in halves]
     blocks = [spread(kept[h][1], ways) for h in halves]
+    if paired:
+        out_cross, ffn_gate = join(early, head_width, w_gate.shape[1])
+        attn_w = [early[:, :head_width], out_cross]
     made = [
-        cross_layer(blocks[h], attn_w, cross_cache, kept[h][0], enc_len, starts[h], count)
+        cross_layer(
+            blocks[h], attn_w, cross_orders, cross_cache, kept[h][0], enc_len, starts[h], count
+        )
         for h in halves
     ]
     sent = [send_each(made[h][1:], ways) for h in halves]
     kept = [norm(made[h][0], sent[h], gain_ffn, pieces) for h in halves]
     blocks = [spread(kept[h][1], ways) for h in halves]
     if paired:
-        ffn_w = join(ffn_w)
-    made = [ffn(blocks[h], ffn_w, kept[h][0]) for h in halves]
+        (ffn_late,) = join(late, w_up.shape[1] + w_down.shape[0])
+    made = [ffn(blocks[h], ffn_gate, ffn_late, kept[h][0]) for h in halves]
     sent = [send_each(made[h][1:], ways) for h in halves]
     kept = [norm(made[h][0], sent[h], gain_next, pieces, True) for h in halves]
     blocks = [spread(kept[h][1], ways) for h in halves]

time: 125 us -> 122 us (0.976)
  waiting for transfers between devices: 23.7 us -> 18.2 us
    all_gather x3, waiting for transfers between devices: 7.99 us -> 2.2 us  [all_slices(): return lax.all_gather(shard, 'tok', axis=0, tiled=False)]
    unnamed x32 -> x30, local copies, waits for them, and re-layouts: 7.13 us -> 8.26 us
    pallas_call x3 -> x4, Pallas kernels: 6.3 us -> 6.31 us  [the longest x2 4.94 us: cross_layer(): pl.pallas_call(functools.partial(cross_kernel, ways, orders, first), grid...]
  transfers between devices with their start and end apart: 43 -> 43, of which waited for: 17 -> 12; matrix products, arithmetic and copies ran while one was open for 1% -> 1% of each run, Pallas kernels for 17% -> 18%
where the time goes in v4:
time: 122 us; the launch traced here: 121 us
  starting transfers between devices  53.9 us (44%)
  Pallas kernels  22.8 us (19%)
  waiting for transfers between devices  18.2 us (15%)
  between operations  14.1 us (12%)
  local copies, waits for them, and re-layouts  9.08 us (7%)
  other arithmetic  3.24 us (3%)
    ppermute x40, starting transfers between devices, partner(): return lax.ppermute(value, axis, [(i, i ^ k) for i in range(size)])  53.6 us
    ppermute x40, waiting for transfers between devices, partner(): return lax.ppermute(value, axis, [(i, i ^ k) for i in range(size)])  16 us
    unnamed x30, local copies, waits for them, and re-layouts  8.26 us
    pallas_call x1, Pallas kernels, self_attention(): pl.pallas_call(self_kernel, grid=(HALVES,), out_shape=jax.ShapeDtypeStruc...  5.98 us
    pallas_call x2, Pallas kernels, cross_layer(): pl.pallas_call(functools.partial(cross_kernel, ways, orders, first), grid...  4.94 us
    pallas_call x1, Pallas kernels, bias_and_mask(): pl.pallas_call(bias_kernel, out_shape=jax.ShapeDtypeStruct((requests, hea...  3.29 us
    pallas_call x2, Pallas kernels, ffn(): pl.pallas_call(functools.partial(ffn_kernel, ways), out_shape=[jax.ShapeD...  2.85 us
    pallas_call x2, Pallas kernels, project(): pl.pallas_call(functools.partial(project_kernel, ways, first), out_shape=...  2.69 us
  transfers between devices with their start and end apart: 43, of which 12 were waited for; matrix products, arithmetic and copies ran while one was open for 1% of the time, Pallas kernels for 18%

profile of v4, /device:TPU:0, one launch (start us, length us, event | category | flops | bytes accessed | tf_op | source)
XLA Modules:
  0.0 121.3 jit_solution(16439601835447976431)
XLA Ops:
  8.0 1.7 %pad_maximum_fusion.1 = bf16[1216,128]{1,0:T(8,128)(2,1)} fusion(bf16[704,128]{1,0:T(8,128)(2,1)} %bitcast.28, bf16[256,128]{1,0:T(8,128)(2,1)} %param.35, bf16[128,128]{1,0:T(8,128)(2,1)S(1)} %get-tuple-element.105, bf16[128,128]{1,0:T(8,128)(2,1)S(1)} %get-tuple-element.104), kind=kLoop, calls=%fused_computation.1 | loop fusion | flops 1245184 | bytes 622592 | tf_op jit(solution)/shard_map/concatenate | solution.py:467
  9.8 5.1 %collective-permute-start.1 = (bf16[256,128]{1,0:T(8,128)(2,1)}, bf16[256,128]{1,0:T(8,128)(2,1)S(1)}, u32[]{:S(2)}, u32[]{:S(2)}) collective-permute-start(bf16[256,128]{1,0:T(8,128)(2,1)} %param.33), channel_id=1, source_target_pairs={{0,6},{1,7},{2,4},{3,5},{4,2},{5,3},{6,0},{7,1},{8,14},{9,15},{10,... | collective-permute-start | bytes 196616 | tf_op jit(solution)/shard_map/ppermute | solution.py:411
  15.5 3.3 %bias_and_mask.1.bias_ref = f32[8,256,64]{2,1,0:T(8,128)} custom-call(s32[8,64]{1,0:T(8,128)} %parents_ref.1, s32[8]{0:T(128)} %counts_ref.1, s32[8,64,64]{2,1,0:T(8,128)} %buckets_ref.1, f32[4,32]{1,0:T(4,128)} %bitcast.34), custom_call_target="tpu_custom_call" | custom-call | flops 60000000 | bytes 1200000 | tf_op jit(solution)/shard_map/bias_and_mask/pallas_call | solution.py:97
  18.8 6.0 %self_attention.1.refs_2_ = bf16[8,64,256]{2,1,0:T(8,128)(2,1)} custom-call(s32[8]{0:T(128)} %length_ref.3, bf16[3,8,64,256]{3,2,1,0:T(8,128)(2,1)} %qkv_ref.1, bf16[8,2,512,256]{3,2,1,0:T(8,128)(2,1)} %cache_ref.3, f32[8,256,64]{2,1,0:T(8,128)} %bias_and_mask.1.bias_ref), custom_call_target="tpu_custom_call" | custom-call | flops 5000000000 | bytes 6000000 | tf_op jit(solution)/shard_map/self_attention/pallas_call | solution.py:131
  29.3 1.7 %collective-permute-start.4 = (bf16[64,1024]{1,0:T(8,128)(2,1)S(1)}, bf16[64,1024]{1,0:T(8,128)(2,1)S(1)}, u32[]{:S(2)}, u32[]{:S(2)}) collective-permute-start(bf16[64,1024]{1,0:T(8,128)(2,1)S(1)} %get-tuple-element.62), channel_id=1, source_target_pairs={{0,8},{8,0},{16,24},{24,16},{1,9},{9,1},{17,25},{25,17},{2,10},{10... | collective-permute-start | bytes 393224 | tf_op jit(solution)/shard_map/ppermute | solution.py:411
  31.0 1.6 %collective-permute-start.5 = (bf16[64,1024]{1,0:T(8,128)(2,1)S(1)}, bf16[64,1024]{1,0:T(8,128)(2,1)S(1)}, u32[]{:S(2)}, u32[]{:S(2)}) collective-permute-start(bf16[64,1024]{1,0:T(8,128)(2,1)S(1)} %get-tuple-element.63), channel_id=1, source_target_pairs={{0,16},{8,24},{16,0},{24,8},{1,17},{9,25},{17,1},{25,9},{2,18},{10... | collective-permute-start | bytes 393224 | tf_op jit(solution)/shard_map/ppermute | solution.py:411
  32.8 1.7 %collective-permute-start.19 = (bf16[64,1024]{1,0:T(8,128)(2,1)S(1)}, bf16[64,1024]{1,0:T(8,128)(2,1)S(1)}, u32[]{:S(2)}, u32[]{:S(2)}) collective-permute-start(bf16[64,1024]{1,0:T(8,128)(2,1)S(1)} %get-tuple-element.85), channel_id=1, source_target_pairs={{0,8},{8,0},{16,24},{24,16},{1,9},{9,1},{17,25},{25,17},{2,10},{10... | collective-permute-start | bytes 393224 | tf_op jit(solution)/shard_map/ppermute | solution.py:411
  34.5 1.6 %collective-permute-start.20 = (bf16[64,1024]{1,0:T(8,128)(2,1)S(1)}, bf16[64,1024]{1,0:T(8,128)(2,1)S(1)}, u32[]{:S(2)}, u32[]{:S(2)}) collective-permute-start(bf16[64,1024]{1,0:T(8,128)(2,1)S(1)} %get-tuple-element.86), channel_id=1, source_target_pairs={{0,16},{8,24},{16,0},{24,8},{1,17},{9,25},{17,1},{25,9},{2,18},{10... | collective-permute-start | bytes 393224 | tf_op jit(solution)/shard_map/ppermute | solution.py:411
  36.1 2.3 %collective-permute-start.21 = (bf16[64,1024]{1,0:T(8,128)(2,1)S(1)}, bf16[64,1024]{1,0:T(8,128)(2,1)S(1)}, u32[]{:S(2)}, u32[]{:S(2)}) collective-permute-start(bf16[64,1024]{1,0:T(8,128)(2,1)S(1)} %get-tuple-element.87), channel_id=1, source_target_pairs={{0,24},{8,16},{16,8},{24,0},{1,25},{9,17},{17,9},{25,1},{2,26},{10... | collective-permute-start | bytes 393224 | tf_op jit(solution)/shard_map/ppermute | solution.py:411
  41.4 1.6 %collective-permute-start.8 = (bf16[64,1024]{1,0:T(8,128)(2,1)S(1)}, bf16[64,1024]{1,0:T(8,128)(2,1)S(1)}, u32[]{:S(2)}, u32[]{:S(2)}) collective-permute-start(bf16[64,1024]{1,0:T(8,128)(2,1)S(1)} %get-tuple-element.66.refs_0_), channel_id=1, source_target_pairs={{0,16},{8,24},{16,0},{24,8},{1,17},{9,25},{17,1},{25,9},{2,18},{10... | collective-permute-start | bytes 393224 | tf_op jit(solution)/shard_map/ppermute | solution.py:411
  44.4 3.3 %collective-permute-done.20.refs_1_ = bf16[64,1024]{1,0:T(8,128)(2,1)S(1)} collective-permute-done((bf16[64,1024]{1,0:T(8,128)(2,1)S(1)}, bf16[64,1024]{1,0:T(8,128)(2,1)S(1)}, u32[]{:S(2)}, u32[]{:S(2)}) %collective-permute-start.20) | collective-permute-done | bytes 131104 | tf_op jit(solution)/shard_map/ppermute | solution.py:411
  47.9 1.6 %collective-permute-start.24 = (bf16[64,1024]{1,0:T(8,128)(2,1)S(1)}, bf16[64,1024]{1,0:T(8,128)(2,1)S(1)}, u32[]{:S(2)}, u32[]{:S(2)}) collective-permute-start(bf16[64,1024]{1,0:T(8,128)(2,1)S(1)} %get-tuple-element.89.refs_0_), channel_id=1, source_target_pairs={{0,24},{8,16},{16,8},{24,0},{1,25},{9,17},{17,9},{25,1},{2,26},{10... | collective-permute-start | bytes 393224 | tf_op jit(solution)/shard_map/ppermute | solution.py:411
  50.5 1.7 %copy-done.1 = bf16[9728,128]{1,0:T(8,128)(2,1)S(1)} copy-done((bf16[9728,128]{1,0:T(8,128)(2,1)S(1)}, bf16[9728,128]{1,0:T(8,128)(2,1)}, u32[]{:S(2)}) %copy-start.1) | copy-done | bytes 2490392
  54.3 2.3 %copy-done.9 = bf16[8,2,512,256]{3,2,1,0:T(8,128)(2,1)S(1)} copy-done((bf16[8,2,512,256]{3,2,1,0:T(8,128)(2,1)S(1)}, bf16[8,2,512,256]{3,2,1,0:T(8,128)(2,1)}, u32[]{:S(2)}) %copy-start.9) | copy-done | bytes 4194328
  56.7 2.5 %cross_layer.2 = (f32[64,1024]{1,0:T(8,128)S(1)}, bf16[64,1024]{1,0:T(8,128)(2,1)S(1)}, bf16[64,1024]{1,0:T(8,128)(2,1)S(1)}, bf16[64,1024]{1,0:T(8,128)(2,1)S(1)}) custom-call(s32[8]{0:T(128)S(1)} %copy-done.11, bf16[8,2,512,256]{3,2,1,0:T(8,128)(2,1)S(1)} %copy-done.9, f32[64,1024]{1,0:T(8,128)S(1)} %get-tuple-element.65.stream_ref, ...), custom_call_target="tpu_custom_call" | custom-call | flops 2500000000 | bytes 4000000 | tf_op jit(solution)/shard_map/cross_layer/pallas_call | solution.py:286
  62.7 2.5 %cross_layer.3 = (f32[64,1024]{1,0:T(8,128)S(1)}, bf16[64,1024]{1,0:T(8,128)(2,1)S(1)}, bf16[64,1024]{1,0:T(8,128)(2,1)S(1)}, bf16[64,1024]{1,0:T(8,128)(2,1)S(1)}) custom-call(s32[8]{0:T(128)S(1)} %copy-done.11, bf16[8,2,512,256]{3,2,1,0:T(8,128)(2,1)S(1)} %copy-done.10, f32[64,1024]{1,0:T(8,128)S(1)} %get-tuple-element.88.stream_ref, ...), custom_call_target="tpu_custom_call" | custom-call | flops 2500000000 | bytes 4000000 | tf_op jit(solution)/shard_map/cross_layer/pallas_call | solution.py:286
  69.9 3.5 %collective-permute-start.15 = (bf16[64,1024]{1,0:T(8,128)(2,1)S(1)}, bf16[64,1024]{1,0:T(8,128)(2,1)S(1)}, u32[]{:S(2)}, u32[]{:S(2)}) collective-permute-start(bf16[64,1024]{1,0:T(8,128)(2,1)S(1)} %get-tuple-element.73.refs_0_), channel_id=1, source_target_pairs={{0,24},{8,16},{16,8},{24,0},{1,25},{9,17},{17,9},{25,1},{2,26},{10... | collective-permute-start | bytes 393224 | tf_op jit(solution)/shard_map/ppermute | solution.py:411
  74.1 2.1 %collective-permute-done.26.refs_1_ = bf16[64,1024]{1,0:T(8,128)(2,1)S(1)} collective-permute-done((bf16[64,1024]{1,0:T(8,128)(2,1)S(1)}, bf16[64,1024]{1,0:T(8,128)(2,1)S(1)}, u32[]{:S(2)}, u32[]{:S(2)}) %collective-permute-start.26) | collective-permute-done | bytes 131104 | tf_op jit(solution)/shard_map/ppermute | solution.py:411
  76.3 3.6 %collective-permute-start.30 = (bf16[64,1024]{1,0:T(8,128)(2,1)S(1)}, bf16[64,1024]{1,0:T(8,128)(2,1)S(1)}, u32[]{:S(2)}, u32[]{:S(2)}) collective-permute-start(bf16[64,1024]{1,0:T(8,128)(2,1)S(1)} %get-tuple-element.95.refs_0_), channel_id=1, source_target_pairs={{0,24},{8,16},{16,8},{24,0},{1,25},{9,17},{17,9},{25,1},{2,26},{10... | collective-permute-start | bytes 393224 | tf_op jit(solution)/shard_map/ppermute | solution.py:411
  80.6 2.2 %all-gather.9.cloned.1.call-done = bf16[11264,128]{1,0:T(8,128)(2,1)} async-done(((bf16[1408,128]{1,0:T(8,128)(2,1)}), bf16[11264,128]{1,0:T(8,128)(2,1)}) %all-gather.9.cloned.1.call-update) | async-done | bytes 2883600 | tf_op jit(solution)/shard_map/all_gather | solution.py:415
  82.8 1.8 %copy-done.2 = bf16[11264,128]{1,0:T(8,128)(2,1)S(1)} copy-done((bf16[11264,128]{1,0:T(8,128)(2,1)S(1)}, bf16[11264,128]{1,0:T(8,128)(2,1)}, u32[]{:S(2)}) %copy-start.2) | copy-done | bytes 2883608
  86.9 1.5 %collective-permute-start.16 = (bf16[64,1024]{1,0:T(8,128)(2,1)S(1)}, bf16[64,1024]{1,0:T(8,128)(2,1)S(1)}, u32[]{:S(2)}, u32[]{:S(2)}) collective-permute-start(bf16[64,1024]{1,0:T(8,128)(2,1)S(1)} %get-tuple-element.75), channel_id=1, source_target_pairs={{0,8},{8,0},{16,24},{24,16},{1,9},{9,1},{17,25},{25,17},{2,10},{10... | collective-permute-start | bytes 393224 | tf_op jit(solution)/shard_map/ppermute | solution.py:411
  101.0 3.9 %collective-permute-done.32.refs_1_ = bf16[64,1024]{1,0:T(8,128)(2,1)S(1)} collective-permute-done((bf16[64,1024]{1,0:T(8,128)(2,1)S(1)}, bf16[64,1024]{1,0:T(8,128)(2,1)S(1)}, u32[]{:S(2)}, u32[]{:S(2)}) %collective-permute-start.32) | collective-permute-done | bytes 131104 | tf_op jit(solution)/shard_map/ppermute | solution.py:411
  105.1 1.6 %collective-permute-start.36 = (bf16[64,1024]{1,0:T(8,128)(2,1)S(1)}, bf16[64,1024]{1,0:T(8,128)(2,1)S(1)}, u32[]{:S(2)}, u32[]{:S(2)}) collective-permute-start(bf16[64,1024]{1,0:T(8,128)(2,1)S(1)} %get-tuple-element.102.refs_0_), channel_id=1, source_target_pairs={{0,24},{8,16},{16,8},{24,0},{1,25},{9,17},{17,9},{25,1},{2,26},{10... | collective-permute-start | bytes 393224 | tf_op jit(solution)/shard_map/ppermute | solution.py:411
  (119 shorter events, 46.4 us)
Async XLA Ops:
  7.2 43.4 %all-gather.7.cloned.1.call-start = ((), (), s32[]{:S(2)}) async-start(), calls=%async_computation | async-start | bytes 2801664 | tf_op jit(solution)/shard_map/all_gather | solution.py:415
  9.7 73.0 %all-gather.9.cloned.1.call-start = ((), (), s32[]{:S(2)}) async-start(), calls=%async_computation.1 | async-start | bytes 3244032 | tf_op jit(solution)/shard_map/all_gather | solution.py:415
  9.8 15.0 %collective-permute-start.1 = (bf16[256,128]{1,0:T(8,128)(2,1)}, bf16[256,128]{1,0:T(8,128)(2,1)S(1)}, u32[]{:S(2)}, u32[]{:S(2)}) collective-permute-start(bf16[256,128]{1,0:T(8,128)(2,1)} %param.33), channel_id=1, source_target_pairs={{0,6},{1,7},{2,4},{3,5},{4,2},{5,3},{6,0},{7,1},{8,14},{9,15},{10,... | collective-permute-start | bytes 196616 | tf_op jit(solution)/shard_map/ppermute | solution.py:411
  14.9 9.9 %collective-permute-start.2 = (bf16[256,128]{1,0:T(8,128)(2,1)}, bf16[256,128]{1,0:T(8,128)(2,1)S(1)}, u32[]{:S(2)}, u32[]{:S(2)}) collective-permute-start(bf16[256,128]{1,0:T(8,128)(2,1)} %param.33), channel_id=1, source_target_pairs={{0,2},{1,3},{2,0},{3,1},{4,6},{5,7},{6,4},{7,5},{8,10},{9,11},{10,... | collective-permute-start | bytes 196616 | tf_op jit(solution)/shard_map/ppermute | solution.py:411
  25.7 84.0 %all-gather.11.cloned.1.call-start = ((), (), s32[]{:S(2)}) async-start(), calls=%async_computation.2 | async-start | bytes 1769472 | tf_op jit(solution)/shard_map/all_gather | solution.py:415
  32.8 10.2 %collective-permute-start.19 = (bf16[64,1024]{1,0:T(8,128)(2,1)S(1)}, bf16[64,1024]{1,0:T(8,128)(2,1)S(1)}, u32[]{:S(2)}, u32[]{:S(2)}) collective-permute-start(bf16[64,1024]{1,0:T(8,128)(2,1)S(1)} %get-tuple-element.85), channel_id=1, source_target_pairs={{0,8},{8,0},{16,24},{24,16},{1,9},{9,1},{17,25},{25,17},{2,10},{10... | collective-permute-start | bytes 393224 | tf_op jit(solution)/shard_map/ppermute | solution.py:411
  34.5 13.2 %collective-permute-start.20 = (bf16[64,1024]{1,0:T(8,128)(2,1)S(1)}, bf16[64,1024]{1,0:T(8,128)(2,1)S(1)}, u32[]{:S(2)}, u32[]{:S(2)}) collective-permute-start(bf16[64,1024]{1,0:T(8,128)(2,1)S(1)} %get-tuple-element.86), channel_id=1, source_target_pairs={{0,16},{8,24},{16,0},{24,8},{1,17},{9,25},{17,1},{25,9},{2,18},{10... | collective-permute-start | bytes 393224 | tf_op jit(solution)/shard_map/ppermute | solution.py:411
  36.1 11.7 %collective-permute-start.21 = (bf16[64,1024]{1,0:T(8,128)(2,1)S(1)}, bf16[64,1024]{1,0:T(8,128)(2,1)S(1)}, u32[]{:S(2)}, u32[]{:S(2)}) collective-permute-start(bf16[64,1024]{1,0:T(8,128)(2,1)S(1)} %get-tuple-element.87), channel_id=1, source_target_pairs={{0,24},{8,16},{16,8},{24,0},{1,25},{9,17},{17,9},{25,1},{2,26},{10... | collective-permute-start | bytes 393224 | tf_op jit(solution)/shard_map/ppermute | solution.py:411
  40.1 12.7 %collective-permute-start.9 = (bf16[64,1024]{1,0:T(8,128)(2,1)S(1)}, bf16[64,1024]{1,0:T(8,128)(2,1)S(1)}, u32[]{:S(2)}, u32[]{:S(2)}) collective-permute-start(bf16[64,1024]{1,0:T(8,128)(2,1)S(1)} %get-tuple-element.66.refs_0_), channel_id=1, source_target_pairs={{0,24},{8,16},{16,8},{24,0},{1,25},{9,17},{17,9},{25,1},{2,26},{10... | collective-permute-start | bytes 393224 | tf_op jit(solution)/shard_map/ppermute | solution.py:411
  41.4 12.9 %collective-permute-start.8 = (bf16[64,1024]{1,0:T(8,128)(2,1)S(1)}, bf16[64,1024]{1,0:T(8,128)(2,1)S(1)}, u32[]{:S(2)}, u32[]{:S(2)}) collective-permute-start(bf16[64,1024]{1,0:T(8,128)(2,1)S(1)} %get-tuple-element.66.refs_0_), channel_id=1, source_target_pairs={{0,16},{8,24},{16,0},{24,8},{1,17},{9,25},{17,1},{25,9},{2,18},{10... | collective-permute-start | bytes 393224 | tf_op jit(solution)/shard_map/ppermute | solution.py:411
  43.0 11.2 %collective-permute-start.7 = (bf16[64,1024]{1,0:T(8,128)(2,1)S(1)}, bf16[64,1024]{1,0:T(8,128)(2,1)S(1)}, u32[]{:S(2)}, u32[]{:S(2)}) collective-permute-start(bf16[64,1024]{1,0:T(8,128)(2,1)S(1)} %get-tuple-element.66.refs_0_), channel_id=1, source_target_pairs={{0,8},{8,0},{16,24},{24,16},{1,9},{9,1},{17,25},{25,17},{2,10},{10... | collective-permute-start | bytes 393224 | tf_op jit(solution)/shard_map/ppermute | solution.py:411
  47.9 13.5 %collective-permute-start.24 = (bf16[64,1024]{1,0:T(8,128)(2,1)S(1)}, bf16[64,1024]{1,0:T(8,128)(2,1)S(1)}, u32[]{:S(2)}, u32[]{:S(2)}) collective-permute-start(bf16[64,1024]{1,0:T(8,128)(2,1)S(1)} %get-tuple-element.89.refs_0_), channel_id=1, source_target_pairs={{0,24},{8,16},{16,8},{24,0},{1,25},{9,17},{17,9},{25,1},{2,26},{10... | collective-permute-start | bytes 393224 | tf_op jit(solution)/shard_map/ppermute | solution.py:411
  49.5 13.2 %collective-permute-start.23 = (bf16[64,1024]{1,0:T(8,128)(2,1)S(1)}, bf16[64,1024]{1,0:T(8,128)(2,1)S(1)}, u32[]{:S(2)}, u32[]{:S(2)}) collective-permute-start(bf16[64,1024]{1,0:T(8,128)(2,1)S(1)} %get-tuple-element.89.refs_0_), channel_id=1, source_target_pairs={{0,16},{8,24},{16,0},{24,8},{1,17},{9,25},{17,1},{25,9},{2,18},{10... | collective-permute-start | bytes 393224 | tf_op jit(solution)/shard_map/ppermute | solution.py:411
  66.1 10.1 %collective-permute-start.26 = (bf16[64,1024]{1,0:T(8,128)(2,1)S(1)}, bf16[64,1024]{1,0:T(8,128)(2,1)S(1)}, u32[]{:S(2)}, u32[]{:S(2)}) collective-permute-start(bf16[64,1024]{1,0:T(8,128)(2,1)S(1)} %get-tuple-element.92), channel_id=1, source_target_pairs={{0,16},{8,24},{16,0},{24,8},{1,17},{9,25},{17,1},{25,9},{2,18},{10... | collective-permute-start | bytes 393224 | tf_op jit(solution)/shard_map/ppermute | solution.py:411
  69.9 10.4 %collective-permute-start.15 = (bf16[64,1024]{1,0:T(8,128)(2,1)S(1)}, bf16[64,1024]{1,0:T(8,128)(2,1)S(1)}, u32[]{:S(2)}, u32[]{:S(2)}) collective-permute-start(bf16[64,1024]{1,0:T(8,128)(2,1)S(1)} %get-tuple-element.73.refs_0_), channel_id=1, source_target_pairs={{0,24},{8,16},{16,8},{24,0},{1,25},{9,17},{17,9},{25,1},{2,26},{10... | collective-permute-start | bytes 393224 | tf_op jit(solution)/shard_map/ppermute | solution.py:411
  73.4 12.0 %collective-permute-start.14 = (bf16[64,1024]{1,0:T(8,128)(2,1)S(1)}, bf16[64,1024]{1,0:T(8,128)(2,1)S(1)}, u32[]{:S(2)}, u32[]{:S(2)}) collective-permute-start(bf16[64,1024]{1,0:T(8,128)(2,1)S(1)} %get-tuple-element.73.refs_0_), channel_id=1, source_target_pairs={{0,16},{8,24},{16,0},{24,8},{1,17},{9,25},{17,1},{25,9},{2,18},{10... | collective-permute-start | bytes 393224 | tf_op jit(solution)/shard_map/ppermute | solution.py:411
  73.4 12.0 %collective-permute-start.13 = (bf16[64,1024]{1,0:T(8,128)(2,1)S(1)}, bf16[64,1024]{1,0:T(8,128)(2,1)S(1)}, u32[]{:S(2)}, u32[]{:S(2)}) collective-permute-start(bf16[64,1024]{1,0:T(8,128)(2,1)S(1)} %get-tuple-element.73.refs_0_), channel_id=1, source_target_pairs={{0,8},{8,0},{16,24},{24,16},{1,9},{9,1},{17,25},{25,17},{2,10},{10... | collective-permute-start | bytes 393224 | tf_op jit(solution)/shard_map/ppermute | solution.py:411
  76.3 13.6 %collective-permute-start.30 = (bf16[64,1024]{1,0:T(8,128)(2,1)S(1)}, bf16[64,1024]{1,0:T(8,128)(2,1)S(1)}, u32[]{:S(2)}, u32[]{:S(2)}) collective-permute-start(bf16[64,1024]{1,0:T(8,128)(2,1)S(1)} %get-tuple-element.95.refs_0_), channel_id=1, source_target_pairs={{0,24},{8,16},{16,8},{24,0},{1,25},{9,17},{17,9},{25,1},{2,26},{10... | collective-permute-start | bytes 393224 | tf_op jit(solution)/shard_map/ppermute | solution.py:411
  79.9 10.5 %collective-permute-start.29 = (bf16[64,1024]{1,0:T(8,128)(2,1)S(1)}, bf16[64,1024]{1,0:T(8,128)(2,1)S(1)}, u32[]{:S(2)}, u32[]{:S(2)}) collective-permute-start(bf16[64,1024]{1,0:T(8,128)(2,1)S(1)} %get-tuple-element.95.refs_0_), channel_id=1, source_target_pairs={{0,16},{8,24},{16,0},{24,8},{1,17},{9,25},{17,1},{25,9},{2,18},{10... | collective-permute-start | bytes 393224 | tf_op jit(solution)/shard_map/ppermute | solution.py:411
  80.3 10.1 %collective-permute-start.28 = (bf16[64,1024]{1,0:T(8,128)(2,1)S(1)}, bf16[64,1024]{1,0:T(8,128)(2,1)S(1)}, u32[]{:S(2)}, u32[]{:S(2)}) collective-permute-start(bf16[64,1024]{1,0:T(8,128)(2,1)S(1)} %get-tuple-element.95.refs_0_), channel_id=1, source_target_pairs={{0,8},{8,0},{16,24},{24,16},{1,9},{9,1},{17,25},{25,17},{2,10},{10... | collective-permute-start | bytes 393224 | tf_op jit(solution)/shard_map/ppermute | solution.py:411
  93.4 11.5 %collective-permute-start.32 = (bf16[64,1024]{1,0:T(8,128)(2,1)S(1)}, bf16[64,1024]{1,0:T(8,128)(2,1)S(1)}, u32[]{:S(2)}, u32[]{:S(2)}) collective-permute-start(bf16[64,1024]{1,0:T(8,128)(2,1)S(1)} %get-tuple-element.98), channel_id=1, source_target_pairs={{0,16},{8,24},{16,0},{24,8},{1,17},{9,25},{17,1},{25,9},{2,18},{10... | collective-permute-start | bytes 393224 | tf_op jit(solution)/shard_map/ppermute | solution.py:411
  94.9 10.0 %collective-permute-start.33 = (bf16[64,1024]{1,0:T(8,128)(2,1)S(1)}, bf16[64,1024]{1,0:T(8,128)(2,1)S(1)}, u32[]{:S(2)}, u32[]{:S(2)}) collective-permute-start(bf16[64,1024]{1,0:T(8,128)(2,1)S(1)} %get-tuple-element.99), channel_id=1, source_target_pairs={{0,24},{8,16},{16,8},{24,0},{1,25},{9,17},{17,9},{25,1},{2,26},{10... | collective-permute-start | bytes 393224 | tf_op jit(solution)/shard_map/ppermute | solution.py:411
  97.4 10.2 %collective-permute-start.39 = (bf16[64,1024]{1,0:T(8,128)(2,1)S(1)}, bf16[64,1024]{1,0:T(8,128)(2,1)S(1)}, u32[]{:S(2)}, u32[]{:S(2)}) collective-permute-start(bf16[64,1024]{1,0:T(8,128)(2,1)S(1)} %get-tuple-element.103.refs_0_), channel_id=1, source_target_pairs={{0,24},{8,16},{16,8},{24,0},{1,25},{9,17},{17,9},{25,1},{2,26},{10... | collective-permute-start | bytes 393224 | tf_op jit(solution)/shard_map/ppermute | solution.py:411
  98.7 11.0 %collective-permute-start.38 = (bf16[64,1024]{1,0:T(8,128)(2,1)S(1)}, bf16[64,1024]{1,0:T(8,128)(2,1)S(1)}, u32[]{:S(2)}, u32[]{:S(2)}) collective-permute-start(bf16[64,1024]{1,0:T(8,128)(2,1)S(1)} %get-tuple-element.103.refs_0_), channel_id=1, source_target_pairs={{0,16},{8,24},{16,0},{24,8},{1,17},{9,25},{17,1},{25,9},{2,18},{10... | collective-permute-start | bytes 393224 | tf_op jit(solution)/shard_map/ppermute | solution.py:411
  (34 other events, 251.1 us)
Sparse Core Ops, SparseCore 0:
  9.9 35.4 all-gather.6
  47.5 35.1 all-gather.8
  84.4 23.9 all-gather.10

commit v5 on v4

--- a/solution.py
+++ b/solution.py
@@ -237,28 +237,18 @@
     )(own, *others, gain.reshape(1, -1))
 
 
-def cross_kernel(ways, orders, first, length_ref, cache_ref, stream_ref, *refs):
+def cross_kernel(ways, first, length_ref, cache_ref, stream_ref, *refs):
     blocks = refs[:ways]
-    given = refs[ways : -(ways + 2)]
-    own_ref = refs[-(ways + 2)]
-    out_refs = refs[-(ways + 1) : -2]
-    wq_ref, ctx_ref = refs[-2:]
+    given = refs[ways : -(ways + 1)]
+    own_ref = refs[-(ways + 1)]
+    out_refs = refs[-ways:-1]
+    ctx_ref = refs[-1]
+    wq_ref, wo_ref = given
     requests = cache_ref.shape[0]
     width = wq_ref.shape[1]
     heads = width // DH
     rows = blocks[0].shape[0]
     share = rows // requests
-    wo_ref = given[-1]
-    if orders:
-        pieces, _, lanes = given[0].shape
-        for k in range(pieces):
-            piece = given[0].at[jnp.bitwise_xor(lax.axis_index("tok"), k)]
-            for c in range(width // lanes):
-                here = slice(c * lanes, (c + 1) * lanes)
-                block = piece[c * lanes : (c + 1) * lanes, :]
-                wq_ref[k * lanes : (k + 1) * lanes, here] = block
-    else:
-        wq_ref[...] = given[0][...]
     normed = jnp.concatenate([block[...] for block in blocks], axis=0)
     query = dot(normed, wq_ref[...]).astype(BF16).reshape(ways, rows, width)
     position = lax.broadcasted_iota(jnp.int32, (1, cache_ref.shape[2]), 1)
@@ -278,13 +268,13 @@
         out_refs[k - 1][...] = part[k * rows : (k + 1) * rows].astype(BF16)
 
 
-def cross_layer(blocks, weights, orders, cache, stream, length, first, count):
+def cross_layer(blocks, weights, cache, stream, length, first, count):
     ways = len(blocks)
     rows, model = blocks[0].shape
     depth, width = cache.shape[2:]
     full = lambda shape: pl.BlockSpec(shape, lambda i: (0,) * len(shape))
     return pl.pallas_call(
-        functools.partial(cross_kernel, ways, orders, first),
+        functools.partial(cross_kernel, ways, first),
         grid=(1,),
         out_shape=[jax.ShapeDtypeStruct((rows, model), F32)]
         + [jax.ShapeDtypeStruct((rows, model), BF16)] * (ways - 1),
@@ -297,7 +287,6 @@
         + [full(weight.shape) for weight in weights],
         out_specs=[full((rows, model))] * ways,
         scratch_shapes=[
-            pltpu.VMEM((model, width), BF16),
             pltpu.VMEM((ways, rows, width), BF16),
         ],
         compiler_params=params(CROSS_LIMIT),
@@ -306,24 +295,34 @@
     )(length, cache, stream, *blocks, *weights)
 
 
-def join_kernel(slices_ref, *out_refs):
+def join_kernel(query, slices_ref, *out_refs):
     pieces, _, lanes = slices_ref.shape
     for k in range(pieces):
         source = jnp.bitwise_xor(lax.axis_index("tok"), k)
-        at = slices_ref.shape[1] - sum(ref.shape[0] for ref in out_refs)
-        for out_ref in out_refs:
-            rows = out_ref.shape[0]
-            out_ref[:, k * lanes : (k + 1) * lanes] = slices_ref[source, at : at + rows, :]
-            at += rows
-
-
-def join(slices, *depths):
+        at = 0
+        for n, out_ref in enumerate(out_refs):
+            if query and n == 0:
+                for c in range(out_ref.shape[1] // lanes):
+                    block = slices_ref[source, at : at + lanes, :]
+                    here = slice(c * lanes, (c + 1) * lanes)
+                    out_ref[k * lanes : (k + 1) * lanes, here] = block
+                    at += lanes
+            else:
+                rows = out_ref.shape[0]
+                out_ref[:, k * lanes : (k + 1) * lanes] = slices_ref[source, at : at + rows, :]
+                at += rows
+
+
+def join(slices, query, *depths):
     pieces, rows, lanes = slices.shape
-    return pl.pallas_call(
-        join_kernel,
-        out_shape=[jax.ShapeDtypeStruct((depth, lanes * pieces), BF16) for depth in depths],
+    shapes = [(depth, lanes * pieces) for depth in depths]
+    if query:
+        shapes = [(lanes * pieces, query)] + shapes
+    return pl.pallas_call(
+        functools.partial(join_kernel, query),
+        out_shape=[jax.ShapeDtypeStruct(shape, BF16) for shape in shapes],
         in_specs=[VMEM],
-        out_specs=[VMEM] * len(depths),
+        out_specs=[VMEM] * len(shapes),
         compiler_params=params(),
         cost_estimate=cost(1e3, 4 * rows * lanes * pieces),
         name="join",
@@ -413,6 +412,37 @@
 
 def all_slices(shard):
     return lax.all_gather(shard, "tok", axis=0, tiled=False)
+
+
+def pack_kernel(query_ref, *refs):
+    early_ref, late_ref = refs[-2:]
+    lanes = early_ref.shape[1]
+    at = 0
+    for c in range(query_ref.shape[1] // lanes):
+        early_ref[at : at + lanes, :] = query_ref[:, c * lanes : (c + 1) * lanes]
+        at += lanes
+    for ref in refs[:2]:
+        early_ref[at : at + ref.shape[0], :] = ref[...]
+        at += ref.shape[0]
+    at = 0
+    for ref in refs[2:4]:
+        late_ref[at : at + ref.shape[0], :] = ref[...]
+        at += ref.shape[0]
+
+
+def pack(query, out, w_gate, w_up, w_down):
+    lanes = out.shape[1]
+    early = query.size // lanes + out.shape[0] + w_gate.shape[1]
+    late = w_up.shape[1] + w_down.shape[0]
+    return pl.pallas_call(
+        pack_kernel,
+        out_shape=[jax.ShapeDtypeStruct((rows, lanes), BF16) for rows in (early, late)],
+        in_specs=[VMEM] * 5,
+        out_specs=[VMEM] * 2,
+        compiler_params=params(60),
+        cost_estimate=cost(1e3, 2e6),
+        name="pack",
+    )(query, out, w_gate.T, w_up.T, w_down)
 
 
 def along(value, k):
@@ -462,21 +492,21 @@
     bias = bias_and_mask(parents, counts, buckets, bias_table)
     ctx = self_attention(draft_qkv, self_cache, self_len, bias)
     if paired:
-        pieces, orders, cross_orders = total, ATTN_ORDERS, ATTN_ORDERS
-        query_slices = jnp.split(w_query_cross, head_width // slice_lanes, axis=1)
-        early = all_slices(jnp.concatenate(query_slices + [w_out_cross, w_gate.T], axis=0))
+        pieces, orders = total, ATTN_ORDERS
+        early, late = pack(w_query_cross, w_out_cross, w_gate, w_up, w_down)
+        early = all_slices(early)
         out_shard = w_out_self
         out_here = [out_shard] + [along(out_shard, k) for k in (4, 6, 2)]
         ctx, out_here = gate(ctx, out_here)
         out_here = jnp.stack(out_here)
         out_w = [out_here, along(out_here, 1)]
-        out_here, w_up, w_down, qkv_shard = gate(out_here, w_up, w_down, qkv_shard)
-        late = all_slices(jnp.concatenate([w_up.T, w_down], axis=0))
+        out_here, late, qkv_shard = gate(out_here, late, qkv_shard)
+        late = all_slices(late)
     else:
         pieces = 1
         by_row = functools.partial(lax.all_gather, axis_name="tok", axis=0, tiled=True)
         by_col = functools.partial(lax.all_gather, axis_name="tok", axis=1, tiled=True)
-        out_w, orders, cross_orders = [by_col(w_out_self)[None]], ((0,),), ()
+        out_w, orders = [by_col(w_out_self)[None]], ((0,),)
         attn_w = [by_row(w_query_cross), by_col(w_out_cross)]
         ffn_gate = by_row(w_gate).T
         ffn_late = jnp.concatenate([by_row(w_up).T, by_col(w_down)], axis=0)
@@ -489,11 +519,11 @@
     kept = [norm(made[h][0], sent[h], gain_cross, pieces) for h in halves]
     blocks = [spread(kept[h][1], ways) for h in halves]
     if paired:
-        out_cross, ffn_gate = join(early, head_width, w_gate.shape[1])
-        attn_w = [early[:, :head_width], out_cross]
+        query, out_cross, ffn_gate = join(early, head_width, head_width, w_gate.shape[1])
+        attn_w = [query, out_cross]
     made = [
         cross_layer(
-            blocks[h], attn_w, cross_orders, cross_cache, kept[h][0], enc_len, starts[h], count
+            blocks[h], attn_w, cross_cache, kept[h][0], enc_len, starts[h], count
         )
         for h in halves
     ]
@@ -501,7 +531,7 @@
     kept = [norm(made[h][0], sent[h], gain_ffn, pieces) for h in halves]
     blocks = [spread(kept[h][1], ways) for h in halves]
     if paired:
-        (ffn_late,) = join(late, w_up.shape[1] + w_down.shape[0])
+        (ffn_late,) = join(late, 0, w_up.shape[1] + w_down.shape[0])
     made = [ffn(blocks[h], ffn_gate, ffn_late, kept[h][0]) for h in halves]
     sent = [send_each(made[h][1:], ways) for h in halves]
     kept = [norm(made[h][0], sent[h], gain_next, pieces, True) for h in halves]

time: 122 us -> 121 us (level)
  other arithmetic: 3.24 us -> 0.76 us
  Pallas kernels: 22.8 us -> 24.9 us
  waiting for transfers between devices: 18.2 us -> 19.5 us
    all_gather x3, waiting for transfers between devices: 2.2 us -> 6.38 us  [all_slices(): return lax.all_gather(shard, 'tok', axis=0, tiled=False)]
    ppermute x40, waiting for transfers between devices: 16 us -> 13.1 us  [partner(): return lax.ppermute(value, axis, [(i, i ^ k) for i in range(size)])]
    concatenate x2 -> x0, other arithmetic: 2.48 us -> none  [the longest x1 1.72 us: shards(): jnp.concatenate(query_slices + [w_out_cross, w_gate.T], axis=0)]
    pallas_call x4 -> x5, Pallas kernels: 6.31 us -> 8.4 us  [the longest x2 4.91 us: cross_layer(): pl.pallas_call(functools.partial(cross_kernel, ways, first), grid=(1,), o...]
    ppermute x40, starting transfers between devices: 53.6 us -> 52.4 us  [partner(): return lax.ppermute(value, axis, [(i, i ^ k) for i in range(size)])]
    unnamed x30 -> x26, local copies, waits for them, and re-layouts: 8.26 us -> 9.19 us
  transfers between devices with their start and end apart: 43 -> 43, of which waited for: 12 -> 15; matrix products, arithmetic and copies ran while one was open for 1% -> 1% of each run, Pallas kernels for 18% -> 18%
where the time goes in v5:
time: 121 us
  starting transfers between devices  52.7 us (44%)
  Pallas kernels  24.9 us (21%)
  waiting for transfers between devices  19.5 us (16%)
  between operations  14 us (12%)
  local copies, waits for them, and re-layouts  9.19 us (8%)
    ppermute x40, starting transfers between devices, partner(): return lax.ppermute(value, axis, [(i, i ^ k) for i in range(size)])  52.4 us
    ppermute x40, waiting for transfers between devices, partner(): return lax.ppermute(value, axis, [(i, i ^ k) for i in range(size)])  13.1 us
    unnamed x26, local copies, waits for them, and re-layouts  9.19 us
    all_gather x3, waiting for transfers between devices, all_slices(): return lax.all_gather(shard, 'tok', axis=0, tiled=False)  6.38 us
    pallas_call x1, Pallas kernels, self_attention(): pl.pallas_call(self_kernel, grid=(HALVES,), out_shape=jax.ShapeDtypeStruc...  6.01 us
    pallas_call x2, Pallas kernels, cross_layer(): pl.pallas_call(functools.partial(cross_kernel, ways, first), grid=(1,), o...  4.91 us
    pallas_call x1, Pallas kernels, bias_and_mask(): pl.pallas_call(bias_kernel, out_shape=jax.ShapeDtypeStruct((requests, hea...  3.28 us
    pallas_call x2, Pallas kernels, ffn(): pl.pallas_call(functools.partial(ffn_kernel, ways), out_shape=[jax.ShapeD...  2.84 us
  transfers between devices with their start and end apart: 43, of which 15 were waited for; matrix products, arithmetic and copies ran while one was open for 1% of the time, Pallas kernels for 18%

profile of v5, /device:TPU:0, one launch (start us, length us, event | category | flops | bytes accessed | tf_op | source)
XLA Modules:
  0.0 121.1 jit_solution(9945118927903761804)
XLA Ops:
  7.2 2.0 %pack.1 = (bf16[1216,128]{1,0:T(8,128)(2,1)}, bf16[1408,128]{1,0:T(8,128)(2,1)}) custom-call(bf16[128,256]{1,0:T(8,128)(2,1)} %query_ref.1, bf16[256,128]{1,0:T(8,128)(2,1)} %refs_0_.1, bf16[704,128]{1,0:T(8,128)(2,1)} %bitcast.27, bf16[704,128]{1,0:T(8,128)(2,1)} %bitcast.28, bf16[704,128]{1,0:T(8,128)(2,1)} %refs_3_.3), custom_call_target="tpu_custom_call" | custom-call | flops 1000 | bytes 2000000 | tf_op jit(solution)/shard_map/pack/pallas_call | solution.py:437
  9.3 4.1 %collective-permute-start = (bf16[256,128]{1,0:T(8,128)(2,1)}, bf16[256,128]{1,0:T(8,128)(2,1)S(1)}, u32[]{:S(2)}, u32[]{:S(2)}) collective-permute-start(bf16[256,128]{1,0:T(8,128)(2,1)} %param.33), channel_id=1, source_target_pairs={{0,4},{1,5},{2,6},{3,7},{4,0},{5,1},{6,2},{7,3},{8,12},{9,13},{10,... | collective-permute-start | bytes 196616 | tf_op jit(solution)/shard_map/ppermute | solution.py:410
  15.0 3.3 %bias_and_mask.1.bias_ref = f32[8,256,64]{2,1,0:T(8,128)} custom-call(s32[8,64]{1,0:T(8,128)} %parents_ref.1, s32[8]{0:T(128)} %counts_ref.1, s32[8,64,64]{2,1,0:T(8,128)} %buckets_ref.1, f32[4,32]{1,0:T(4,128)} %bitcast.33), custom_call_target="tpu_custom_call" | custom-call | flops 60000000 | bytes 1200000 | tf_op jit(solution)/shard_map/bias_and_mask/pallas_call | solution.py:97
  18.3 6.0 %self_attention.1.refs_2_ = bf16[8,64,256]{2,1,0:T(8,128)(2,1)} custom-call(s32[8]{0:T(128)} %length_ref.3, bf16[3,8,64,256]{3,2,1,0:T(8,128)(2,1)} %qkv_ref.1, bf16[8,2,512,256]{3,2,1,0:T(8,128)(2,1)} %cache_ref.3, f32[8,256,64]{2,1,0:T(8,128)} %bias_and_mask.1.bias_ref), custom_call_target="tpu_custom_call" | custom-call | flops 5000000000 | bytes 6000000 | tf_op jit(solution)/shard_map/self_attention/pallas_call | solution.py:131
  24.7 1.5 %collective-permute-done.3.refs_1_ = bf16[4,256,128]{2,1,0:T(8,128)(2,1)S(1)} collective-permute-done((bf16[4,256,128]{2,1,0:T(8,128)(2,1)S(1)}, bf16[4,256,128]{2,1,0:T(8,128)(2,1)S(1)}, u32[]{:S(2)}, u32[]{:S(2)}) %collective-permute-start.3) | collective-permute-done | bytes 262176 | tf_op jit(solution)/shard_map/ppermute | solution.py:410
  28.9 1.5 %collective-permute-start.4 = (bf16[64,1024]{1,0:T(8,128)(2,1)S(1)}, bf16[64,1024]{1,0:T(8,128)(2,1)S(1)}, u32[]{:S(2)}, u32[]{:S(2)}) collective-permute-start(bf16[64,1024]{1,0:T(8,128)(2,1)S(1)} %get-tuple-element.65), channel_id=1, source_target_pairs={{0,8},{8,0},{16,24},{24,16},{1,9},{9,1},{17,25},{25,17},{2,10},{10... | collective-permute-start | bytes 393224 | tf_op jit(solution)/shard_map/ppermute | solution.py:410
  30.5 1.5 %collective-permute-start.5 = (bf16[64,1024]{1,0:T(8,128)(2,1)S(1)}, bf16[64,1024]{1,0:T(8,128)(2,1)S(1)}, u32[]{:S(2)}, u32[]{:S(2)}) collective-permute-start(bf16[64,1024]{1,0:T(8,128)(2,1)S(1)} %get-tuple-element.66), channel_id=1, source_target_pairs={{0,16},{8,24},{16,0},{24,8},{1,17},{9,25},{17,1},{25,9},{2,18},{10... | collective-permute-start | bytes 393224 | tf_op jit(solution)/shard_map/ppermute | solution.py:410
  32.5 1.5 %collective-permute-start.19 = (bf16[64,1024]{1,0:T(8,128)(2,1)S(1)}, bf16[64,1024]{1,0:T(8,128)(2,1)S(1)}, u32[]{:S(2)}, u32[]{:S(2)}) collective-permute-start(bf16[64,1024]{1,0:T(8,128)(2,1)S(1)} %get-tuple-element.89), channel_id=1, source_target_pairs={{0,8},{8,0},{16,24},{24,16},{1,9},{9,1},{17,25},{25,17},{2,10},{10... | collective-permute-start | bytes 393224 | tf_op jit(solution)/shard_map/ppermute | solution.py:410
  34.0 1.5 %collective-permute-start.20 = (bf16[64,1024]{1,0:T(8,128)(2,1)S(1)}, bf16[64,1024]{1,0:T(8,128)(2,1)S(1)}, u32[]{:S(2)}, u32[]{:S(2)}) collective-permute-start(bf16[64,1024]{1,0:T(8,128)(2,1)S(1)} %get-tuple-element.90), channel_id=1, source_target_pairs={{0,16},{8,24},{16,0},{24,8},{1,17},{9,25},{17,1},{25,9},{2,18},{10... | collective-permute-start | bytes 393224 | tf_op jit(solution)/shard_map/ppermute | solution.py:410
  35.5 2.3 %collective-permute-start.21 = (bf16[64,1024]{1,0:T(8,128)(2,1)S(1)}, bf16[64,1024]{1,0:T(8,128)(2,1)S(1)}, u32[]{:S(2)}, u32[]{:S(2)}) collective-permute-start(bf16[64,1024]{1,0:T(8,128)(2,1)S(1)} %get-tuple-element.91), channel_id=1, source_target_pairs={{0,24},{8,16},{16,8},{24,0},{1,25},{9,17},{17,9},{25,1},{2,26},{10... | collective-permute-start | bytes 393224 | tf_op jit(solution)/shard_map/ppermute | solution.py:410
  47.7 1.7 %copy-done.2 = bf16[9728,128]{1,0:T(8,128)(2,1)S(1)} copy-done((bf16[9728,128]{1,0:T(8,128)(2,1)S(1)}, bf16[9728,128]{1,0:T(8,128)(2,1)}, u32[]{:S(2)}) %copy-start.2) | copy-done | bytes 2490392
  51.5 2.3 %copy-done.9 = bf16[8,2,512,256]{3,2,1,0:T(8,128)(2,1)S(1)} copy-done((bf16[8,2,512,256]{3,2,1,0:T(8,128)(2,1)S(1)}, bf16[8,2,512,256]{3,2,1,0:T(8,128)(2,1)}, u32[]{:S(2)}) %copy-start.9) | copy-done | bytes 4194328
  53.9 2.4 %cross_layer.2 = (f32[64,1024]{1,0:T(8,128)S(1)}, bf16[64,1024]{1,0:T(8,128)(2,1)S(1)}, bf16[64,1024]{1,0:T(8,128)(2,1)S(1)}, bf16[64,1024]{1,0:T(8,128)(2,1)S(1)}) custom-call(s32[8]{0:T(128)S(1)} %copy-done.11, bf16[8,2,512,256]{3,2,1,0:T(8,128)(2,1)S(1)} %copy-done.9, f32[64,1024]{1,0:T(8,128)S(1)} %get-tuple-element.68.stream_ref, ...), custom_call_target="tpu_custom_call" | custom-call | flops 2500000000 | bytes 4000000 | tf_op jit(solution)/shard_map/cross_layer/pallas_call | solution.py:276
  59.9 2.5 %cross_layer.3 = (f32[64,1024]{1,0:T(8,128)S(1)}, bf16[64,1024]{1,0:T(8,128)(2,1)S(1)}, bf16[64,1024]{1,0:T(8,128)(2,1)S(1)}, bf16[64,1024]{1,0:T(8,128)(2,1)S(1)}) custom-call(s32[8]{0:T(128)S(1)} %copy-done.11, bf16[8,2,512,256]{3,2,1,0:T(8,128)(2,1)S(1)} %copy-done.10, f32[64,1024]{1,0:T(8,128)S(1)} %get-tuple-element.92.stream_ref, ...), custom_call_target="tpu_custom_call" | custom-call | flops 2500000000 | bytes 4000000 | tf_op jit(solution)/shard_map/cross_layer/pallas_call | solution.py:276
  67.8 1.5 %collective-permute-start.14 = (bf16[64,1024]{1,0:T(8,128)(2,1)S(1)}, bf16[64,1024]{1,0:T(8,128)(2,1)S(1)}, u32[]{:S(2)}, u32[]{:S(2)}) collective-permute-start(bf16[64,1024]{1,0:T(8,128)(2,1)S(1)} %get-tuple-element.77.refs_0_), channel_id=1, source_target_pairs={{0,16},{8,24},{16,0},{24,8},{1,17},{9,25},{17,1},{25,9},{2,18},{10... | collective-permute-start | bytes 393224 | tf_op jit(solution)/shard_map/ppermute | solution.py:410
  70.5 2.7 %collective-permute-done.27.refs_2_ = bf16[64,1024]{1,0:T(8,128)(2,1)S(1)} collective-permute-done((bf16[64,1024]{1,0:T(8,128)(2,1)S(1)}, bf16[64,1024]{1,0:T(8,128)(2,1)S(1)}, u32[]{:S(2)}, u32[]{:S(2)}) %collective-permute-start.27) | collective-permute-done | bytes 131104 | tf_op jit(solution)/shard_map/ppermute | solution.py:410
  74.1 1.9 %collective-permute-start.29 = (bf16[64,1024]{1,0:T(8,128)(2,1)S(1)}, bf16[64,1024]{1,0:T(8,128)(2,1)S(1)}, u32[]{:S(2)}, u32[]{:S(2)}) collective-permute-start(bf16[64,1024]{1,0:T(8,128)(2,1)S(1)} %get-tuple-element.99.refs_0_), channel_id=1, source_target_pairs={{0,16},{8,24},{16,0},{24,8},{1,17},{9,25},{17,1},{25,9},{2,18},{10... | collective-permute-start | bytes 393224 | tf_op jit(solution)/shard_map/ppermute | solution.py:410
  76.9 5.6 %all-gather.9.cloned.1.call-done = bf16[11264,128]{1,0:T(8,128)(2,1)} async-done(((bf16[1408,128]{1,0:T(8,128)(2,1)}), bf16[11264,128]{1,0:T(8,128)(2,1)}) %all-gather.9.cloned.1.call-update) | async-done | bytes 2883600 | tf_op jit(solution)/shard_map/all_gather | solution.py:414
  82.5 1.8 %copy-done.1 = bf16[11264,128]{1,0:T(8,128)(2,1)S(1)} copy-done((bf16[11264,128]{1,0:T(8,128)(2,1)S(1)}, bf16[11264,128]{1,0:T(8,128)(2,1)}, u32[]{:S(2)}) %copy-start.1) | copy-done | bytes 2883608
  86.6 1.5 %collective-permute-start.16 = (bf16[64,1024]{1,0:T(8,128)(2,1)S(1)}, bf16[64,1024]{1,0:T(8,128)(2,1)S(1)}, u32[]{:S(2)}, u32[]{:S(2)}) collective-permute-start(bf16[64,1024]{1,0:T(8,128)(2,1)S(1)} %get-tuple-element.79), channel_id=1, source_target_pairs={{0,8},{8,0},{16,24},{24,16},{1,9},{9,1},{17,25},{25,17},{2,10},{10... | collective-permute-start | bytes 393224 | tf_op jit(solution)/shard_map/ppermute | solution.py:410
  91.6 1.5 %collective-permute-start.31 = (bf16[64,1024]{1,0:T(8,128)(2,1)S(1)}, bf16[64,1024]{1,0:T(8,128)(2,1)S(1)}, u32[]{:S(2)}, u32[]{:S(2)}) collective-permute-start(bf16[64,1024]{1,0:T(8,128)(2,1)S(1)} %get-tuple-element.101), channel_id=1, source_target_pairs={{0,8},{8,0},{16,24},{24,16},{1,9},{9,1},{17,25},{25,17},{2,10},{10... | collective-permute-start | bytes 393224 | tf_op jit(solution)/shard_map/ppermute | solution.py:410
  99.1 2.0 %collective-permute-start.39 = (bf16[64,1024]{1,0:T(8,128)(2,1)S(1)}, bf16[64,1024]{1,0:T(8,128)(2,1)S(1)}, u32[]{:S(2)}, u32[]{:S(2)}) collective-permute-start(bf16[64,1024]{1,0:T(8,128)(2,1)S(1)} %get-tuple-element.107.refs_0_), channel_id=1, source_target_pairs={{0,24},{8,16},{16,8},{24,0},{1,25},{9,17},{17,9},{25,1},{2,26},{10... | collective-permute-start | bytes 393224 | tf_op jit(solution)/shard_map/ppermute | solution.py:410
  104.7 2.0 %collective-permute-start.36 = (bf16[64,1024]{1,0:T(8,128)(2,1)S(1)}, bf16[64,1024]{1,0:T(8,128)(2,1)S(1)}, u32[]{:S(2)}, u32[]{:S(2)}) collective-permute-start(bf16[64,1024]{1,0:T(8,128)(2,1)S(1)} %get-tuple-element.106.refs_0_), channel_id=1, source_target_pairs={{0,24},{8,16},{16,8},{24,0},{1,25},{9,17},{17,9},{25,1},{2,26},{10... | collective-permute-start | bytes 393224 | tf_op jit(solution)/shard_map/ppermute | solution.py:410
  111.1 2.1 %collective-permute-done.35.refs_2_ = bf16[64,1024]{1,0:T(8,128)(2,1)S(1)} collective-permute-done((bf16[64,1024]{1,0:T(8,128)(2,1)S(1)}, bf16[64,1024]{1,0:T(8,128)(2,1)S(1)}, u32[]{:S(2)}, u32[]{:S(2)}) %collective-permute-start.35) | collective-permute-done | bytes 131104 | tf_op jit(solution)/shard_map/ppermute | solution.py:410
  (112 shorter events, 50.2 us)
Async XLA Ops:
  7.2 40.5 %all-gather.7.cloned.1.call-start = ((), (), s32[]{:S(2)}) async-start(), calls=%async_computation | async-start | bytes 2801664 | tf_op jit(solution)/shard_map/all_gather | solution.py:414
  9.3 73.3 %all-gather.9.cloned.1.call-start = ((), (), s32[]{:S(2)}) async-start(), calls=%async_computation.1 | async-start | bytes 3244032 | tf_op jit(solution)/shard_map/all_gather | solution.py:414
  9.3 15.0 %collective-permute-start = (bf16[256,128]{1,0:T(8,128)(2,1)}, bf16[256,128]{1,0:T(8,128)(2,1)S(1)}, u32[]{:S(2)}, u32[]{:S(2)}) collective-permute-start(bf16[256,128]{1,0:T(8,128)(2,1)} %param.33), channel_id=1, source_target_pairs={{0,4},{1,5},{2,6},{3,7},{4,0},{5,1},{6,2},{7,3},{8,12},{9,13},{10,... | collective-permute-start | bytes 196616 | tf_op jit(solution)/shard_map/ppermute | solution.py:410
  13.4 10.9 %collective-permute-start.1 = (bf16[256,128]{1,0:T(8,128)(2,1)}, bf16[256,128]{1,0:T(8,128)(2,1)S(1)}, u32[]{:S(2)}, u32[]{:S(2)}) collective-permute-start(bf16[256,128]{1,0:T(8,128)(2,1)} %param.33), channel_id=1, source_target_pairs={{0,6},{1,7},{2,4},{3,5},{4,2},{5,3},{6,0},{7,1},{8,14},{9,15},{10,... | collective-permute-start | bytes 196616 | tf_op jit(solution)/shard_map/ppermute | solution.py:410
  14.8 9.6 %collective-permute-start.2 = (bf16[256,128]{1,0:T(8,128)(2,1)}, bf16[256,128]{1,0:T(8,128)(2,1)S(1)}, u32[]{:S(2)}, u32[]{:S(2)}) collective-permute-start(bf16[256,128]{1,0:T(8,128)(2,1)} %param.33), channel_id=1, source_target_pairs={{0,2},{1,3},{2,0},{3,1},{4,6},{5,7},{6,4},{7,5},{8,10},{9,11},{10,... | collective-permute-start | bytes 196616 | tf_op jit(solution)/shard_map/ppermute | solution.py:410
  24.4 83.7 %all-gather.11.cloned.1.call-start = ((), (), s32[]{:S(2)}) async-start(), calls=%async_computation.2 | async-start | bytes 1769472 | tf_op jit(solution)/shard_map/all_gather | solution.py:414
  32.5 9.6 %collective-permute-start.19 = (bf16[64,1024]{1,0:T(8,128)(2,1)S(1)}, bf16[64,1024]{1,0:T(8,128)(2,1)S(1)}, u32[]{:S(2)}, u32[]{:S(2)}) collective-permute-start(bf16[64,1024]{1,0:T(8,128)(2,1)S(1)} %get-tuple-element.89), channel_id=1, source_target_pairs={{0,8},{8,0},{16,24},{24,16},{1,9},{9,1},{17,25},{25,17},{2,10},{10... | collective-permute-start | bytes 393224 | tf_op jit(solution)/shard_map/ppermute | solution.py:410
  34.0 10.5 %collective-permute-start.20 = (bf16[64,1024]{1,0:T(8,128)(2,1)S(1)}, bf16[64,1024]{1,0:T(8,128)(2,1)S(1)}, u32[]{:S(2)}, u32[]{:S(2)}) collective-permute-start(bf16[64,1024]{1,0:T(8,128)(2,1)S(1)} %get-tuple-element.90), channel_id=1, source_target_pairs={{0,16},{8,24},{16,0},{24,8},{1,17},{9,25},{17,1},{25,9},{2,18},{10... | collective-permute-start | bytes 393224 | tf_op jit(solution)/shard_map/ppermute | solution.py:410
  35.5 9.5 %collective-permute-start.21 = (bf16[64,1024]{1,0:T(8,128)(2,1)S(1)}, bf16[64,1024]{1,0:T(8,128)(2,1)S(1)}, u32[]{:S(2)}, u32[]{:S(2)}) collective-permute-start(bf16[64,1024]{1,0:T(8,128)(2,1)S(1)} %get-tuple-element.91), channel_id=1, source_target_pairs={{0,24},{8,16},{16,8},{24,0},{1,25},{9,17},{17,9},{25,1},{2,26},{10... | collective-permute-start | bytes 393224 | tf_op jit(solution)/shard_map/ppermute | solution.py:410
  39.5 10.5 %collective-permute-start.7 = (bf16[64,1024]{1,0:T(8,128)(2,1)S(1)}, bf16[64,1024]{1,0:T(8,128)(2,1)S(1)}, u32[]{:S(2)}, u32[]{:S(2)}) collective-permute-start(bf16[64,1024]{1,0:T(8,128)(2,1)S(1)} %get-tuple-element.69.refs_0_), channel_id=1, source_target_pairs={{0,8},{8,0},{16,24},{24,16},{1,9},{9,1},{17,25},{25,17},{2,10},{10... | collective-permute-start | bytes 393224 | tf_op jit(solution)/shard_map/ppermute | solution.py:410
  40.9 10.6 %collective-permute-start.8 = (bf16[64,1024]{1,0:T(8,128)(2,1)S(1)}, bf16[64,1024]{1,0:T(8,128)(2,1)S(1)}, u32[]{:S(2)}, u32[]{:S(2)}) collective-permute-start(bf16[64,1024]{1,0:T(8,128)(2,1)S(1)} %get-tuple-element.69.refs_0_), channel_id=1, source_target_pairs={{0,16},{8,24},{16,0},{24,8},{1,17},{9,25},{17,1},{25,9},{2,18},{10... | collective-permute-start | bytes 393224 | tf_op jit(solution)/shard_map/ppermute | solution.py:410
  42.1 9.4 %collective-permute-start.9 = (bf16[64,1024]{1,0:T(8,128)(2,1)S(1)}, bf16[64,1024]{1,0:T(8,128)(2,1)S(1)}, u32[]{:S(2)}, u32[]{:S(2)}) collective-permute-start(bf16[64,1024]{1,0:T(8,128)(2,1)S(1)} %get-tuple-element.69.refs_0_), channel_id=1, source_target_pairs={{0,24},{8,16},{16,8},{24,0},{1,25},{9,17},{17,9},{25,1},{2,26},{10... | collective-permute-start | bytes 393224 | tf_op jit(solution)/shard_map/ppermute | solution.py:410
  45.2 13.4 %collective-permute-start.22 = (bf16[64,1024]{1,0:T(8,128)(2,1)S(1)}, bf16[64,1024]{1,0:T(8,128)(2,1)S(1)}, u32[]{:S(2)}, u32[]{:S(2)}) collective-permute-start(bf16[64,1024]{1,0:T(8,128)(2,1)S(1)} %get-tuple-element.93.refs_0_), channel_id=1, source_target_pairs={{0,8},{8,0},{16,24},{24,16},{1,9},{9,1},{17,25},{25,17},{2,10},{10... | collective-permute-start | bytes 393224 | tf_op jit(solution)/shard_map/ppermute | solution.py:410
  46.5 13.4 %collective-permute-start.23 = (bf16[64,1024]{1,0:T(8,128)(2,1)S(1)}, bf16[64,1024]{1,0:T(8,128)(2,1)S(1)}, u32[]{:S(2)}, u32[]{:S(2)}) collective-permute-start(bf16[64,1024]{1,0:T(8,128)(2,1)S(1)} %get-tuple-element.93.refs_0_), channel_id=1, source_target_pairs={{0,16},{8,24},{16,0},{24,8},{1,17},{9,25},{17,1},{25,9},{2,18},{10... | collective-permute-start | bytes 393224 | tf_op jit(solution)/shard_map/ppermute | solution.py:410
  50.1 9.8 %collective-permute-start.24 = (bf16[64,1024]{1,0:T(8,128)(2,1)S(1)}, bf16[64,1024]{1,0:T(8,128)(2,1)S(1)}, u32[]{:S(2)}, u32[]{:S(2)}) collective-permute-start(bf16[64,1024]{1,0:T(8,128)(2,1)S(1)} %get-tuple-element.93.refs_0_), channel_id=1, source_target_pairs={{0,24},{8,16},{16,8},{24,0},{1,25},{9,17},{17,9},{25,1},{2,26},{10... | collective-permute-start | bytes 393224 | tf_op jit(solution)/shard_map/ppermute | solution.py:410
  66.3 9.7 %collective-permute-start.13 = (bf16[64,1024]{1,0:T(8,128)(2,1)S(1)}, bf16[64,1024]{1,0:T(8,128)(2,1)S(1)}, u32[]{:S(2)}, u32[]{:S(2)}) collective-permute-start(bf16[64,1024]{1,0:T(8,128)(2,1)S(1)} %get-tuple-element.77.refs_0_), channel_id=1, source_target_pairs={{0,8},{8,0},{16,24},{24,16},{1,9},{9,1},{17,25},{25,17},{2,10},{10... | collective-permute-start | bytes 393224 | tf_op jit(solution)/shard_map/ppermute | solution.py:410
  67.8 17.4 %collective-permute-start.14 = (bf16[64,1024]{1,0:T(8,128)(2,1)S(1)}, bf16[64,1024]{1,0:T(8,128)(2,1)S(1)}, u32[]{:S(2)}, u32[]{:S(2)}) collective-permute-start(bf16[64,1024]{1,0:T(8,128)(2,1)S(1)} %get-tuple-element.77.refs_0_), channel_id=1, source_target_pairs={{0,16},{8,24},{16,0},{24,8},{1,17},{9,25},{17,1},{25,9},{2,18},{10... | collective-permute-start | bytes 393224 | tf_op jit(solution)/shard_map/ppermute | solution.py:410
  69.3 15.9 %collective-permute-start.15 = (bf16[64,1024]{1,0:T(8,128)(2,1)S(1)}, bf16[64,1024]{1,0:T(8,128)(2,1)S(1)}, u32[]{:S(2)}, u32[]{:S(2)}) collective-permute-start(bf16[64,1024]{1,0:T(8,128)(2,1)S(1)} %get-tuple-element.77.refs_0_), channel_id=1, source_target_pairs={{0,24},{8,16},{16,8},{24,0},{1,25},{9,17},{17,9},{25,1},{2,26},{10... | collective-permute-start | bytes 393224 | tf_op jit(solution)/shard_map/ppermute | solution.py:410
  73.3 16.3 %collective-permute-start.28 = (bf16[64,1024]{1,0:T(8,128)(2,1)S(1)}, bf16[64,1024]{1,0:T(8,128)(2,1)S(1)}, u32[]{:S(2)}, u32[]{:S(2)}) collective-permute-start(bf16[64,1024]{1,0:T(8,128)(2,1)S(1)} %get-tuple-element.99.refs_0_), channel_id=1, source_target_pairs={{0,8},{8,0},{16,24},{24,16},{1,9},{9,1},{17,25},{25,17},{2,10},{10... | collective-permute-start | bytes 393224 | tf_op jit(solution)/shard_map/ppermute | solution.py:410
  74.1 16.1 %collective-permute-start.29 = (bf16[64,1024]{1,0:T(8,128)(2,1)S(1)}, bf16[64,1024]{1,0:T(8,128)(2,1)S(1)}, u32[]{:S(2)}, u32[]{:S(2)}) collective-permute-start(bf16[64,1024]{1,0:T(8,128)(2,1)S(1)} %get-tuple-element.99.refs_0_), channel_id=1, source_target_pairs={{0,16},{8,24},{16,0},{24,8},{1,17},{9,25},{17,1},{25,9},{2,18},{10... | collective-permute-start | bytes 393224 | tf_op jit(solution)/shard_map/ppermute | solution.py:410
  76.0 14.2 %collective-permute-start.30 = (bf16[64,1024]{1,0:T(8,128)(2,1)S(1)}, bf16[64,1024]{1,0:T(8,128)(2,1)S(1)}, u32[]{:S(2)}, u32[]{:S(2)}) collective-permute-start(bf16[64,1024]{1,0:T(8,128)(2,1)S(1)} %get-tuple-element.99.refs_0_), channel_id=1, source_target_pairs={{0,24},{8,16},{16,8},{24,0},{1,25},{9,17},{17,9},{25,1},{2,26},{10... | collective-permute-start | bytes 393224 | tf_op jit(solution)/shard_map/ppermute | solution.py:410
  98.5 9.7 %collective-permute-start.38 = (bf16[64,1024]{1,0:T(8,128)(2,1)S(1)}, bf16[64,1024]{1,0:T(8,128)(2,1)S(1)}, u32[]{:S(2)}, u32[]{:S(2)}) collective-permute-start(bf16[64,1024]{1,0:T(8,128)(2,1)S(1)} %get-tuple-element.107.refs_0_), channel_id=1, source_target_pairs={{0,16},{8,24},{16,0},{24,8},{1,17},{9,25},{17,1},{25,9},{2,18},{10... | collective-permute-start | bytes 393224 | tf_op jit(solution)/shard_map/ppermute | solution.py:410
  99.1 9.3 %collective-permute-start.39 = (bf16[64,1024]{1,0:T(8,128)(2,1)S(1)}, bf16[64,1024]{1,0:T(8,128)(2,1)S(1)}, u32[]{:S(2)}, u32[]{:S(2)}) collective-permute-start(bf16[64,1024]{1,0:T(8,128)(2,1)S(1)} %get-tuple-element.107.refs_0_), channel_id=1, source_target_pairs={{0,24},{8,16},{16,8},{24,0},{1,25},{9,17},{17,9},{25,1},{2,26},{10... | collective-permute-start | bytes 393224 | tf_op jit(solution)/shard_map/ppermute | solution.py:410
  104.1 9.1 %collective-permute-start.35 = (bf16[64,1024]{1,0:T(8,128)(2,1)S(1)}, bf16[64,1024]{1,0:T(8,128)(2,1)S(1)}, u32[]{:S(2)}, u32[]{:S(2)}) collective-permute-start(bf16[64,1024]{1,0:T(8,128)(2,1)S(1)} %get-tuple-element.106.refs_0_), channel_id=1, source_target_pairs={{0,16},{8,24},{16,0},{24,8},{1,17},{9,25},{17,1},{25,9},{2,18},{10... | collective-permute-start | bytes 393224 | tf_op jit(solution)/shard_map/ppermute | solution.py:410
  (32 other events, 231.0 us)
Sparse Core Ops, SparseCore 0:
  9.6 34.9 all-gather.6
  46.8 35.6 all-gather.8
  84.2 23.9 all-gather.10
